TPU v7x, 32 devices: a whole 2x2x4 slice. The times are simulated.
32 devices in a mesh: dp: 4 (over y, x), expert: 8 (over z, core).
Axes of the slice: x: 2, y: 2, z: 4, core: 2. Of those that a mesh axis runs over, the one named last changes fastest.
Arguments:
- tokens: bfloat16 [4, 1024, 2048], P('dp', 'expert'), may hold values from -6 to 6
- cotangent: bfloat16 [4, 1024, 2048], P('dp', 'expert'), may hold values from -6 to 6
- lengths: int32 [4], P('dp'), may hold values from 256 to 1024, as said below
- routes: int32 [4, 1024, 8], P('dp', 'expert'), may hold values from 0 to 15, all different within a row; in each aligned block of 128 rows (0 to 127, 128 to 255, ..., all dimensions but the last counted through in order) at most 128 rows name the same one
- w_query: float32 [2048, 2048], P(('dp', 'expert')), may hold values from -0.125 to 0.125
- w_key: float32 [2048, 2048], P(('dp', 'expert')), may hold values from -0.125 to 0.125
- w_value: float32 [2048, 2048], P(('dp', 'expert')), may hold values from -0.125 to 0.125
- w_output: float32 [2048, 2048], P(('dp', 'expert')), may hold values from -0.5 to 0.5
- router: float32 [2048, 16], P(('dp', 'expert')), may hold values from -0.0625 to 0.0625
- gain_attn: float32 [2048], P(('dp', 'expert')), may hold values from 0.5 to 1.5
- gain_query: float32 [2048], P(('dp', 'expert')), may hold values from 0.5 to 1.5
- gain_key: float32 [2048], P(('dp', 'expert')), may hold values from 0.5 to 1.5
- gain_mlp: float32 [2048], P(('dp', 'expert')), may hold values from 0.5 to 1.5
- w_gate: float32 [16, 2048, 1024], P('expert', None, 'dp'), may hold values from -0.125 to 0.125
- w_up: float32 [16, 2048, 1024], P('expert', None, 'dp'), may hold values from -0.125 to 0.125
- w_down: float32 [16, 1024, 2048], P('expert', 'dp'), may hold values from -0.5 to 0.5
Outputs:
- output: bfloat16 [4, 1024, 2048], P('dp', 'expert')
- grad_tokens: bfloat16 [4, 1024, 2048], P('dp', 'expert')
- grad_w_query: float32 [2048, 2048], P(('dp', 'expert'))
- grad_w_key: float32 [2048, 2048], P(('dp', 'expert'))
- grad_w_value: float32 [2048, 2048], P(('dp', 'expert'))
- grad_w_output: float32 [2048, 2048], P(('dp', 'expert'))
- grad_router: float32 [2048, 16], P(('dp', 'expert'))
- grad_gain_attn: float32 [2048], P(('dp', 'expert'))
- grad_gain_query: float32 [2048], P(('dp', 'expert'))
- grad_gain_key: float32 [2048], P(('dp', 'expert'))
- grad_gain_mlp: float32 [2048], P(('dp', 'expert'))
- grad_w_gate: float32 [16, 2048, 1024], P('expert', None, 'dp')
- grad_w_up: float32 [16, 2048, 1024], P('expert', None, 'dp')
- grad_w_down: float32 [16, 1024, 2048], P('expert', 'dp')
Inputs may be any that keep to these rules, and one draw needn't show every extreme that they name: `lengths`: at least one sequence has the full length 1024. `routes`: A token's 8 experts differ. Among the 128 tokens of one device (aligned blocks of the flattened positions) no expert is named by more than 128 tokens, a bound that some block reaches of them in some of these blocks.
All inputs are finite; a program needn't handle non-finite values.
Results may differ from a plain program's by a relative error of at most 0.019.
Values may be sent and summed in bfloat16 or wider, within the bound.
No kernel may reach another device: no remote copies, remote signals or barrier semaphores. Data moves between devices by JAX's collectives and lax.ppermute only.
A program may use at most 384 MiB of HBM per device.

v0:
```python
import jax
import jax.numpy as jnp
from jax import lax
from jax.sharding import PartitionSpec as P

HEAD_DIM = 128
TOP = 8


PRECISE = lax.Precision.HIGHEST
EPSILON = 1e-05
ROPE_BASE = 10000.0
MASKED = -1e30


def rms_parts(values, gain):
    factor = lax.rsqrt(jnp.mean(values * values, axis=-1, keepdims=True) + EPSILON)
    normal = values * factor
    return (normal * gain, normal, factor)


def rms_back(upstream, normal, factor, gain):
    scaled = upstream * gain
    inner_mean = jnp.mean(scaled * normal, axis=-1, keepdims=True)
    return (factor * (scaled - normal * inner_mean), jnp.sum(upstream * normal, axis=0))


def rope_tables(positions):
    half_dim = HEAD_DIM // 2
    frequency = ROPE_BASE ** (-2.0 * jnp.arange(half_dim).astype(jnp.float32) / HEAD_DIM)
    angles = positions.astype(jnp.float32)[:, None] * frequency[None, :]
    return (jnp.cos(angles)[:, None, :], jnp.sin(angles)[:, None, :])


def rotate(values, cosine, sine_part, direction):
    half_dim = values.shape[-1] // 2
    front_half = values[..., :half_dim]
    behind = values[..., half_dim:]
    return jnp.concatenate(
        [
            front_half * cosine - direction * behind * sine_part,
            behind * cosine + direction * front_half * sine_part,
        ],
        axis=-1,
    )


def contract_rows(left_side, right_side):
    return lax.dot_general(
        left_side, right_side, (((0,), (0,)), ((), ())), preferred_element_type=jnp.float32
    )


def times_transpose(left_side, right_side):
    return lax.dot_general(
        left_side, right_side, (((1,), (1,)), ((), ())), preferred_element_type=jnp.float32
    )


def score_grads(
    query_heads,
    key_heads,
    value_heads,
    grad_heads,
    log_total,
    row_delta,
    query_place,
    key_place,
    length,
):
    factor = HEAD_DIM ** (-0.5)
    scores = (
        jnp.einsum("qhd,khd->hqk", query_heads, key_heads, preferred_element_type=jnp.float32)
        * factor
    )
    allowed = (key_place[None, :] <= query_place[:, None]) & (key_place[None, :] < length)
    weights_full = jnp.where(allowed[None], jnp.exp(scores - log_total[:, :, None]), 0.0)
    grad_weights = jnp.einsum(
        "qhd,khd->hqk", grad_heads, value_heads, preferred_element_type=jnp.float32
    )
    grad_scores = (weights_full * (grad_weights - row_delta[:, :, None])).astype(jnp.bfloat16)
    return (weights_full.astype(jnp.bfloat16), grad_scores)


def per_device(
    tokens,
    cotangent,
    lengths,
    routes,
    w_query,
    w_key,
    w_value,
    w_output,
    router,
    gain_attn,
    gain_query,
    gain_key,
    gain_mlp,
    w_gate,
    w_up,
    w_down,
):
    tok_rows = tokens.shape[1]
    model_width = tokens.shape[2]
    head_count = model_width // HEAD_DIM
    groups = lax.axis_size("expert")
    seq_len = tok_rows * groups
    length = lengths[0]
    factor = HEAD_DIM ** (-0.5)
    gathered = (
        lax.all_gather(w_query.astype(jnp.bfloat16), ("dp", "expert"), axis=0, tiled=True),
        lax.all_gather(w_key.astype(jnp.bfloat16), ("dp", "expert"), axis=0, tiled=True),
        lax.all_gather(w_value.astype(jnp.bfloat16), ("dp", "expert"), axis=0, tiled=True),
        lax.all_gather(w_output.astype(jnp.bfloat16), ("dp", "expert"), axis=0, tiled=True),
        lax.all_gather(router.astype(jnp.bfloat16), ("dp", "expert"), axis=0, tiled=True),
        lax.all_gather(gain_attn.astype(jnp.bfloat16), ("dp", "expert"), axis=0, tiled=True),
        lax.all_gather(gain_query.astype(jnp.bfloat16), ("dp", "expert"), axis=0, tiled=True),
        lax.all_gather(gain_key.astype(jnp.bfloat16), ("dp", "expert"), axis=0, tiled=True),
        lax.all_gather(gain_mlp.astype(jnp.bfloat16), ("dp", "expert"), axis=0, tiled=True),
    )
    query_weight, key_weight, value_weight, output_weight, router_weight = (
        gathered[0],
        gathered[1],
        gathered[2],
        gathered[3],
        gathered[4],
    )
    attn_gain = gathered[5].astype(jnp.float32)
    query_gain = gathered[6].astype(jnp.float32)
    key_gain = gathered[7].astype(jnp.float32)
    mlp_gain = gathered[8].astype(jnp.float32)
    gate_weight, up_weight, down_weight = (
        lax.all_gather(w_gate.astype(jnp.bfloat16), "dp", axis=2, tiled=True),
        lax.all_gather(w_up.astype(jnp.bfloat16), "dp", axis=2, tiled=True),
        lax.all_gather(w_down.astype(jnp.bfloat16), "dp", axis=1, tiled=True),
    )
    token_rows = tokens[0].astype(jnp.float32)
    attn_in, attn_normal, attn_factor = rms_parts(token_rows, attn_gain)
    attn_low = attn_in.astype(jnp.bfloat16)
    query_pre = jnp.dot(attn_low, query_weight, preferred_element_type=jnp.float32)
    key_pre = jnp.dot(attn_low, key_weight, preferred_element_type=jnp.float32)
    value_low = jnp.dot(attn_low, value_weight, preferred_element_type=jnp.float32).astype(
        jnp.bfloat16
    )
    query_norm, query_normal, query_factor = rms_parts(query_pre, query_gain)
    key_norm, key_normal, key_factor = rms_parts(key_pre, key_gain)
    positions = lax.axis_index("expert") * tok_rows + jnp.arange(tok_rows)
    cosine, sine_part = rope_tables(positions)
    query_low = rotate(
        query_norm.reshape(tok_rows, head_count, HEAD_DIM), cosine, sine_part, 1.0
    ).astype(jnp.bfloat16)
    key_low = (
        rotate(key_norm.reshape(tok_rows, head_count, HEAD_DIM), cosine, sine_part, 1.0)
        .astype(jnp.bfloat16)
        .reshape(tok_rows, model_width)
    )
    whole_keys, whole_values = (
        lax.all_gather(key_low, "expert", axis=0, tiled=True),
        lax.all_gather(value_low, "expert", axis=0, tiled=True),
    )
    all_keys = whole_keys.reshape(seq_len, head_count, HEAD_DIM)
    all_values = whole_values.reshape(seq_len, head_count, HEAD_DIM)
    key_place = jnp.arange(seq_len)
    allowed = (key_place[None, :] <= positions[:, None]) & (key_place[None, :] < length)
    scores = (
        jnp.einsum("qhd,khd->hqk", query_low, all_keys, preferred_element_type=jnp.float32) * factor
    )
    scores = jnp.where(allowed[None], scores, MASKED)
    log_total = jax.nn.logsumexp(scores, axis=-1)
    weights_low = jnp.where(allowed[None], jnp.exp(scores - log_total[:, :, None]), 0.0).astype(
        jnp.bfloat16
    )
    attended = jnp.einsum(
        "hqk,khd->qhd", weights_low, all_values, preferred_element_type=jnp.float32
    ).reshape(tok_rows, model_width)
    attended_low = attended.astype(jnp.bfloat16)
    hidden = token_rows + jnp.dot(attended_low, output_weight, preferred_element_type=jnp.float32)
    mlp_in, mlp_normal, mlp_factor = rms_parts(hidden, mlp_gain)
    mlp_low = mlp_in.astype(jnp.bfloat16)
    logits = jnp.dot(mlp_low, router_weight, preferred_element_type=jnp.float32)
    route_ids = routes[0]
    gate_probs = jax.nn.softmax(jnp.take_along_axis(logits, route_ids, axis=1), axis=-1)
    experts = router_weight.shape[1]
    slot_cap = 2 * tok_rows * TOP // experts
    local_count = experts // groups
    pair_count = tok_rows * TOP
    flat_routes = route_ids.reshape(-1)
    expert_ids = jnp.arange(experts)
    hit_table = (flat_routes[:, None] == expert_ids[None, :]).astype(jnp.int32)
    slot_rank = jnp.sum((jnp.cumsum(hit_table, axis=0) - hit_table) * hit_table, axis=1)
    counts = jnp.sum(hit_table, axis=0)
    slot_ids = flat_routes * slot_cap + slot_rank
    slot_pair = (
        jnp.zeros((experts * slot_cap,), jnp.int32)
        .at[slot_ids]
        .set(jnp.arange(pair_count, dtype=jnp.int32))
    )
    send_rows = mlp_low[slot_pair // TOP].reshape(groups, local_count, slot_cap, model_width)
    send_counts = counts.reshape(groups, local_count).astype(jnp.bfloat16)
    arrived_rows, arrived_counts = (
        lax.all_to_all(send_rows, "expert", split_axis=0, concat_axis=0, tiled=True),
        lax.all_to_all(send_counts, "expert", split_axis=0, concat_axis=0, tiled=True),
    )
    living = (jnp.arange(slot_cap)[None, None, :] < arrived_counts.astype(jnp.int32)[:, :, None])[
        ..., None
    ]
    gate_pre = jnp.einsum(
        "nemd,edf->nemf", arrived_rows, gate_weight, preferred_element_type=jnp.float32
    )
    up_pre = jnp.einsum(
        "nemd,edf->nemf", arrived_rows, up_weight, preferred_element_type=jnp.float32
    )
    gate_sigmoid = jax.nn.sigmoid(gate_pre)
    activity = (gate_pre * gate_sigmoid * up_pre).astype(jnp.bfloat16)
    expert_out = jnp.einsum(
        "nemf,efd->nemd", activity, down_weight, preferred_element_type=jnp.float32
    ).astype(jnp.bfloat16)
    returned = lax.all_to_all(expert_out, "expert", split_axis=0, concat_axis=0, tiled=True)
    pair_out = (
        returned.reshape(experts * slot_cap, model_width)[slot_ids]
        .reshape(tok_rows, TOP, model_width)
        .astype(jnp.float32)
    )
    output = hidden + jnp.sum(gate_probs[:, :, None] * pair_out, axis=1)
    grad_out = cotangent[0].astype(jnp.float32)
    grad_gates = jnp.sum(grad_out[:, None, :] * pair_out, axis=-1)
    pair_grad = (
        (gate_probs[:, :, None] * grad_out[:, None, :])
        .astype(jnp.bfloat16)
        .reshape(pair_count, model_width)
    )
    send_grad = pair_grad[slot_pair].reshape(groups, local_count, slot_cap, model_width)
    arrived_grad = lax.all_to_all(send_grad, "expert", split_axis=0, concat_axis=0, tiled=True)
    arrived_grad = jnp.where(living, arrived_grad, jnp.zeros((), jnp.bfloat16))
    grad_activity = jnp.einsum(
        "nemd,efd->nemf", arrived_grad, down_weight, preferred_element_type=jnp.float32
    )
    grad_gate_pre = (
        grad_activity * up_pre * gate_sigmoid * (1.0 + gate_pre * (1.0 - gate_sigmoid))
    ).astype(jnp.bfloat16)
    grad_up_pre = (grad_activity * gate_pre * gate_sigmoid).astype(jnp.bfloat16)
    grad_down = jnp.einsum(
        "nemf,nemd->efd", activity, arrived_grad, preferred_element_type=jnp.float32
    )
    grad_gate = jnp.einsum(
        "nemd,nemf->edf", arrived_rows, grad_gate_pre, preferred_element_type=jnp.float32
    )
    grad_up = jnp.einsum(
        "nemd,nemf->edf", arrived_rows, grad_up_pre, preferred_element_type=jnp.float32
    )
    input_grad = (
        jnp.einsum("nemf,edf->nemd", grad_gate_pre, gate_weight, preferred_element_type=jnp.float32)
        + jnp.einsum("nemf,edf->nemd", grad_up_pre, up_weight, preferred_element_type=jnp.float32)
    ).astype(jnp.bfloat16)
    sent_back = lax.all_to_all(input_grad, "expert", split_axis=0, concat_axis=0, tiled=True)
    grad_mlp_in = jnp.sum(
        sent_back.reshape(experts * slot_cap, model_width)[slot_ids]
        .reshape(tok_rows, TOP, model_width)
        .astype(jnp.float32),
        axis=1,
    )
    grad_chosen = gate_probs * (
        grad_gates - jnp.sum(gate_probs * grad_gates, axis=-1, keepdims=True)
    )
    route_table = (route_ids[:, :, None] == expert_ids[None, None, :]).astype(jnp.float32)
    grad_logits = jnp.sum(grad_chosen[:, :, None] * route_table, axis=1)
    grad_router = jnp.einsum(
        "td,te->de", mlp_low.astype(jnp.float32), grad_logits, precision=PRECISE
    )
    grad_mlp_in = grad_mlp_in + jnp.einsum(
        "te,de->td", grad_logits, router_weight.astype(jnp.float32), precision=PRECISE
    )
    grad_hidden_norm, grad_gain_mlp = rms_back(grad_mlp_in, mlp_normal, mlp_factor, mlp_gain)
    grad_hidden = grad_out + grad_hidden_norm
    grad_attn_low = grad_hidden.astype(jnp.bfloat16)
    grad_w_out = contract_rows(attended_low, grad_attn_low)
    grad_attended = times_transpose(grad_attn_low, output_weight).astype(jnp.bfloat16)
    row_delta = jnp.sum(
        (grad_attended.astype(jnp.float32) * attended).reshape(tok_rows, head_count, HEAD_DIM),
        axis=-1,
    ).T
    grad_heads = grad_attended.reshape(tok_rows, head_count, HEAD_DIM)
    block_rows = min(512, seq_len)
    block_total = seq_len // block_rows

    def key_part(number):
        offset = number * block_rows
        block_keys = lax.dynamic_slice_in_dim(all_keys, offset, block_rows, 0)
        block_values = lax.dynamic_slice_in_dim(all_values, offset, block_rows, 0)
        weights_part, grad_scores = score_grads(
            query_low,
            block_keys,
            block_values,
            grad_heads,
            log_total,
            row_delta,
            positions,
            offset + jnp.arange(block_rows),
            length,
        )
        grad_query_part = (
            jnp.einsum("hqk,khd->qhd", grad_scores, block_keys, preferred_element_type=jnp.float32)
            * factor
        )
        grad_key_part = (
            jnp.einsum("hqk,qhd->khd", grad_scores, query_low, preferred_element_type=jnp.float32)
            * factor
        )
        grad_value_part = jnp.einsum(
            "hqk,qhd->khd", weights_part, grad_heads, preferred_element_type=jnp.float32
        )
        return (
            grad_query_part,
            grad_key_part.reshape(block_rows, model_width),
            grad_value_part.reshape(block_rows, model_width),
        )

    query_parts, key_parts, value_parts = lax.map(
        lambda number: key_part(number), jnp.arange(block_total)
    )
    grad_query = jnp.sum(query_parts, axis=0).reshape(tok_rows, model_width)
    grad_key, grad_value = (
        lax.psum_scatter(
            key_parts.reshape(seq_len, model_width).astype(jnp.bfloat16),
            "expert",
            scatter_dimension=0,
            tiled=True,
        ).astype(jnp.float32),
        lax.psum_scatter(
            value_parts.reshape(seq_len, model_width).astype(jnp.bfloat16),
            "expert",
            scatter_dimension=0,
            tiled=True,
        ).astype(jnp.float32),
    )
    grad_value_low = grad_value.astype(jnp.bfloat16)
    grad_query_rot = (
        grad_query.astype(jnp.bfloat16).astype(jnp.float32).reshape(tok_rows, head_count, HEAD_DIM)
    )
    grad_key_rot = (
        grad_key.astype(jnp.bfloat16).astype(jnp.float32).reshape(tok_rows, head_count, HEAD_DIM)
    )
    grad_query_norm = rotate(grad_query_rot, cosine, sine_part, -1.0).reshape(tok_rows, model_width)
    grad_key_norm = rotate(grad_key_rot, cosine, sine_part, -1.0).reshape(tok_rows, model_width)
    grad_query_pre, grad_gain_query = rms_back(
        grad_query_norm, query_normal, query_factor, query_gain
    )
    grad_key_pre, grad_gain_key = rms_back(grad_key_norm, key_normal, key_factor, key_gain)
    grad_query_low = grad_query_pre.astype(jnp.bfloat16)
    grad_key_low = grad_key_pre.astype(jnp.bfloat16)
    grad_wq = contract_rows(attn_low, grad_query_low)
    grad_wk = contract_rows(attn_low, grad_key_low)
    grad_wv = contract_rows(attn_low, grad_value_low)
    grad_attn_in = (
        times_transpose(grad_query_low, query_weight)
        + times_transpose(grad_key_low, key_weight)
        + times_transpose(grad_value_low, value_weight)
    )
    grad_attn_x, grad_gain_attn = rms_back(grad_attn_in, attn_normal, attn_factor, attn_gain)
    grad_tokens = (grad_hidden + grad_attn_x).astype(jnp.bfloat16)
    summed_grads = (
        lax.psum_scatter(grad_wq, ("dp", "expert"), scatter_dimension=0, tiled=True),
        lax.psum_scatter(grad_wk, ("dp", "expert"), scatter_dimension=0, tiled=True),
        lax.psum_scatter(grad_wv, ("dp", "expert"), scatter_dimension=0, tiled=True),
        lax.psum_scatter(grad_w_out, ("dp", "expert"), scatter_dimension=0, tiled=True),
        lax.psum_scatter(grad_router, ("dp", "expert"), scatter_dimension=0, tiled=True),
        lax.psum_scatter(grad_gain_attn, ("dp", "expert"), scatter_dimension=0, tiled=True),
        lax.psum_scatter(grad_gain_query, ("dp", "expert"), scatter_dimension=0, tiled=True),
        lax.psum_scatter(grad_gain_key, ("dp", "expert"), scatter_dimension=0, tiled=True),
        lax.psum_scatter(grad_gain_mlp, ("dp", "expert"), scatter_dimension=0, tiled=True),
    )
    expert_grads = (
        lax.psum_scatter(
            grad_gate.astype(jnp.bfloat16), "dp", scatter_dimension=2, tiled=True
        ).astype(jnp.float32),
        lax.psum_scatter(
            grad_up.astype(jnp.bfloat16), "dp", scatter_dimension=2, tiled=True
        ).astype(jnp.float32),
        lax.psum_scatter(
            grad_down.astype(jnp.bfloat16), "dp", scatter_dimension=1, tiled=True
        ).astype(jnp.float32),
    )
    return (
        output.astype(jnp.bfloat16)[None],
        grad_tokens[None],
        summed_grads[0],
        summed_grads[1],
        summed_grads[2],
        summed_grads[3],
        summed_grads[4],
        summed_grads[5],
        summed_grads[6],
        summed_grads[7],
        summed_grads[8],
        expert_grads[0],
        expert_grads[1],
        expert_grads[2],
    )


def solution(mesh):
    return jax.shard_map(
        per_device,
        mesh=mesh,
        in_specs=(
            P("dp", "expert", None),
            P("dp", "expert", None),
            P("dp"),
            P("dp", "expert", None),
            P(("dp", "expert"), None),
            P(("dp", "expert"), None),
            P(("dp", "expert"), None),
            P(("dp", "expert"), None),
            P(("dp", "expert"), None),
            P(("dp", "expert")),
            P(("dp", "expert")),
            P(("dp", "expert")),
            P(("dp", "expert")),
            P("expert", None, "dp"),
            P("expert", None, "dp"),
            P("expert", "dp", None),
        ),
        out_specs=(
            P("dp", "expert", None),
            P("dp", "expert", None),
            P(("dp", "expert"), None),
            P(("dp", "expert"), None),
            P(("dp", "expert"), None),
            P(("dp", "expert"), None),
            P(("dp", "expert"), None),
            P(("dp", "expert")),
            P(("dp", "expert")),
            P(("dp", "expert")),
            P(("dp", "expert")),
            P("expert", None, "dp"),
            P("expert", None, "dp"),
            P("expert", "dp", None),
        ),
        check_vma=False,
    )
```

profile of v0, /device:TPU:0, one launch (start us, length us, event | category | flops | bytes accessed | tf_op | source)
XLA Modules:
  0.0 2666.3 jit_solution(7748637217895553611)
XLA Ops:
  16.3 42.5 %all-reduce.9 = (bf16[2048]{0:T(1024)(128)(2,1)S(1)}, bf16[2048]{0:T(1024)(128)(2,1)S(1)}, bf16[2048]{0:T(1024)(128)(2,1)S(1)}, bf16[2048]{0:T(1024)(128)(2,1)S(1)}) all-reduce(bf16[2048]{0:T(1024)(128)(2,1)S(1)} %dynamic-update-slice, bf16[2048]{0:T(1024)(128)(2,1)S(1)} %dynamic-update-slice.1, ...), channel_id=1, replica_groups=mesh['dp'=4,'expert'=8] {'dp','expert'}, use_global_device_ids=true, to_apply=%add | all-reduce | flops 8192 | bytes 32768
  61.0 30.8 %all-gather.15.cloned.1.call-done = bf16[2048,2048]{1,0:T(8,128)(2,1)} async-done(((bf16[64,2048]{1,0:T(8,128)(2,1)}), bf16[2048,2048]{1,0:T(8,128)(2,1)}) %all-gather.15.cloned.1.call-update) | async-done | bytes 8388624 | tf_op jit(solution)/shard_map/all_gather | solution.py:111
  98.1 73.3 %all-gather.17.cloned.1.call-done = bf16[2048,2048]{1,0:T(8,128)(2,1)} async-done(((bf16[64,2048]{1,0:T(8,128)(2,1)}), bf16[2048,2048]{1,0:T(8,128)(2,1)}) %all-gather.17.cloned.1.call-update) | async-done | bytes 8388624 | tf_op jit(solution)/shard_map/all_gather | solution.py:112
  181.1 70.0 %all-gather.11.cloned.1.call-done = bf16[2048,2048]{1,0:T(8,128)(2,1)} async-done(((bf16[64,2048]{1,0:T(8,128)(2,1)}), bf16[2048,2048]{1,0:T(8,128)(2,1)}) %all-gather.11.cloned.1.call-update) | async-done | bytes 8388624 | tf_op jit(solution)/shard_map/all_gather | solution.py:113
  276.8 22.7 all-gather.19.cloned.1.call-done
  309.1 39.4 %all-gather.13.cloned.1.call-done = bf16[1024,2048]{1,0:T(8,128)(2,1)} async-done(((bf16[128,2048]{1,0:T(8,128)(2,1)}), bf16[1024,2048]{1,0:T(8,128)(2,1)}) %all-gather.13.cloned.1.call-update) | async-done | bytes 4194320 | tf_op jit(solution)/shard_map/all_gather | solution.py:159
  356.1 72.0 %all-gather.21.cloned.1.call-done = bf16[2048,2048]{1,0:T(8,128)(2,1)} async-done(((bf16[64,2048]{1,0:T(8,128)(2,1)}), bf16[2048,2048]{1,0:T(8,128)(2,1)}) %all-gather.21.cloned.1.call-update) | async-done | bytes 8388624 | tf_op jit(solution)/shard_map/all_gather | solution.py:114
  453.9 209.6 %all-gather = bf16[32,64,16]{1,2,0:T(8,128)(2,1)S(1)} all-gather(bf16[1,64,16]{1,2,0:T(8,128)(2,1)S(1)} %convert_bitcast_fusion.1), channel_id=1, replica_groups=mesh['dp'=4,'expert'=8] {'dp','expert'}, dimensions={0}, use_global_device_ids=true | all-gather | bytes 67584 | tf_op jit(solution)/shard_map/all_gather | solution.py:115
  674.7 19.1 gather_fusion.2
  734.8 56.5 %all-gather.27.cloned.1.call-done = bf16[2,1024,2048]{2,1,0:T(8,128)(2,1)} async-done(((bf16[2,256,2048]{2,1,0:T(8,128)(2,1)}), bf16[2,1024,2048]{2,1,0:T(8,128)(2,1)}) %all-gather.27.cloned.1.call-update) | async-done | bytes 8388624 | tf_op jit(solution)/shard_map/all_gather | solution.py:135
  791.3 91.4 %all-to-all-done.3 = bf16[8,2,128,2048]{3,2,1,0:T(8,128)(2,1)} async-done(((bf16[8,2,128,2048]{3,2,1,0:T(8,128)(2,1)}), bf16[8,2,128,2048]{3,2,1,0:T(8,128)(2,1)}, u32[]{:S(2)}, u32[]{:S(2)}) %all-to-all-start.3) | async-done | bytes 8388640 | tf_op jit(solution)/shard_map/all_to_all | solution.py:233
  882.7 19.8 fusion.41
  973.7 142.6 %all-to-all-done.1 = bf16[8,2,128,2048]{3,2,1,0:T(8,128)(2,1)} async-done(((bf16[8,2,128,2048]{3,2,1,0:T(8,128)(2,1)}), bf16[8,2,128,2048]{3,2,1,0:T(8,128)(2,1)}, u32[]{:S(2)}, u32[]{:S(2)}) %all-to-all-start.1) | async-done | bytes 8388640 | tf_op jit(solution)/shard_map/all_to_all | solution.py:218
  1148.6 156.6 %all-to-all-done.4 = bf16[8,2,128,2048]{3,2,1,0:T(8,128)(2,1)} async-done(((bf16[8,2,128,2048]{3,2,1,0:T(8,128)(2,1)}), bf16[8,2,128,2048]{3,2,1,0:T(8,128)(2,1)}, u32[]{:S(2)}, u32[]{:S(2)}) %all-to-all-start.4) | async-done | bytes 8388640 | tf_op jit(solution)/shard_map/all_to_all | solution.py:255
  1334.8 67.7 %while.15 = (s32[]{:T(128)}, f32[2,128,16,128]{1,3,2,0:T(8,128)}, bf16[2,512,2048]{1,2,0:T(8,128)(2,1)}, bf16[2,512,2048]{2,1,0:T(8,128)(2,1)}, s32[2]{0:T(128)S...) while((s32[]{:T(128)}, f32[2,128,16,128]{1,3,2,0:T(8,128)}, ...), condition=%wide.region_21.22_spmd.clone, body=%wide.region_20.21_spmd.clone.sunk | while | flops 1355155072 | bytes 70483728 | solution.py:318
  1516.5 125.8 %reduce-scatter.33.cloned.1.call-done = f32[64,16]{1,0:T(8,128)} async-done(((f32[2048,16]{1,0:T(8,128)}), f32[64,16]{1,0:T(8,128)}) %reduce-scatter.33.cloned.1.call-update) | async-done | bytes 4112
  1643.8 84.7 %reduce-scatter.29.cloned.1.call-done = bf16[2,256,2048]{2,1,0:T(8,128)(2,1)} async-done(((bf16[2,1024,2048]{2,1,0:T(8,128)(2,1)}), bf16[2,256,2048]{2,1,0:T(8,128)(2,1)}) %reduce-scatter.29.cloned.1.call-update) | async-done | bytes 2097168 | tf_op jit(solution)/shard_map/reduce_scatter | solution.py:379
  1732.6 85.2 %reduce-scatter.25.cloned.1.call-done = bf16[2,2048,256]{2,1,0:T(8,128)(2,1)} async-done(((bf16[2,2048,1024]{2,1,0:T(8,128)(2,1)}), bf16[2,2048,256]{2,1,0:T(8,128)(2,1)}) %reduce-scatter.25.cloned.1.call-update) | async-done | bytes 2097168 | tf_op jit(solution)/shard_map/reduce_scatter | solution.py:373
  1821.7 85.7 %reduce-scatter.27.cloned.1.call-done = bf16[2,2048,256]{2,1,0:T(8,128)(2,1)} async-done(((bf16[2,2048,1024]{2,1,0:T(8,128)(2,1)}), bf16[2,2048,256]{2,1,0:T(8,128)(2,1)}) %reduce-scatter.27.cloned.1.call-update) | async-done | bytes 2097168 | tf_op jit(solution)/shard_map/reduce_scatter | solution.py:376
  1924.0 41.9 %all-reduce.8 = (f32[2048]{0:T(1024)S(1)}, f32[2048]{0:T(1024)S(1)}, f32[2048]{0:T(1024)S(1)}, f32[2048]{0:T(1024)S(1)}) all-reduce(f32[2048]{0:T(1024)S(1)} %get-tuple-element.188, f32[2048]{0:T(1024)S(1)} %get-tuple-element.186, f32[2048]{0:T(1024)S(1)} %get-tuple-element.184, ...), channel_id=9, replica_groups=mesh['dp'=4,'expert'=8] {'dp','expert'}, use_global_device_ids=true, to_apply=%region_34.35.clone | all-reduce | flops 8192 | bytes 65536
  1969.4 128.4 %reduce-scatter.23.cloned.1.call-done = f32[64,2048]{1,0:T(8,128)} async-done(((f32[2048,2048]{1,0:T(8,128)}), f32[64,2048]{1,0:T(8,128)}) %reduce-scatter.23.cloned.1.call-update) | async-done | bytes 524304 | tf_op jit(solution)/shard_map/reduce_scatter | solution.py:365
  2097.8 187.1 %reduce-scatter.19.cloned.1.call-done = f32[64,2048]{1,0:T(8,128)} async-done(((f32[2048,2048]{1,0:T(8,128)}), f32[64,2048]{1,0:T(8,128)}) %reduce-scatter.19.cloned.1.call-update) | async-done | bytes 524304 | tf_op jit(solution)/shard_map/reduce_scatter | solution.py:363
  2284.9 187.1 %reduce-scatter.17.cloned.1.call-done = f32[64,2048]{1,0:T(8,128)} async-done(((f32[2048,2048]{1,0:T(8,128)}), f32[64,2048]{1,0:T(8,128)}) %reduce-scatter.17.cloned.1.call-update) | async-done | bytes 524304 | tf_op jit(solution)/shard_map/reduce_scatter | solution.py:362
  2472.0 187.2 %reduce-scatter.21.cloned.1.call-done = f32[64,2048]{1,0:T(8,128)} async-done(((f32[2048,2048]{1,0:T(8,128)}), f32[64,2048]{1,0:T(8,128)}) %reduce-scatter.21.cloned.1.call-update) | async-done | bytes 524304 | tf_op jit(solution)/shard_map/reduce_scatter | solution.py:364
  (395 shorter events, 488.7 us)
Async XLA Ops:
  7.2 84.6 %all-gather.15.cloned.1.call-start = ((), (), s32[]{:S(2)}) async-start(), calls=%async_computation.17 | async-start | bytes 8650752 | tf_op jit(solution)/shard_map/all_gather | solution.py:111
  9.0 162.4 %all-gather.17.cloned.1.call-start = ((), (), s32[]{:S(2)}) async-start(), calls=%async_computation.18 | async-start | bytes 8650752 | tf_op jit(solution)/shard_map/all_gather | solution.py:112
  10.9 240.1 %all-gather.11.cloned.1.call-start = ((), (), s32[]{:S(2)}) async-start(), calls=%async_computation.15 | async-start | bytes 8650752 | tf_op jit(solution)/shard_map/all_gather | solution.py:113
  12.7 286.8 %all-gather.19.cloned.1.call-start = ((), (), s32[]{:S(2)}) async-start(), calls=%async_computation.19 | async-start | bytes 4718592 | tf_op jit(solution)/shard_map/all_gather | solution.py:158
  181.0 167.5 %all-gather.13.cloned.1.call-start = ((), (), s32[]{:S(2)}) async-start(), calls=%async_computation.16 | async-start | bytes 4718592 | tf_op jit(solution)/shard_map/all_gather | solution.py:159
  256.5 171.6 %all-gather.21.cloned.1.call-start = ((), (), s32[]{:S(2)}) async-start(), calls=%async_computation.20 | async-start | bytes 8650752 | tf_op jit(solution)/shard_map/all_gather | solution.py:114
  257.3 446.1 %all-gather.23.cloned.1.call-start = ((), (), s32[]{:S(2)}) async-start(), calls=%async_computation.21 | async-start | bytes 10485760 | tf_op jit(solution)/shard_map/all_gather | solution.py:133
  267.5 177.6 %all-to-all-start.2 = ((bf16[8,1,2]{2,1,0:T(2,128)(2,1)}), bf16[8,1,2]{2,1,0:T(2,128)(2,1)S(1)}, u32[]{:S(2)}, u32[]{:S(2)}) async-start(bf16[8,1,2]{2,1,0:T(2,128)(2,1)} %convert_element_type.315), calls=%async_computation.2 | async-start | bytes 8192 | tf_op jit(solution)/shard_map/all_to_all | solution.py:202
  445.0 248.8 %all-to-all-start = ((bf16[8,2,128,2048]{3,2,1,0:T(8,128)(2,1)}), bf16[8,2,128,2048]{3,2,1,0:T(8,128)(2,1)}, u32[]{:S(2)}, u32[]{:S(2)}) async-start(bf16[8,2,128,2048]{3,2,1,0:T(8,128)(2,1)} %bitcast.309), calls=%async_computation | async-start | bytes 16777216 | tf_op jit(solution)/shard_map/all_to_all | solution.py:201
  450.1 269.1 %all-gather.25.cloned.1.call-start = ((), (), s32[]{:S(2)}) async-start(), calls=%async_computation.22 | async-start | bytes 10485760 | tf_op jit(solution)/shard_map/all_gather | solution.py:134
  693.8 188.9 %all-to-all-start.3 = ((bf16[8,2,128,2048]{3,2,1,0:T(8,128)(2,1)}), bf16[8,2,128,2048]{3,2,1,0:T(8,128)(2,1)}, u32[]{:S(2)}, u32[]{:S(2)}) async-start(bf16[8,2,128,2048]{3,2,1,0:T(8,128)(2,1)} %bitcast.310), calls=%async_computation.3 | async-start | bytes 16777216 | tf_op jit(solution)/shard_map/all_to_all | solution.py:233
  698.8 92.5 %all-gather.27.cloned.1.call-start = ((), (), s32[]{:S(2)}) async-start(), calls=%async_computation.23 | async-start | bytes 10485760 | tf_op jit(solution)/shard_map/all_gather | solution.py:135
  927.5 188.9 %all-to-all-start.1 = ((bf16[8,2,128,2048]{3,2,1,0:T(8,128)(2,1)}), bf16[8,2,128,2048]{3,2,1,0:T(8,128)(2,1)}, u32[]{:S(2)}, u32[]{:S(2)}) async-start(bf16[8,2,128,2048]{3,2,1,0:T(8,128)(2,1)} %copy.226), calls=%async_computation.1 | async-start | bytes 16777216 | tf_op jit(solution)/shard_map/all_to_all | solution.py:218
  1116.4 188.8 %all-to-all-start.4 = ((bf16[8,2,128,2048]{3,2,1,0:T(8,128)(2,1)}), bf16[8,2,128,2048]{3,2,1,0:T(8,128)(2,1)}, u32[]{:S(2)}, u32[]{:S(2)}) async-start(bf16[8,2,128,2048]{3,2,1,0:T(8,128)(2,1)} %copy.231), calls=%async_computation.4 | async-start | bytes 16777216 | tf_op jit(solution)/shard_map/all_to_all | solution.py:255
  1121.4 348.5 %reduce-scatter.31.cloned.1.call-start = ((), (), s32[]{:S(2)}) async-start(), calls=%async_computation.32 | async-start | bytes 4718592
  1408.7 98.5 %reduce-scatter.15.cloned.1.call-start = ((), (), s32[]{:S(2)}) async-start(), calls=%async_computation.24 | async-start | bytes 4718592 | tf_op jit(solution)/shard_map/reduce_scatter | solution.py:329
  1409.5 232.9 %reduce-scatter.33.cloned.1.call-start = ((), (), s32[]{:S(2)}) async-start(), calls=%async_computation.33 | async-start | bytes 1081344
  1411.2 317.2 %reduce-scatter.29.cloned.1.call-start = ((), (), s32[]{:S(2)}) async-start(), calls=%async_computation.31 | async-start | bytes 10485760 | tf_op jit(solution)/shard_map/reduce_scatter | solution.py:379
  1426.7 391.1 %reduce-scatter.25.cloned.1.call-start = ((), (), s32[]{:S(2)}) async-start(), calls=%async_computation.29 | async-start | bytes 10485760 | tf_op jit(solution)/shard_map/reduce_scatter | solution.py:373
  1441.5 465.9 %reduce-scatter.27.cloned.1.call-start = ((), (), s32[]{:S(2)}) async-start(), calls=%async_computation.30 | async-start | bytes 10485760 | tf_op jit(solution)/shard_map/reduce_scatter | solution.py:376
  1456.5 641.4 %reduce-scatter.23.cloned.1.call-start = ((), (), s32[]{:S(2)}) async-start(), calls=%async_computation.28 | async-start | bytes 17301504 | tf_op jit(solution)/shard_map/reduce_scatter | solution.py:365
  1466.3 818.6 %reduce-scatter.19.cloned.1.call-start = ((), (), s32[]{:S(2)}) async-start(), calls=%async_computation.26 | async-start | bytes 17301504 | tf_op jit(solution)/shard_map/reduce_scatter | solution.py:363
  1489.8 982.3 %reduce-scatter.17.cloned.1.call-start = ((), (), s32[]{:S(2)}) async-start(), calls=%async_computation.25 | async-start | bytes 17301504 | tf_op jit(solution)/shard_map/reduce_scatter | solution.py:362
  1503.3 1155.9 %reduce-scatter.21.cloned.1.call-start = ((), (), s32[]{:S(2)}) async-start(), calls=%async_computation.27 | async-start | bytes 17301504 | tf_op jit(solution)/shard_map/reduce_scatter | solution.py:364
  (74 other events, 3222.5 us)
Sparse Core Ops, SparseCore 0:
  11.6 80.1 all-gather.14
  95.4 76.0 all-gather.16
  175.0 75.9 all-gather.10
  253.0 46.4 all-gather.18
  301.5 46.9 all-gather.12
  352.0 76.1 all-gather.20
  430.5 86.0 all-gather.22
  519.0 87.6 all-gather.24
  703.3 87.9 all-gather.26
  1408.9 47.8 reduce-scatter.30
  1459.1 48.1 reduce-scatter.14
  1509.4 132.9 reduce-scatter.32
  1645.7 82.6 reduce-scatter.28
  1731.3 86.3 reduce-scatter.24
  1821.0 86.3 reduce-scatter.26
  1910.1 187.6 reduce-scatter.22
  2100.6 184.3 reduce-scatter.18
  2287.7 184.3 reduce-scatter.16
  2474.9 184.3 reduce-scatter.20
where the time goes:
time: 2680 us; the launch traced here: 2670 us
  waiting for transfers between devices  1830 us (68%)
  blocking collectives  294 us (11%)
  matrix products  259 us (10%)
  local copies, waits for them, and re-layouts  164 us (6%)
  other arithmetic  75.1 us (3%)
    all_gather x1, blocking collectives, per_device(): lax.all_gather(router.astype(jnp.bfloat16), ('dp', 'expert'), axis=0, til...  210 us
    reduce_scatter x1, waiting for transfers between devices, per_device(): lax.psum_scatter(grad_wv, ('dp', 'expert'), scatter_dimension=0, tiled=True)  187 us
    reduce_scatter x1, waiting for transfers between devices, per_device(): lax.psum_scatter(grad_wq, ('dp', 'expert'), scatter_dimension=0, tiled=True)  187 us
    reduce_scatter x1, waiting for transfers between devices, per_device(): lax.psum_scatter(grad_wk, ('dp', 'expert'), scatter_dimension=0, tiled=True)  187 us
    all_to_all x1, waiting for transfers between devices, per_device(): lax.all_to_all(input_grad, 'expert', split_axis=0, concat_axis=0, tiled=T...  157 us
    all_to_all x1, waiting for transfers between devices, per_device(): lax.all_to_all(expert_out, 'expert', split_axis=0, concat_axis=0, tiled=T...  143 us
    reduce_scatter x1, waiting for transfers between devices, per_device(): lax.psum_scatter(grad_w_out, ('dp', 'expert'), scatter_dimension=0, tiled...  128 us
    unnamed x21, waiting for transfers between devices  127 us
  transfers between devices with their start and end apart: 24, of which 19 were waited for; matrix products, arithmetic and copies ran while one was open for 13% of the time, Pallas kernels for 0%

commit v1 on v0

--- a/solution.py
+++ b/solution.py
@@ -398,43 +398,401 @@
     )
 
 
+FLIP = [(0, 1), (1, 0)]
+
+
+def in_order(own, other, index):
+    first = jnp.where(index == 0, own, other)
+    second = jnp.where(index == 0, other, own)
+    return jnp.stack([first, second])
+
+
+def swap_x(block):
+    return lax.ppermute(block, "dx", FLIP)
+
+
+def swap_y(block):
+    return lax.ppermute(block, "dy", FLIP)
+
+
+def swap_core(block):
+    groups = lax.axis_size("expert")
+    return lax.ppermute(block, "expert", [(i, i ^ 1) for i in range(groups)])
+
+
+def gather_quad(block):
+    pair = in_order(block, swap_x(block), lax.axis_index("dx"))
+    return in_order(pair, swap_y(pair), lax.axis_index("dy"))
+
+
+def scatter_quad(blocks):
+    column, row = lax.axis_index("dx"), lax.axis_index("dy")
+    low = jnp.bfloat16
+    sent = lax.dynamic_index_in_dim(blocks, 1 - column, 1, keepdims=False).astype(low)
+    kept = lax.dynamic_index_in_dim(blocks, column, 1, keepdims=False).astype(jnp.float32)
+    half = kept + swap_x(sent).astype(jnp.float32)
+    sent = lax.dynamic_index_in_dim(half, 1 - row, 0, keepdims=False).astype(low)
+    kept = lax.dynamic_index_in_dim(half, row, 0, keepdims=False)
+    return kept + swap_y(sent).astype(jnp.float32)
+
+
+def sum_experts(values):
+    groups = lax.axis_size("expert")
+    flat = values.reshape(-1, 128)
+    spread = jnp.broadcast_to(flat[None], (groups,) + flat.shape)
+    arrived = lax.all_to_all(spread, "expert", split_axis=0, concat_axis=0)
+    return jnp.sum(arrived, axis=0).reshape(values.shape)
+
+
+def dense_gates(logits, route_ids):
+    columns = jnp.arange(logits.shape[-1])
+    chosen = jnp.any(route_ids[:, :, None] == columns[None, None, :], axis=1)
+    highest = jnp.max(jnp.where(chosen, logits, -jnp.inf), axis=-1, keepdims=True)
+    weights = jnp.where(chosen, jnp.exp(logits - highest), 0.0)
+    return weights / jnp.sum(weights, axis=-1, keepdims=True)
+
+
+def expert_block(rows_in, grad_rows, gates, gate_w, up_w, down_w):
+    wide = jnp.float32
+    gate_pre = jnp.einsum("td,edf->etf", rows_in, gate_w, preferred_element_type=wide)
+    up_pre = jnp.einsum("td,edf->etf", rows_in, up_w, preferred_element_type=wide)
+    back = jnp.einsum("td,efd->etf", grad_rows, down_w, preferred_element_type=wide)
+    sigmoid = jax.nn.sigmoid(gate_pre)
+    silu = gate_pre * sigmoid
+    activity = silu * up_pre
+    gate_grads = jnp.sum(activity * back, axis=-1)
+    weight = gates.T[:, :, None]
+    scaled = (activity * weight).astype(jnp.bfloat16)
+    back = back * weight
+    grad_gate_pre = (back * up_pre * sigmoid * (1.0 + gate_pre * (1.0 - sigmoid))).astype(
+        jnp.bfloat16
+    )
+    grad_up_pre = (back * silu).astype(jnp.bfloat16)
+    grad_in = (
+        jnp.einsum("etf,edf->td", grad_gate_pre, gate_w, preferred_element_type=wide)
+        + jnp.einsum("etf,edf->td", grad_up_pre, up_w, preferred_element_type=wide)
+    ).astype(jnp.bfloat16)
+    mixed = jnp.einsum("etf,efd->td", scaled, down_w, preferred_element_type=wide).astype(
+        jnp.bfloat16
+    )
+    return (grad_in, mixed, gate_grads, scaled, grad_gate_pre, grad_up_pre)
+
+
+def per_device_by_heads(
+    tokens,
+    cotangent,
+    lengths,
+    routes,
+    w_query,
+    w_key,
+    w_value,
+    w_output,
+    router,
+    gain_attn,
+    gain_query,
+    gain_key,
+    gain_mlp,
+    w_gate,
+    w_up,
+    w_down,
+):
+    low, wide = jnp.bfloat16, jnp.float32
+    everyone = ("dy", "dx", "expert")
+    tok_rows, model_width = tokens.shape[1], tokens.shape[2]
+    groups = lax.axis_size("expert")
+    devices = 4 * groups
+    chips = groups // 2
+    seq_len = tok_rows * groups
+    shard = w_query.shape[0]
+    experts = router.shape[1]
+    local_count = experts // groups
+    group = lax.axis_index("expert")
+    chip, core = group // 2, group % 2
+    column, row = lax.axis_index("dx"), lax.axis_index("dy")
+    length = lengths[0]
+    factor = HEAD_DIM ** (-0.5)
+    own_width = 2 * HEAD_DIM
+    tok, cot = tokens[0], cotangent[0]
+
+    packed = jnp.concatenate(
+        [router.T, gain_attn[None], gain_query[None], gain_key[None], gain_mlp[None]], axis=0
+    ).astype(low)
+    pack_rows = experts + 4
+    packed = packed.reshape(-1, 128)
+    packed = lax.all_to_all(
+        jnp.broadcast_to(packed[None], (devices,) + packed.shape),
+        everyone,
+        split_axis=0,
+        concat_axis=0,
+    )
+    packed = (
+        packed.reshape(devices, pack_rows, shard).transpose(1, 0, 2).reshape(pack_rows, model_width)
+    )
+    router_t = packed[:experts]
+    attn_gain, query_gain, key_gain, mlp_gain = (
+        packed[experts + i].astype(wide) for i in range(4)
+    )
+
+    def own_heads(vector):
+        blocks = vector.reshape(2, 2, chips, HEAD_DIM)
+        blocks = lax.dynamic_index_in_dim(blocks, core, 0, keepdims=False)
+        return lax.dynamic_index_in_dim(blocks, chip, 1, keepdims=False).reshape(own_width)
+
+    def spread_heads(vector):
+        at_core = (jnp.arange(2) == core)[:, None, None, None]
+        at_chip = (jnp.arange(chips) == chip)[None, None, :, None]
+        return jnp.where(
+            at_core & at_chip, vector.reshape(1, 2, 1, HEAD_DIM), 0.0
+        ).reshape(model_width)
+
+    def by_heads(weight):
+        blocks = weight.astype(low).reshape(shard, 2, 2, chips, HEAD_DIM)
+        return blocks.transpose(3, 1, 0, 2, 4).reshape(groups, shard, own_width)
+
+    sent = jnp.concatenate([by_heads(w_query), by_heads(w_key), by_heads(w_value)], axis=2)
+    arrived = lax.all_to_all(sent, "expert", split_axis=0, concat_axis=0)
+    qkv_w = gather_quad(arrived.reshape(groups * shard, 3 * own_width)).reshape(
+        model_width, 3 * own_width
+    )
+    tok_all = lax.all_gather(tok, "expert", axis=0, tiled=True)
+
+    out_quad = gather_quad(w_output.astype(low))
+    out_own = lax.dynamic_index_in_dim(out_quad, core, 0, keepdims=False)
+    out_other = swap_core(lax.dynamic_index_in_dim(out_quad, 1 - core, 0, keepdims=False))
+    out_w = jnp.moveaxis(in_order(out_own, out_other, core), 0, 1).reshape(own_width, model_width)
+
+    gate_w, up_w, down_w = w_gate.astype(low), w_up.astype(low), w_down.astype(low)
+    gate_w = jnp.concatenate([gate_w, swap_x(gate_w)], axis=2)
+    up_w = jnp.concatenate([up_w, swap_x(up_w)], axis=2)
+    down_w = jnp.concatenate([down_w, swap_x(down_w)], axis=1)
+    block_width = w_gate.shape[2]
+
+    route_pair = jnp.stack([routes[0], swap_y(routes[0])]).reshape(-1, 128)
+    route_pair = lax.all_to_all(
+        jnp.broadcast_to(route_pair[None], (groups,) + route_pair.shape),
+        "expert",
+        split_axis=0,
+        concat_axis=0,
+    ).reshape(groups, 2, tok_rows, TOP)
+    cot_all = lax.all_gather(cot, "expert", axis=0, tiled=True)
+    cot_near = lax.all_gather(swap_y(cot), "expert", axis=0, tiled=True)
+
+    all_normal_in = tok_all.astype(wide)
+    attn_in, attn_normal, _ = rms_parts(all_normal_in, attn_gain)
+    attn_low = attn_in.astype(low)
+    qkv = jnp.dot(attn_low, qkv_w, preferred_element_type=wide)
+    query_pre, key_pre = qkv[:, :own_width], qkv[:, own_width : 2 * own_width]
+    value_low = qkv[:, 2 * own_width :].astype(low)
+    squares = jnp.stack([jnp.sum(query_pre * query_pre, axis=1), jnp.sum(key_pre * key_pre, axis=1)])
+    squares = sum_experts(squares)
+    factors = lax.rsqrt(squares / model_width + EPSILON)
+    query_factor, key_factor = factors[0][:, None], factors[1][:, None]
+    query_gain_own, key_gain_own = own_heads(query_gain), own_heads(key_gain)
+    query_normal, key_normal = query_pre * query_factor, key_pre * key_factor
+    positions = jnp.arange(seq_len)
+    cosine, sine_part = rope_tables(positions)
+
+    def turned(values, direction):
+        return rotate(values.reshape(seq_len, 2, HEAD_DIM), cosine, sine_part, direction)
+
+    query_low = turned(query_normal * query_gain_own, 1.0).astype(low)
+    key_low = turned(key_normal * key_gain_own, 1.0).astype(low)
+    values = value_low.reshape(seq_len, 2, HEAD_DIM)
+
+    allowed = (positions[None, :] <= positions[:, None]) & (positions[None, :] < length)
+    scores = jnp.einsum("qhd,khd->hqk", query_low, key_low, preferred_element_type=wide) * factor
+    scores = jnp.where(allowed[None], scores, MASKED)
+    log_total = jax.nn.logsumexp(scores, axis=-1)
+    weights_low = jnp.where(allowed[None], jnp.exp(scores - log_total[:, :, None]), 0.0).astype(low)
+    attended = jnp.einsum("hqk,khd->qhd", weights_low, values, preferred_element_type=wide).reshape(
+        seq_len, own_width
+    )
+    attended_low = attended.astype(low)
+    attn_part = jnp.dot(attended_low, out_w, preferred_element_type=wide).astype(low)
+    attn_out = lax.psum_scatter(attn_part, "expert", scatter_dimension=0, tiled=True)
+    hidden = tok.astype(wide) + attn_out.astype(wide)
+    mlp_in, mlp_normal, mlp_factor = rms_parts(hidden, mlp_gain)
+    mlp_low = mlp_in.astype(low)
+    gates_own = dense_gates(times_transpose(mlp_low, router_t), routes[0])
+
+    rows_own = lax.all_gather(mlp_low, "expert", axis=0, tiled=True)
+    rows_near = lax.all_gather(swap_y(mlp_low), "expert", axis=0, tiled=True)
+
+    def expert_part(rows_in, grad_rows, number):
+        ids = route_pair[:, number].reshape(seq_len, TOP)
+        gates = dense_gates(times_transpose(rows_in, router_t), ids)
+        gates = lax.dynamic_slice_in_dim(gates, group * local_count, local_count, 1)
+        return expert_block(rows_in, grad_rows, gates, gate_w, up_w, down_w)
+
+    part_own = expert_part(rows_own, cot_all, 0)
+    part_near = expert_part(rows_near, cot_near, 1)
+
+    def home(own, near):
+        own = lax.psum_scatter(own, "expert", scatter_dimension=0, tiled=True)
+        near = lax.psum_scatter(near, "expert", scatter_dimension=0, tiled=True)
+        return own.astype(wide) + swap_y(near).astype(wide)
+
+    gate_grads = jnp.stack([part_own[2], part_near[2]])
+    gate_grads = gate_grads.reshape(2, local_count, groups, tok_rows).transpose(2, 0, 1, 3)
+    gate_grads = lax.all_to_all(gate_grads, "expert", split_axis=0, concat_axis=0)
+    gate_grads = gate_grads.transpose(1, 3, 0, 2).reshape(2, tok_rows, experts)
+    gate_grads = gate_grads[0] + swap_y(gate_grads[1])
+
+    grad_mlp_in = home(part_own[0], part_near[0])
+    grad_logits = gates_own * (gate_grads - jnp.sum(gates_own * gate_grads, axis=-1, keepdims=True))
+    grad_router = jnp.einsum("te,td->ed", grad_logits, mlp_low.astype(wide), precision=PRECISE)
+    grad_mlp_in = grad_mlp_in + jnp.einsum(
+        "te,ed->td", grad_logits, router_t.astype(wide), precision=PRECISE
+    )
+    grad_out = cot.astype(wide)
+    grad_hidden_norm, grad_gain_mlp = rms_back(grad_mlp_in, mlp_normal, mlp_factor, mlp_gain)
+    grad_hidden = grad_out + grad_hidden_norm
+    grad_attn_all = lax.all_gather(grad_hidden.astype(low), "expert", axis=0, tiled=True)
+
+    grad_w_out = contract_rows(attended_low, grad_attn_all)
+    grad_attended = times_transpose(grad_attn_all, out_w).astype(low)
+    grad_heads = grad_attended.reshape(seq_len, 2, HEAD_DIM)
+    row_delta = jnp.sum(
+        grad_heads.astype(wide) * attended.reshape(seq_len, 2, HEAD_DIM), axis=-1
+    ).T
+    weights_part, grad_scores = score_grads(
+        query_low,
+        key_low,
+        values,
+        grad_heads,
+        log_total,
+        row_delta,
+        positions,
+        positions,
+        length,
+    )
+    grad_query = (
+        jnp.einsum("hqk,khd->qhd", grad_scores, key_low, preferred_element_type=wide) * factor
+    ).astype(low)
+    grad_key = (
+        jnp.einsum("hqk,qhd->khd", grad_scores, query_low, preferred_element_type=wide) * factor
+    ).astype(low)
+    grad_value_low = (
+        jnp.einsum("hqk,qhd->khd", weights_part, grad_heads, preferred_element_type=wide)
+        .astype(low)
+        .reshape(seq_len, own_width)
+    )
+    grad_query_norm = turned(grad_query.astype(wide), -1.0).reshape(seq_len, own_width)
+    grad_key_norm = turned(grad_key.astype(wide), -1.0).reshape(seq_len, own_width)
+    grad_gain_query = jnp.sum(grad_query_norm * query_normal, axis=0)
+    grad_gain_key = jnp.sum(grad_key_norm * key_normal, axis=0)
+    query_scaled, key_scaled = grad_query_norm * query_gain_own, grad_key_norm * key_gain_own
+    inner = jnp.stack(
+        [jnp.sum(query_scaled * query_normal, axis=1), jnp.sum(key_scaled * key_normal, axis=1)]
+    )
+    inner = sum_experts(inner) / model_width
+    grad_query_low = (query_factor * (query_scaled - query_normal * inner[0][:, None])).astype(low)
+    grad_key_low = (key_factor * (key_scaled - key_normal * inner[1][:, None])).astype(low)
+    grad_qkv = jnp.concatenate([grad_query_low, grad_key_low, grad_value_low], axis=1)
+    grad_in_part = times_transpose(grad_qkv, qkv_w)
+    grad_attn_in = lax.psum_scatter(
+        grad_in_part.astype(low), "expert", scatter_dimension=0, tiled=True
+    ).astype(wide)
+    grad_gain_attn = jnp.sum(grad_in_part * attn_normal, axis=0)
+    _, own_normal, own_factor = rms_parts(tok.astype(wide), attn_gain)
+    grad_attn_x, _ = rms_back(grad_attn_in, own_normal, own_factor, attn_gain)
+    grad_tokens = (grad_hidden + grad_attn_x).astype(low)
+
+    grad_w_qkv = contract_rows(attn_low, grad_qkv).reshape(2, 2, groups * shard, 3 * own_width)
+    grad_w_qkv = scatter_quad(grad_w_qkv).astype(low).reshape(groups, shard, 3 * own_width)
+    grad_w_qkv = lax.all_to_all(grad_w_qkv, "expert", split_axis=0, concat_axis=0)
+    grad_w_qkv = grad_w_qkv.reshape(chips, 2, shard, 3, 2, HEAD_DIM).astype(wide)
+    grad_w_qkv = grad_w_qkv.transpose(3, 2, 1, 4, 0, 5).reshape(3, shard, model_width)
+
+    grad_w_out = grad_w_out.reshape(2, 2, shard, model_width)
+    kept = lax.dynamic_index_in_dim(grad_w_out, core, 1, keepdims=False)
+    given = lax.dynamic_index_in_dim(grad_w_out, 1 - core, 1, keepdims=False)
+    grad_w_out = scatter_quad(in_order(kept.astype(low), swap_core(given.astype(low)), core))
+
+    small = jnp.concatenate(
+        [
+            grad_router,
+            grad_gain_attn[None],
+            spread_heads(grad_gain_query)[None],
+            spread_heads(grad_gain_key)[None],
+            grad_gain_mlp[None],
+        ],
+        axis=0,
+    )
+    small = small.reshape(pack_rows, devices, shard).transpose(1, 0, 2).reshape(devices, -1, 128)
+    small = lax.all_to_all(small, everyone, split_axis=0, concat_axis=0)
+    small = jnp.sum(small, axis=0).reshape(pack_rows, shard)
+
+    mix_part = home(part_own[1], part_near[1])
+    output = (hidden + mix_part).astype(low)
+
+    all_rows = jnp.concatenate([rows_own, rows_near], axis=0)
+    all_cot = jnp.concatenate([cot_all, cot_near], axis=0)
+    scaled, grad_gate_pre, grad_up_pre = (
+        jnp.concatenate([part_own[i], part_near[i]], axis=1) for i in (3, 4, 5)
+    )
+    grad_down = jnp.einsum("etf,td->efd", scaled, all_cot, preferred_element_type=wide)
+    grad_gate = jnp.einsum("td,etf->edf", all_rows, grad_gate_pre, preferred_element_type=wide)
+    grad_up = jnp.einsum("td,etf->edf", all_rows, grad_up_pre, preferred_element_type=wide)
+    grad_gate = grad_gate[:, :, :block_width] + swap_x(
+        grad_gate[:, :, block_width:].astype(low)
+    ).astype(wide)
+    grad_up = grad_up[:, :, :block_width] + swap_x(grad_up[:, :, block_width:].astype(low)).astype(
+        wide
+    )
+    grad_down = grad_down[:, :block_width] + swap_x(
+        grad_down[:, block_width:].astype(low)
+    ).astype(wide)
+    return (
+        output[None],
+        grad_tokens[None],
+        grad_w_qkv[0],
+        grad_w_qkv[1],
+        grad_w_qkv[2],
+        grad_w_out,
+        small[:experts].T,
+        small[experts],
+        small[experts + 1],
+        small[experts + 2],
+        small[experts + 3],
+        grad_gate,
+        grad_up,
+        grad_down,
+    )
+
+
+def specs(dp):
+    both = (dp, "expert") if isinstance(dp, str) else dp + ("expert",)
+    rows, weight, vector = P(dp, "expert", None), P(both, None), P(both)
+    columns, depth = P("expert", None, dp), P("expert", dp, None)
+    taken = (rows, rows, P(dp), rows) + (weight,) * 5 + (vector,) * 4 + (columns, columns, depth)
+    given = (rows, rows) + (weight,) * 5 + (vector,) * 4 + (columns, columns, depth)
+    return (taken, given)
+
+
 def solution(mesh):
-    return jax.shard_map(
-        per_device,
-        mesh=mesh,
-        in_specs=(
-            P("dp", "expert", None),
-            P("dp", "expert", None),
-            P("dp"),
-            P("dp", "expert", None),
-            P(("dp", "expert"), None),
-            P(("dp", "expert"), None),
-            P(("dp", "expert"), None),
-            P(("dp", "expert"), None),
-            P(("dp", "expert"), None),
-            P(("dp", "expert")),
-            P(("dp", "expert")),
-            P(("dp", "expert")),
-            P(("dp", "expert")),
-            P("expert", None, "dp"),
-            P("expert", None, "dp"),
-            P("expert", "dp", None),
-        ),
-        out_specs=(
-            P("dp", "expert", None),
-            P("dp", "expert", None),
-            P(("dp", "expert"), None),
-            P(("dp", "expert"), None),
-            P(("dp", "expert"), None),
-            P(("dp", "expert"), None),
-            P(("dp", "expert"), None),
-            P(("dp", "expert")),
-            P(("dp", "expert")),
-            P(("dp", "expert")),
-            P(("dp", "expert")),
-            P("expert", None, "dp"),
-            P("expert", None, "dp"),
-            P("expert", "dp", None),
-        ),
-        check_vma=False,
-    )
+    parts, groups = mesh.shape["dp"], mesh.shape["expert"]
+
+    def whole(*args):
+        model_width = args[0].shape[2]
+        by_heads = (
+            parts == 4
+            and groups % 2 == 0
+            and model_width == 2 * HEAD_DIM * groups
+            and 2 * model_width == parts * groups * HEAD_DIM
+        )
+        if by_heads:
+            used = jax.sharding.Mesh(
+                mesh.devices.reshape(2, 2, groups), ("dy", "dx", "expert")
+            )
+            taken, given = specs(("dy", "dx"))
+            body = per_device_by_heads
+        else:
+            used = mesh
+            taken, given = specs("dp")
+            body = per_device
+        return jax.shard_map(
+            body, mesh=used, in_specs=taken, out_specs=given, check_vma=False
+        )(*args)
+
+    return whole

time: 2680 us -> 910 us (0.34)
  waiting for transfers between devices: 1830 us -> 460 us
  blocking collectives: 294 us -> 0 us
  local copies, waits for them, and re-layouts: 164 us -> 74.3 us
  matrix products: 259 us -> 202 us
  starting transfers between devices: 25.2 us -> 75.2 us
    reduce_scatter x8 -> x6, waiting for transfers between devices: 949 us -> 82.2 us  [the longest x1 48.1 us: per_device_by_heads(): lax.psum_scatter(attn_part, 'expert', scatter_dimension=0, tiled=True)]
    all_to_all x5 -> x8, waiting for transfers between devices: 391 us -> 54.1 us  [the longest x1 38.3 us: per_device_by_heads(): arrived = lax.all_to_all(sent, 'expert', split_axis=0, concat_axis=0)]
    all_gather x9 -> x6, waiting for transfers between devices: 365 us -> 42.4 us  [the longest x1 36 us: per_device_by_heads(): lax.all_gather(grad_hidden.astype(low), 'expert', axis=0, tiled=True)]
    ppermute x0 -> x22, waiting for transfers between devices: none -> 279 us  [the longest x10 215 us: swap_x(): return lax.ppermute(block, 'dx', FLIP)]
    all_gather x1 -> x0, blocking collectives: 210 us -> none  [per_device(): lax.all_gather(router.astype(jnp.bfloat16), ('dp', 'expert'), axis=0, til...]
    unnamed x21 -> x12, waiting for transfers between devices: 127 us -> 1.87 us
    unnamed x2 -> x0, blocking collectives: 84.4 us -> none
    gather x8 -> x0, local copies, waits for them, and re-layouts: 64.3 us -> none  [the longest x1 19.1 us: per_device(): pair_grad[slot_pair].reshape(groups, local_count, slot_cap, model_width)]
  transfers between devices with their start and end apart: 24 -> 42, of which waited for: 19 -> 20; matrix products, arithmetic and copies ran while one was open for 13% -> 33% of each run, Pallas kernels for 0% -> 0%
where the time goes in v1:
time: 910 us; the launch traced here: 900 us
  waiting for transfers between devices  460 us (51%)
  matrix products  202 us (22%)
  starting transfers between devices  75.2 us (8%)
  local copies, waits for them, and re-layouts  74.3 us (8%)
  other arithmetic  72.2 us (8%)
  between operations  16.9 us (2%)
    ppermute x10, waiting for transfers between devices, swap_x(): return lax.ppermute(block, 'dx', FLIP)  215 us
    ppermute x10, waiting for transfers between devices, swap_y(): return lax.ppermute(block, 'dy', FLIP)  64.5 us
    reduce_scatter x1, waiting for transfers between devices, per_device_by_heads(): lax.psum_scatter(attn_part, 'expert', scatter_dimension=0, tiled=True)  48.1 us
    unnamed x186, local copies, waits for them, and re-layouts  38.8 us
    all_to_all x1, waiting for transfers between devices, per_device_by_heads(): arrived = lax.all_to_all(sent, 'expert', split_axis=0, concat_axis=0)  38.3 us
    all_gather x1, waiting for transfers between devices, per_device_by_heads(): lax.all_gather(grad_hidden.astype(low), 'expert', axis=0, tiled=True)  36 us
    reduce_scatter x2, waiting for transfers between devices, home(): own = lax.psum_scatter(own, 'expert', scatter_dimension=0, tiled=True)  34.1 us
    dot_general x2, matrix products, expert_block(): jnp.einsum('td,efd->etf', grad_rows, down_w, preferred_element_type=wide)  23.6 us
  transfers between devices with their start and end apart: 42, of which 20 were waited for; matrix products, arithmetic and copies ran while one was open for 33% of the time, Pallas kernels for 0%

profile of v1, /device:TPU:0, one launch (start us, length us, event | category | flops | bytes accessed | tf_op | source)
XLA Modules:
  0.0 900.0 jit_solution(2188815566426417765)
XLA Ops:
  23.0 38.3 %all-to-all-done.1 = bf16[8,64,768]{2,1,0:T(8,128)(2,1)S(1)} async-done(((bf16[8,64,768]{2,1,0:T(8,128)(2,1)}), bf16[8,64,768]{2,1,0:T(8,128)(2,1)S(1)}, u32[]{:S(2)}, u32[]{:S(2)}) %all-to-all-start.1) | async-done | bytes 786464 | tf_op jit(solution)/shard_map/all_to_all | solution.py:553
  69.4 17.6 %collective-permute-done = bf16[512,768]{1,0:T(8,128)(2,1)S(1)} collective-permute-done((bf16[512,768]{1,0:T(8,128)(2,1)S(1)}, bf16[512,768]{1,0:T(8,128)(2,1)S(1)}, u32[]{:S(2)}, u32[]{:S(2)}) %collective-permute-start) | collective-permute-done | bytes 786464 | tf_op jit(solution)/shard_map/ppermute | solution.py:411
  96.1 28.6 %collective-permute-done.1 = bf16[2,512,768]{2,1,0:T(8,128)(2,1)} collective-permute-done((bf16[2,512,768]{2,1,0:T(8,128)(2,1)}, bf16[2,512,768]{2,1,0:T(8,128)(2,1)}, u32[]{:S(2)}, u32[]{:S(2)}) %collective-permute-start.1) | collective-permute-done | bytes 1572896 | tf_op jit(solution)/shard_map/ppermute | solution.py:415
  171.4 48.1 %reduce-scatter.7.cloned.1.call-done = bf16[128,2048]{1,0:T(8,128)(2,1)} async-done(((bf16[1024,2048]{1,0:T(8,128)(2,1)}), bf16[128,2048]{1,0:T(8,128)(2,1)}) %reduce-scatter.7.cloned.1.call-update) | async-done | bytes 524304 | tf_op jit(solution)/shard_map/reduce_scatter | solution.py:612
  223.6 10.0 %collective-permute-done.9 = bf16[128,2048]{1,0:T(8,128)(2,1)S(1)} collective-permute-done((bf16[128,2048]{1,0:T(8,128)(2,1)S(1)}, bf16[128,2048]{1,0:T(8,128)(2,1)S(1)}, u32[]{:S(2)}, u32[]{:S(2)}) %collective-permute-start.9) | collective-permute-done | bytes 524320 | tf_op jit(solution)/shard_map/ppermute | solution.py:415
  236.1 9.1 %collective-permute-done.11 = bf16[128,2048]{1,0:T(8,128)(2,1)S(1)} collective-permute-done((bf16[128,2048]{1,0:T(8,128)(2,1)S(1)}, bf16[128,2048]{1,0:T(8,128)(2,1)S(1)}, u32[]{:S(2)}, u32[]{:S(2)}) %collective-permute-start.11) | collective-permute-done | bytes 524320 | tf_op jit(solution)/shard_map/ppermute | solution.py:415
  287.3 12.9 %collective-permute-done.6 = bf16[2,2048,256]{1,2,0:T(8,128)(2,1)} collective-permute-done((bf16[2,2048,256]{1,2,0:T(8,128)(2,1)}, bf16[2,2048,256]{1,2,0:T(8,128)(2,1)}, u32[]{:S(2)}, u32[]{:S(2)}) %collective-permute-start.6) | collective-permute-done | bytes 2097184 | tf_op jit(solution)/shard_map/ppermute | solution.py:411
  308.5 76.2 %collective-permute-done.5 = bf16[2,2048,256]{1,2,0:T(8,128)(2,1)} collective-permute-done((bf16[2,2048,256]{1,2,0:T(8,128)(2,1)}, bf16[2,2048,256]{1,2,0:T(8,128)(2,1)}, u32[]{:S(2)}, u32[]{:S(2)}) %collective-permute-start.5) | collective-permute-done | bytes 2097184 | tf_op jit(solution)/shard_map/ppermute | solution.py:411
  392.4 11.8 %fusion.27 = (f32[2,1024]{1,0:T(2,128)S(1)}, bf16[2,1024,512]{1,2,0:T(8,128)(2,1)S(1)}, bf16[2,1024,512]{1,2,0:T(8,128)(2,1)}, bf16[2,1024,512]{1,2,0:T(8,128)(2,1)S(1)}) fusion(f32[2,512,1024]{2,1,0:T(8,128)} %fusion.40, f32[2,512,1024]{2,1,0:T(8,128)} %fusion.42, f32[2,1024]{1,0:T(2,128)S(1)} %fusion.114, ...), kind=kOutput, calls=%fused_computation.51 | convolution fusion | flops 4323276800 | bytes 23085056 | tf_op jit(solution)/shard_map/td,efd->etf/dot_general | solution.py:459
  424.6 8.5 fusion.51
  440.9 11.9 %fusion.30 = (f32[2,1024]{1,0:T(2,128)S(1)}, bf16[2,1024,512]{1,2,0:T(8,128)(2,1)S(1)}, bf16[2,1024,512]{1,2,0:T(8,128)(2,1)}, bf16[2,1024,512]{1,2,0:T(8,128)(2,1)S(1)}) fusion(f32[2,512,1024]{2,1,0:T(8,128)} %fusion.51, f32[2,512,1024]{2,1,0:T(8,128)} %fusion.53, f32[2,1024]{1,0:T(2,128)S(1)} %fusion.113, ...), kind=kOutput, calls=%fused_computation.56 | convolution fusion | flops 4323276800 | bytes 23085056 | tf_op jit(solution)/shard_map/td,efd->etf/dot_general | solution.py:459
  460.7 8.4 fusion.9
  469.7 10.6 %all-to-all-start.4 = ((f32[8,2,2,128]{3,2,1,0:T(2,128)}), f32[8,2,2,128]{3,2,1,0:T(2,128)S(1)}, u32[]{:S(2)}, u32[]{:S(2)}) async-start(f32[8,2,2,128]{3,2,1,0:T(2,128)} %maximum_bitcast_fusion.10), calls=%async_computation.9 | async-start | bytes 32768 | tf_op jit(solution)/shard_map/all_to_all | solution.py:637
  495.5 34.1 %reduce-scatter.13.cloned.1.call-done = bf16[128,2048]{1,0:T(8,128)(2,1)} async-done(((bf16[1024,2048]{1,0:T(8,128)(2,1)}), bf16[128,2048]{1,0:T(8,128)(2,1)}) %reduce-scatter.13.cloned.1.call-update) | async-done | bytes 524304 | tf_op jit(solution)/shard_map/reduce_scatter | solution.py:631
  534.0 9.4 %bitcast_convert_fusion = bf16[1024,2048]{1,0:T(8,128)(2,1)} fusion(bf16[2,1024,512]{1,2,0:T(8,128)(2,1)} %get-tuple-element.109, bf16[2,256,2048]{2,1,0:T(8,128)(2,1)} %collective-permute-done.8, bf16[2,256,2048]{2,1,0:T(8,128)(2,1)} %convert_element_type.369), kind=kOutput, calls=%fused_computation.16 | convolution fusion | flops 4305453056 | bytes 10485760 | tf_op jit(solution)/shard_map/etf,efd->td/dot_general | solution.py:475
  543.4 36.0 %all-gather.15.cloned.1.call-done = bf16[1024,2048]{1,0:T(8,128)(2,1)} async-done(((bf16[128,2048]{1,0:T(8,128)(2,1)}), bf16[1024,2048]{1,0:T(8,128)(2,1)}) %all-gather.15.cloned.1.call-update) | async-done | bytes 4194320 | tf_op jit(solution)/shard_map/all_gather | solution.py:650
  630.2 8.4 bitcast_convert_fusion.1
  638.6 12.7 %fusion.5 = f32[2,512,2048]{2,1,0:T(8,128)S(1)} fusion(bf16[1024,2048]{1,0:T(8,128)(2,1)} %all-gather.13.cloned.1.call-done, bf16[1024,2048]{1,0:T(8,128)(2,1)} %bitcast.435, bf16[2,1024,512]{1,2,0:T(8,128)(2,1)} %get-tuple-element.109, bf16[2,1024,512]{1,2,0:T(8,128)(2,1)} %get-tuple-element.111), kind=kOutput, calls=%fused_computation.9 | convolution fusion | flops 8615100416 | bytes 20971520 | tf_op jit(solution)/shard_map/etf,td->efd/dot_general | solution.py:734
  656.6 12.7 %fusion.14 = f32[2,2048,512]{1,2,0:T(8,128)} fusion(bf16[1024,2048]{1,0:T(8,128)(2,1)S(1)} %copy-done.11, bf16[1024,2048]{1,0:T(8,128)(2,1)S(1)} %copy-done.13, bf16[2,1024,512]{1,2,0:T(8,128)(2,1)S(1)} %copy-done.82, bf16[2,1024,512]{1,2,0:T(8,128)(2,1)} %copy-done.83), kind=kOutput, calls=%fused_computation.27 | convolution fusion | flops 8615100416 | bytes 20971520 | tf_op jit(solution)/shard_map/td,etf->edf/dot_general | solution.py:735
  669.4 11.2 %fusion.15 = f32[2,2048,512]{1,2,0:T(8,128)S(1)} fusion(bf16[1024,2048]{1,0:T(8,128)(2,1)S(1)} %copy-done.11, bf16[1024,2048]{1,0:T(8,128)(2,1)S(1)} %copy-done.13, bf16[2,1024,512]{1,2,0:T(8,128)(2,1)} %copy-done.85, bf16[2,1024,512]{1,2,0:T(8,128)(2,1)} %copy-done.86), kind=kOutput, calls=%fused_computation.28 | convolution fusion | flops 8615100416 | bytes 20971520 | tf_op jit(solution)/shard_map/td,etf->edf/dot_general | solution.py:736
  692.0 9.7 %collective-permute-done.21 = bf16[2,256,2048]{2,1,0:T(8,128)(2,1)} collective-permute-done((bf16[2,256,2048]{2,1,0:T(8,128)(2,1)}, bf16[2,256,2048]{2,1,0:T(8,128)(2,1)}, u32[]{:S(2)}, u32[]{:S(2)}) %collective-permute-start.21) | collective-permute-done | bytes 2097184 | tf_op jit(solution)/shard_map/ppermute | solution.py:411
  717.6 28.9 %collective-permute-done.19 = bf16[2,2048,256]{1,2,0:T(8,128)(2,1)S(1)} collective-permute-done((bf16[2,2048,256]{1,2,0:T(8,128)(2,1)}, bf16[2,2048,256]{1,2,0:T(8,128)(2,1)S(1)}, u32[]{:S(2)}, u32[]{:S(2)}) %collective-permute-start.19) | collective-permute-done | bytes 2097184 | tf_op jit(solution)/shard_map/ppermute | solution.py:411
  757.8 69.4 %collective-permute-done.14 = bf16[2,512,768]{2,1,0:T(8,128)(2,1)} collective-permute-done((bf16[2,512,768]{2,1,0:T(8,128)(2,1)}, bf16[2,512,768]{2,1,0:T(8,128)(2,1)}, u32[]{:S(2)}, u32[]{:S(2)}) %collective-permute-start.14) | collective-permute-done | bytes 1572896 | tf_op jit(solution)/shard_map/ppermute | solution.py:411
  870.3 9.4 %all-to-all-done.6 = bf16[8,64,768]{2,1,0:T(8,128)(2,1)S(1)} async-done(((bf16[8,64,768]{2,1,0:T(8,128)(2,1)}), bf16[8,64,768]{2,1,0:T(8,128)(2,1)S(1)}, u32[]{:S(2)}, u32[]{:S(2)}) %all-to-all-start.6) | async-done | bytes 786464 | tf_op jit(solution)/shard_map/all_to_all | solution.py:703
  (438 shorter events, 349.3 us)
Async XLA Ops:
  7.2 121.1 %all-gather.17.cloned.1.call-start = ((), (), s32[]{:S(2)}) async-start(), calls=%async_computation.24 | async-start | bytes 4718592 | tf_op jit(solution)/shard_map/all_gather | solution.py:557
  12.8 48.5 %all-to-all-start.1 = ((bf16[8,64,768]{2,1,0:T(8,128)(2,1)}), bf16[8,64,768]{2,1,0:T(8,128)(2,1)S(1)}, u32[]{:S(2)}, u32[]{:S(2)}) async-start(bf16[8,64,768]{2,1,0:T(8,128)(2,1)} %pad_maximum_fusion.8), calls=%async_computation.1 | async-start | bytes 1572864 | tf_op jit(solution)/shard_map/all_to_all | solution.py:553
  19.2 48.6 %collective-permute-start.2 = (bf16[64,2048]{1,0:T(8,128)(2,1)S(1)}, bf16[64,2048]{1,0:T(8,128)(2,1)S(1)}, u32[]{:S(2)}, u32[]{:S(2)}) collective-permute-start(bf16[64,2048]{1,0:T(8,128)(2,1)S(1)} %convert_element_type.360), channel_id=1, source_target_pairs={{0,8},{8,0},{1,9},{9,1},{2,10},{10,2},{3,11},{11,3},{4,12},{12,4},... | collective-permute-start | bytes 786440 | tf_op jit(solution)/shard_map/ppermute | solution.py:411
  143.3 76.2 %reduce-scatter.7.cloned.1.call-start = ((), (), s32[]{:S(2)}) async-start(), calls=%async_computation.14 | async-start | bytes 4718592 | tf_op jit(solution)/shard_map/reduce_scatter | solution.py:612
  171.3 112.4 %all-gather.11.cloned.1.call-start = ((), (), s32[]{:S(2)}) async-start(), calls=%async_computation.17 | async-start | bytes 4718592 | tf_op jit(solution)/shard_map/all_gather | solution.py:619
  234.5 157.9 %all-gather.13.cloned.1.call-start = ((), (), s32[]{:S(2)}) async-start(), calls=%async_computation.20 | async-start | bytes 4718592 | tf_op jit(solution)/shard_map/all_gather | solution.py:578
  246.0 174.9 %all-gather.9.cloned.1.call-start = ((), (), s32[]{:S(2)}) async-start(), calls=%async_computation.15 | async-start | bytes 4718592 | tf_op jit(solution)/shard_map/all_gather | solution.py:618
  251.3 48.9 %collective-permute-start.6 = (bf16[2,2048,256]{1,2,0:T(8,128)(2,1)}, bf16[2,2048,256]{1,2,0:T(8,128)(2,1)}, u32[]{:S(2)}, u32[]{:S(2)}) collective-permute-start(bf16[2,2048,256]{1,2,0:T(8,128)(2,1)} %copy.199), channel_id=1, source_target_pairs={{0,8},{8,0},{1,9},{9,1},{2,10},{10,2},{3,11},{11,3},{4,12},{12,4},... | collective-permute-start | bytes 6291464 | tf_op jit(solution)/shard_map/ppermute | solution.py:411
  264.5 176.4 %all-gather.19.cloned.1.call-start = ((), (), s32[]{:S(2)}) async-start(), calls=%async_computation.25 | async-start | bytes 4718592 | tf_op jit(solution)/shard_map/all_gather | solution.py:577
  265.1 215.6 %reduce-scatter.15.cloned.1.call-start = ((), (), s32[]{:S(2)}) async-start(), calls=%async_computation.21 | async-start | bytes 4718592 | tf_op jit(solution)/shard_map/reduce_scatter | solution.py:632
  269.4 123.0 %collective-permute-start.8 = (bf16[2,256,2048]{2,1,0:T(8,128)(2,1)}, bf16[2,256,2048]{2,1,0:T(8,128)(2,1)}, u32[]{:S(2)}, u32[]{:S(2)}) collective-permute-start(bf16[2,256,2048]{2,1,0:T(8,128)(2,1)} %convert_element_type.369), channel_id=1, source_target_pairs={{0,8},{8,0},{1,9},{9,1},{2,10},{10,2},{3,11},{11,3},{4,12},{12,4},... | collective-permute-start | bytes 6291464 | tf_op jit(solution)/shard_map/ppermute | solution.py:411
  274.9 109.8 %collective-permute-start.5 = (bf16[2,2048,256]{1,2,0:T(8,128)(2,1)}, bf16[2,2048,256]{1,2,0:T(8,128)(2,1)}, u32[]{:S(2)}, u32[]{:S(2)}) collective-permute-start(bf16[2,2048,256]{1,2,0:T(8,128)(2,1)} %copy.198), channel_id=1, source_target_pairs={{0,8},{8,0},{1,9},{9,1},{2,10},{10,2},{3,11},{11,3},{4,12},{12,4},... | collective-permute-start | bytes 6291464 | tf_op jit(solution)/shard_map/ppermute | solution.py:411
  420.6 109.0 %reduce-scatter.13.cloned.1.call-start = ((), (), s32[]{:S(2)}) async-start(), calls=%async_computation.19 | async-start | bytes 4718592 | tf_op jit(solution)/shard_map/reduce_scatter | solution.py:631
  480.4 99.0 %all-gather.15.cloned.1.call-start = ((), (), s32[]{:S(2)}) async-start(), calls=%async_computation.22 | async-start | bytes 4718592 | tf_op jit(solution)/shard_map/all_gather | solution.py:650
  480.7 48.9 %collective-permute-start.12 = (bf16[128,2048]{1,0:T(8,128)(2,1)}, bf16[128,2048]{1,0:T(8,128)(2,1)S(1)}, u32[]{:S(2)}, u32[]{:S(2)}) collective-permute-start(bf16[128,2048]{1,0:T(8,128)(2,1)} %reduce-scatter.15.cloned.1.call-done), channel_id=1, source_target_pairs={{0,16},{16,0},{1,17},{17,1},{2,18},{18,2},{3,19},{19,3},{4,20},{20... | collective-permute-start | bytes 1572872 | tf_op jit(solution)/shard_map/ppermute | solution.py:415
  534.0 317.1 %reduce-scatter.11.cloned.1.call-start = ((), (), s32[]{:S(2)}) async-start(), calls=%async_computation.18 | async-start | bytes 4718592 | tf_op jit(solution)/shard_map/reduce_scatter | solution.py:632
  610.2 277.8 %reduce-scatter.17.cloned.1.call-start = ((), (), s32[]{:S(2)}) async-start(), calls=%async_computation.23 | async-start | bytes 4718592 | tf_op jit(solution)/shard_map/reduce_scatter | solution.py:693
  628.6 260.9 %reduce-scatter.9.cloned.1.call-start = ((), (), s32[]{:S(2)}) async-start(), calls=%async_computation.16 | async-start | bytes 4718592 | tf_op jit(solution)/shard_map/reduce_scatter | solution.py:631
  652.9 48.8 %collective-permute-start.21 = (bf16[2,256,2048]{2,1,0:T(8,128)(2,1)}, bf16[2,256,2048]{2,1,0:T(8,128)(2,1)}, u32[]{:S(2)}, u32[]{:S(2)}) collective-permute-start(bf16[2,256,2048]{2,1,0:T(8,128)(2,1)} %slice.270), channel_id=1, source_target_pairs={{0,8},{8,0},{1,9},{9,1},{2,10},{10,2},{3,11},{11,3},{4,12},{12,4},... | collective-permute-start | bytes 6291464 | tf_op jit(solution)/shard_map/ppermute | solution.py:411
  689.3 57.2 %collective-permute-start.19 = (bf16[2,2048,256]{1,2,0:T(8,128)(2,1)}, bf16[2,2048,256]{1,2,0:T(8,128)(2,1)S(1)}, u32[]{:S(2)}, u32[]{:S(2)}) collective-permute-start(bf16[2,2048,256]{1,2,0:T(8,128)(2,1)} %slice.272), channel_id=1, source_target_pairs={{0,8},{8,0},{1,9},{9,1},{2,10},{10,2},{3,11},{11,3},{4,12},{12,4},... | collective-permute-start | bytes 6291464 | tf_op jit(solution)/shard_map/ppermute | solution.py:411
  690.8 143.8 %collective-permute-start.20 = (bf16[2,2048,256]{1,2,0:T(8,128)(2,1)}, bf16[2,2048,256]{1,2,0:T(8,128)(2,1)}, u32[]{:S(2)}, u32[]{:S(2)}) collective-permute-start(bf16[2,2048,256]{1,2,0:T(8,128)(2,1)} %slice.271), channel_id=1, source_target_pairs={{0,8},{8,0},{1,9},{9,1},{2,10},{10,2},{3,11},{11,3},{4,12},{12,4},... | collective-permute-start | bytes 6291464 | tf_op jit(solution)/shard_map/ppermute | solution.py:411
  716.1 111.1 %collective-permute-start.14 = (bf16[2,512,768]{2,1,0:T(8,128)(2,1)}, bf16[2,512,768]{2,1,0:T(8,128)(2,1)}, u32[]{:S(2)}, u32[]{:S(2)}) collective-permute-start(bf16[2,512,768]{2,1,0:T(8,128)(2,1)} %fusion.61), channel_id=1, source_target_pairs={{0,8},{8,0},{1,9},{9,1},{2,10},{10,2},{3,11},{11,3},{4,12},{12,4},... | collective-permute-start | bytes 4718600 | tf_op jit(solution)/shard_map/ppermute | solution.py:411
  717.6 38.9 %collective-permute-start.16 = (bf16[2,64,2048]{2,1,0:T(8,128)(2,1)S(1)}, bf16[2,64,2048]{2,1,0:T(8,128)(2,1)}, u32[]{:S(2)}, u32[]{:S(2)}) collective-permute-start(bf16[2,64,2048]{2,1,0:T(8,128)(2,1)S(1)} %fusion.93), channel_id=1, source_target_pairs={{0,1},{1,0},{2,3},{3,2},{4,5},{5,4},{6,7},{7,6},{8,9},{9,8},{10,11... | collective-permute-start | bytes 1572872 | tf_op jit(solution)/shard_map/ppermute | solution.py:420
  750.6 103.2 %all-to-all-start.7 = ((f32[32,10,128]{2,1,0:T(8,128)}), f32[32,10,128]{2,1,0:T(8,128)S(1)}, u32[]{:S(2)}, u32[]{:S(2)}) async-start(f32[32,10,128]{2,1,0:T(8,128)} %reshape.461), calls=%async_computation.13 | async-start | bytes 524288 | tf_op jit(solution)/shard_map/all_to_all | solution.py:723
  (107 other events, 1664.5 us)
Sparse Core Ops, SparseCore 0:
  9.6 68.7 all-gather.16
  171.4 48.0 reduce-scatter.6
  234.6 49.0 all-gather.10
  285.7 45.8 all-gather.12
  333.6 45.8 all-gather.8
  381.0 45.8 all-gather.18
  429.7 48.7 reduce-scatter.14
  481.4 48.1 reduce-scatter.12
  534.1 45.2 all-gather.14
  581.6 49.7 reduce-scatter.10
  633.7 48.1 reduce-scatter.16
  684.0 48.1 reduce-scatter.8

commit v2 on v1

--- a/solution.py
+++ b/solution.py
@@ -1,6 +1,11 @@
+import functools
+
 import jax
 import jax.numpy as jnp
 from jax import lax
+from jax.experimental import pallas as pl
+from jax.experimental.layout import Layout, with_layout_constraint
+from jax.experimental.pallas import tpu as pltpu
 from jax.sharding import PartitionSpec as P
 
 HEAD_DIM = 128
@@ -420,20 +425,67 @@
     return lax.ppermute(block, "expert", [(i, i ^ 1) for i in range(groups)])
 
 
-def gather_quad(block):
-    pair = in_order(block, swap_x(block), lax.axis_index("dx"))
-    return in_order(pair, swap_y(pair), lax.axis_index("dy"))
-
-
-def scatter_quad(blocks):
+def row_major(value):
+    return with_layout_constraint(value, Layout(major_to_minor=tuple(range(value.ndim))))
+
+
+def together(*values):
+    return lax.optimization_barrier(values)
+
+
+def gather_first(block):
+    return (block, swap_x(block), swap_y(block))
+
+
+def gather_second(block, beside, below):
+    half = block.shape[0] // 2
+    return (block, beside, below, swap_x(below[:half]), swap_y(beside[half:]))
+
+
+def gather_last(block, beside, below, upper, under):
+    column, row = lax.axis_index("dx"), lax.axis_index("dy")
+    across = jnp.concatenate([upper, under], axis=0)
+    return in_order(in_order(block, beside, column), in_order(below, across, column), row)
+
+
+def scatter_first(blocks):
     column, row = lax.axis_index("dx"), lax.axis_index("dy")
     low = jnp.bfloat16
-    sent = lax.dynamic_index_in_dim(blocks, 1 - column, 1, keepdims=False).astype(low)
-    kept = lax.dynamic_index_in_dim(blocks, column, 1, keepdims=False).astype(jnp.float32)
-    half = kept + swap_x(sent).astype(jnp.float32)
-    sent = lax.dynamic_index_in_dim(half, 1 - row, 0, keepdims=False).astype(low)
-    kept = lax.dynamic_index_in_dim(half, row, 0, keepdims=False)
-    return kept + swap_y(sent).astype(jnp.float32)
+
+    def pick(at_row, at_column):
+        line = lax.dynamic_index_in_dim(blocks, at_row, 0, keepdims=False)
+        return lax.dynamic_index_in_dim(line, at_column, 0, keepdims=False)
+
+    half = blocks.shape[2] // 2
+    across = pick(1 - row, 1 - column).astype(low)
+    beside, below = pick(row, 1 - column), pick(1 - row, column)
+    return (
+        pick(row, column),
+        beside[:half],
+        below[half:],
+        swap_x(beside[half:].astype(low)),
+        swap_y(below[:half].astype(low)),
+        swap_y(across[:half]),
+        swap_x(across[half:]),
+    )
+
+
+def scatter_ready(kept, beside, below, from_beside, from_below, far_below, far_beside):
+    low, wide = jnp.bfloat16, jnp.float32
+    beside = (beside + far_below.astype(wide)).astype(low)
+    below = (below + far_beside.astype(wide)).astype(low)
+    return (kept, beside, below, from_beside, from_below)
+
+
+def scatter_last(kept, beside, below, from_beside, from_below):
+    wide = jnp.float32
+    added = jnp.concatenate(
+        [
+            swap_x(beside).astype(wide) + from_below.astype(wide),
+            from_beside.astype(wide) + swap_y(below).astype(wide),
+        ]
+    )
+    return kept + added
 
 
 def sum_experts(values):
@@ -452,10 +504,339 @@
     return weights / jnp.sum(weights, axis=-1, keepdims=True)
 
 
-def expert_block(rows_in, grad_rows, gates, gate_w, up_w, down_w):
+def mul_nn(left_side, right_side):
+    return jnp.dot(left_side, right_side, preferred_element_type=jnp.float32)
+
+
+VMEM_BYTES = 56 * 1024 * 1024
+ROWS = 256
+
+
+def whole_blocks(count):
+    return [pl.BlockSpec(memory_space=pltpu.VMEM)] * count
+
+
+def turn(values, cosine, signed_sine):
+    return values * cosine + pltpu.roll(values, HEAD_DIM // 2, 1) * signed_sine
+
+
+def allowed_block(first_row, rows, columns, length):
+    at_row = first_row + lax.broadcasted_iota(jnp.int32, (rows, columns), 0)
+    at_column = lax.broadcasted_iota(jnp.int32, (rows, columns), 1)
+    return (at_column <= at_row) & (at_column < length)
+
+
+def attend_kernel(
+    length_ref,
+    qkv_ref,
+    query_factor_ref,
+    key_factor_ref,
+    query_gain_ref,
+    key_gain_ref,
+    cosine_ref,
+    sine_ref,
+    out_w_ref,
+    query_ref,
+    key_ref,
+    value_ref,
+    attended_ref,
+    total_ref,
+    part_ref,
+):
+    low = jnp.bfloat16
+    seq_len, heads = qkv_ref.shape[0], 2
+    length = length_ref[0]
+    width = heads * HEAD_DIM
+    factor = HEAD_DIM ** (-0.5)
+
+    @pl.loop(0, seq_len // ROWS)
+    def _(number):
+        rows = pl.ds(pl.multiple_of(number * ROWS, ROWS), ROWS)
+        cosine, sine_part = cosine_ref[rows, :], sine_ref[rows, :]
+        for head in range(heads):
+            part = slice(head * HEAD_DIM, (head + 1) * HEAD_DIM)
+            later = slice(width + head * HEAD_DIM, width + (head + 1) * HEAD_DIM)
+            query = qkv_ref[rows, part] * query_factor_ref[rows, :] * query_gain_ref[:, part]
+            key = qkv_ref[rows, later] * key_factor_ref[rows, :] * key_gain_ref[:, part]
+            query_ref[rows, part] = turn(query, cosine, sine_part).astype(low)
+            key_ref[rows, part] = turn(key, cosine, sine_part).astype(low)
+        value_ref[rows, :] = qkv_ref[rows, 2 * width :].astype(low)
+
+    for number in range(seq_len // ROWS):
+        first, end = number * ROWS, (number + 1) * ROWS
+        allowed = allowed_block(first, ROWS, end, length)
+        done = []
+        for head in range(heads):
+            part = slice(head * HEAD_DIM, (head + 1) * HEAD_DIM)
+            scores = times_transpose(query_ref[first:end, part], key_ref[:end, part]) * factor
+            scores = jnp.where(allowed, scores, MASKED)
+            highest = jnp.max(scores, axis=1, keepdims=True)
+            weights = jnp.exp(scores - highest)
+            total = jnp.sum(weights, axis=1, keepdims=True)
+            weights = (weights * (1.0 / total)).astype(low)
+            total_ref[head, first:end, :] = highest + jnp.log(total)
+            attended = mul_nn(weights, value_ref[:end, part])
+            attended_ref[first:end, part] = attended
+            done.append(attended.astype(low))
+        part_ref[first:end, :] = mul_nn(jnp.concatenate(done, axis=1), out_w_ref[...]).astype(low)
+
+
+def attend(length, qkv, query_factor, key_factor, query_gain, key_gain, cosine, sine_part, out_w):
+    seq_len, width, model_width = qkv.shape[0], qkv.shape[1] // 3, out_w.shape[1]
+    low, wide = jnp.bfloat16, jnp.float32
+    rows = jax.ShapeDtypeStruct((seq_len, width), low)
+    return pl.pallas_call(
+        attend_kernel,
+        in_specs=[pl.BlockSpec(memory_space=pltpu.SMEM)] + whole_blocks(8),
+        out_specs=whole_blocks(6),
+        out_shape=[
+            rows,
+            rows,
+            rows,
+            jax.ShapeDtypeStruct((seq_len, width), wide),
+            jax.ShapeDtypeStruct((2, seq_len, 1), wide),
+            jax.ShapeDtypeStruct((seq_len, model_width), low),
+        ],
+        compiler_params=pltpu.CompilerParams(vmem_limit_bytes=VMEM_BYTES),
+        cost_estimate=pl.CostEstimate(
+            flops=2 * seq_len * width * (seq_len + model_width),
+            bytes_accessed=14 * seq_len * width + 2 * seq_len * model_width,
+            transcendentals=seq_len * seq_len,
+        ),
+    )(length, qkv, query_factor, key_factor, query_gain, key_gain, cosine, sine_part, out_w)
+
+
+def attend_back_kernel(
+    length_ref,
+    upstream_ref,
+    out_w_ref,
+    attended_ref,
+    total_ref,
+    query_ref,
+    key_ref,
+    value_ref,
+    qkv_ref,
+    query_factor_ref,
+    key_factor_ref,
+    query_gain_ref,
+    key_gain_ref,
+    cosine_ref,
+    sine_ref,
+    grad_value_ref,
+    query_scaled_ref,
+    key_scaled_ref,
+    query_inner_ref,
+    key_inner_ref,
+    query_gain_grad_ref,
+    key_gain_grad_ref,
+    key_sum_ref,
+    value_sum_ref,
+):
+    low, wide = jnp.bfloat16, jnp.float32
+    seq_len, heads = qkv_ref.shape[0], 2
+    length = length_ref[0]
+    width = heads * HEAD_DIM
+    factor = HEAD_DIM ** (-0.5)
+    blocks = seq_len // ROWS
+
+    def norm_back(sums, rows, head, offset, factor_ref, gain_ref, scaled_ref, inner_ref, grad_ref, fresh):
+        part = slice(head * HEAD_DIM, (head + 1) * HEAD_DIM)
+        place = slice(offset + head * HEAD_DIM, offset + (head + 1) * HEAD_DIM)
+        upstream = turn(sums.astype(low).astype(wide), cosine_ref[rows, :], -sine_ref[rows, :])
+        normal = qkv_ref[rows, place] * factor_ref[rows, :]
+        gain_part = jnp.sum(upstream * normal, axis=0, keepdims=True)
+        scaled = upstream * gain_ref[:, part]
+        scaled_ref[rows, part] = scaled
+        inner = jnp.sum(scaled * normal, axis=1, keepdims=True)
+        if head == 0:
+            inner_ref[rows, :] = inner
+        else:
+            inner_ref[rows, :] += inner
+        if fresh:
+            grad_ref[:, part] = gain_part
+        else:
+            grad_ref[:, part] += gain_part
+
+    for number in reversed(range(blocks)):
+        first, end = number * ROWS, (number + 1) * ROWS
+        allowed = allowed_block(first, ROWS, end, length)
+        rows = slice(first, end)
+        grads = times_transpose(upstream_ref[rows, :], out_w_ref[...]).astype(low)
+        for head in range(heads):
+            part = slice(head * HEAD_DIM, (head + 1) * HEAD_DIM)
+            query, keys = query_ref[rows, part], key_ref[:end, part]
+            grad = grads[:, part]
+            delta = jnp.sum(grad.astype(wide) * attended_ref[rows, part], axis=1, keepdims=True)
+            scores = times_transpose(query, keys) * factor
+            weights = jnp.where(allowed, jnp.exp(scores - total_ref[head, rows, :]), 0.0)
+            grad_weights = times_transpose(grad, value_ref[:end, part])
+            grad_scores = (weights * (grad_weights - delta)).astype(low)
+            query_sum = mul_nn(grad_scores, keys) * factor
+            key_sum = contract_rows(grad_scores, query)
+            value_sum = contract_rows(weights.astype(low), grad)
+            if number == blocks - 1:
+                key_sum_ref[:, part] = key_sum
+                value_sum_ref[:, part] = value_sum
+            else:
+                key_sum_ref[:end, part] += key_sum
+                value_sum_ref[:end, part] += value_sum
+            norm_back(
+                query_sum,
+                rows,
+                head,
+                0,
+                query_factor_ref,
+                query_gain_ref,
+                query_scaled_ref,
+                query_inner_ref,
+                query_gain_grad_ref,
+                number == blocks - 1,
+            )
+    for number in range(blocks):
+        rows = slice(number * ROWS, (number + 1) * ROWS)
+        grad_value_ref[rows, :] = value_sum_ref[rows, :].astype(low)
+        for head in range(heads):
+            part = slice(head * HEAD_DIM, (head + 1) * HEAD_DIM)
+            norm_back(
+                key_sum_ref[rows, part] * factor,
+                rows,
+                head,
+                width,
+                key_factor_ref,
+                key_gain_ref,
+                key_scaled_ref,
+                key_inner_ref,
+                key_gain_grad_ref,
+                number == 0,
+            )
+
+
+def attend_back(length, upstream, out_w, attended, total, query, key, value, qkv, *rest):
+    seq_len, width = attended.shape
+    low, wide = jnp.bfloat16, jnp.float32
+    shape = jax.ShapeDtypeStruct
+    return pl.pallas_call(
+        attend_back_kernel,
+        in_specs=[pl.BlockSpec(memory_space=pltpu.SMEM)] + whole_blocks(14),
+        out_specs=whole_blocks(7),
+        out_shape=[
+            shape((seq_len, width), low),
+            shape((seq_len, width), wide),
+            shape((seq_len, width), wide),
+            shape((seq_len, 1), wide),
+            shape((seq_len, 1), wide),
+            shape((1, width), wide),
+            shape((1, width), wide),
+        ],
+        scratch_shapes=[pltpu.VMEM((seq_len, width), wide), pltpu.VMEM((seq_len, width), wide)],
+        compiler_params=pltpu.CompilerParams(vmem_limit_bytes=VMEM_BYTES),
+        cost_estimate=pl.CostEstimate(
+            flops=2 * seq_len * width * (3 * seq_len + upstream.shape[1]),
+            bytes_accessed=30 * seq_len * width + 2 * upstream.size,
+            transcendentals=seq_len * seq_len,
+        ),
+    )(length, upstream, out_w, attended, total, query, key, value, qkv, *rest)
+
+
+def put_halves(outs, received, place, expert, axis, value):
+    low, wide = jnp.bfloat16, jnp.float32
+    length = value.shape[axis] // 2
+    for half in range(2):
+        span = slice(half * length, (half + 1) * length)
+        at = (span, slice(None)) if axis == 0 else (slice(None), span)
+        number = 2 * place + half
+        if received is None:
+            outs[number][...] = value[at].astype(low)
+        else:
+            outs[expert[0]][(expert[1],) + at] = value[at] + received[number][...].astype(wide)
+
+
+def tall_kernel(count, adding, *refs):
+    outs = refs[2 + (8 if adding else 4) * count :]
+    received = refs[2 + 4 * count : 2 + 8 * count] if adding else None
+    first, second = refs[0][...].T, refs[1][...].T
+    for kind in range(2):
+        for expert in range(count):
+            place = count * kind + expert
+            one, two = refs[2 + 2 * place], refs[3 + 2 * place]
+            value = mul_nn(first, one[...]) + mul_nn(second, two[...])
+            put_halves(outs, received, place, (kind, expert), 1, value)
+
+
+def flat_kernel(count, adding, *refs):
+    outs = refs[2 + (4 if adding else 2) * count : -1]
+    received = refs[2 + 2 * count : 2 + 4 * count] if adding else None
+    turned_ref = refs[-1]
+    length, block = refs[2].shape
+
+    @pl.when(pl.program_id(0) == 0)
+    def _():
+        for expert in range(count):
+            for half in range(2):
+                turned_ref[
+                    expert * block : (expert + 1) * block, half * length : (half + 1) * length
+                ] = refs[2 + 2 * expert + half][...].T
+
+    for expert in range(count):
+        span = slice(expert * block, (expert + 1) * block)
+        value = mul_nn(turned_ref[span, :length], refs[0][...]) + mul_nn(
+            turned_ref[span, length:], refs[1][...]
+        )
+        put_halves(outs, received, expert, (0, expert), 0, value)
+
+
+def weight_grads(rows, sources, which, tall, received=None):
+    length, model_width = rows[0].shape
+    count, _, doubled = sources[0][0].shape
+    block = doubled // 2
+    tile = min(256, model_width)
+    columns = pl.BlockSpec((length, tile), lambda i: (0, i))
+    operands, in_specs = list(rows), [columns] * 2
+    for pair in sources:
+        for expert in range(count):
+            operands += list(pair)
+            in_specs += [
+                pl.BlockSpec(
+                    (None, length, block),
+                    lambda i, expert=expert: (expert, 0, which),
+                    pipeline_mode=pl.Buffered(1),
+                )
+            ] * 2
+    kinds = len(sources)
+    if tall:
+        piece, shape = pl.BlockSpec((tile, block // 2), lambda i: (i, 0)), (model_width, block // 2)
+        full = pl.BlockSpec((count, tile, block), lambda i: (0, i, 0))
+        full_shape = (count, model_width, block)
+    else:
+        piece, shape = pl.BlockSpec((block // 2, tile), lambda i: (0, i)), (block // 2, model_width)
+        full = pl.BlockSpec((count, block, tile), lambda i: (0, 0, i))
+        full_shape = (count, block, model_width)
+    pieces = 2 * count * kinds
+    if received is None:
+        out_specs, shapes, dtype = [piece] * pieces, [shape] * pieces, jnp.bfloat16
+    else:
+        operands += list(received)
+        in_specs += [piece] * pieces
+        out_specs, shapes, dtype = [full] * kinds, [full_shape] * kinds, jnp.float32
+    scratch = [] if tall else [pltpu.VMEM((count * block, 2 * length), jnp.bfloat16)]
+    return pl.pallas_call(
+        functools.partial(tall_kernel if tall else flat_kernel, count, received is not None),
+        grid=(model_width // tile,),
+        in_specs=in_specs,
+        out_specs=out_specs,
+        out_shape=[jax.ShapeDtypeStruct(shape, dtype) for shape in shapes],
+        scratch_shapes=scratch,
+        compiler_params=pltpu.CompilerParams(vmem_limit_bytes=VMEM_BYTES),
+        cost_estimate=pl.CostEstimate(
+            flops=4 * length * model_width * count * block * kinds,
+            bytes_accessed=4 * length * model_width + 6 * count * model_width * block * kinds,
+            transcendentals=0,
+        ),
+    )(*operands)
+
+
+def expert_block(gate_pre, up_pre, grad_rows, gates, gate_w, up_w, down_w):
     wide = jnp.float32
-    gate_pre = jnp.einsum("td,edf->etf", rows_in, gate_w, preferred_element_type=wide)
-    up_pre = jnp.einsum("td,edf->etf", rows_in, up_w, preferred_element_type=wide)
     back = jnp.einsum("td,efd->etf", grad_rows, down_w, preferred_element_type=wide)
     sigmoid = jax.nn.sigmoid(gate_pre)
     silu = gate_pre * sigmoid
@@ -472,10 +853,7 @@
         jnp.einsum("etf,edf->td", grad_gate_pre, gate_w, preferred_element_type=wide)
         + jnp.einsum("etf,edf->td", grad_up_pre, up_w, preferred_element_type=wide)
     ).astype(jnp.bfloat16)
-    mixed = jnp.einsum("etf,efd->td", scaled, down_w, preferred_element_type=wide).astype(
-        jnp.bfloat16
-    )
-    return (grad_in, mixed, gate_grads, scaled, grad_gate_pre, grad_up_pre)
+    return (grad_in, gate_grads, scaled, grad_gate_pre, grad_up_pre)
 
 
 def per_device_by_heads(
@@ -514,25 +892,6 @@
     own_width = 2 * HEAD_DIM
     tok, cot = tokens[0], cotangent[0]
 
-    packed = jnp.concatenate(
-        [router.T, gain_attn[None], gain_query[None], gain_key[None], gain_mlp[None]], axis=0
-    ).astype(low)
-    pack_rows = experts + 4
-    packed = packed.reshape(-1, 128)
-    packed = lax.all_to_all(
-        jnp.broadcast_to(packed[None], (devices,) + packed.shape),
-        everyone,
-        split_axis=0,
-        concat_axis=0,
-    )
-    packed = (
-        packed.reshape(devices, pack_rows, shard).transpose(1, 0, 2).reshape(pack_rows, model_width)
-    )
-    router_t = packed[:experts]
-    attn_gain, query_gain, key_gain, mlp_gain = (
-        packed[experts + i].astype(wide) for i in range(4)
-    )
-
     def own_heads(vector):
         blocks = vector.reshape(2, 2, chips, HEAD_DIM)
         blocks = lax.dynamic_index_in_dim(blocks, core, 0, keepdims=False)
@@ -550,95 +909,189 @@
         return blocks.transpose(3, 1, 0, 2, 4).reshape(groups, shard, own_width)
 
     sent = jnp.concatenate([by_heads(w_query), by_heads(w_key), by_heads(w_value)], axis=2)
+    packed = jnp.concatenate(
+        [router.T, gain_attn[None], gain_query[None], gain_key[None], gain_mlp[None]], axis=0
+    ).astype(low)
+    pack_rows = experts + 4
+    packed = packed.reshape(-1, 128)
+    sent, packed, out_rows, gate_own = together(
+        sent, packed, w_output.astype(low), row_major(w_gate.astype(low))
+    )
     arrived = lax.all_to_all(sent, "expert", split_axis=0, concat_axis=0)
-    qkv_w = gather_quad(arrived.reshape(groups * shard, 3 * own_width)).reshape(
-        model_width, 3 * own_width
+    gate_far = [swap_x(gate_own[0])]
+    up_own, down_own = row_major(w_up.astype(low)), row_major(w_down.astype(low))
+    held = together(
+        arrived, packed, gate_far[0], gate_own, up_own, down_own, cot, *gather_first(out_rows)
+    )
+    arrived, packed, gate_far[0], gate_own, up_own, down_own, cot = held[:7]
+    out_parts = held[7:]
+    packed = lax.all_to_all(
+        jnp.broadcast_to(packed[None], (devices,) + packed.shape),
+        everyone,
+        split_axis=0,
+        concat_axis=0,
+    )
+    qkv_parts = gather_first(arrived.reshape(groups * shard, 3 * own_width))
+    held = together(packed, *qkv_parts, *gather_second(*out_parts))
+    packed, qkv_parts, out_parts = held[0], held[1:4], held[4:]
+    packed = (
+        packed.reshape(devices, pack_rows, shard).transpose(1, 0, 2).reshape(pack_rows, model_width)
+    )
+    router_t = packed[:experts]
+    attn_gain, query_gain, key_gain, mlp_gain = (
+        packed[experts + i].astype(wide) for i in range(4)
     )
     tok_all = lax.all_gather(tok, "expert", axis=0, tiled=True)
-
-    out_quad = gather_quad(w_output.astype(low))
+    attn_in, attn_normal, _ = rms_parts(tok_all.astype(wide), attn_gain)
+    held = together(attn_in.astype(low), *gather_second(*qkv_parts))
+    attn_low, qkv_parts = held[0], held[1:]
+    qkv_w = gather_last(*qkv_parts).reshape(model_width, 3 * own_width)
+
+    cot_all = lax.all_gather(cot, "expert", axis=0, tiled=True)
+    cot_half = lax.dynamic_slice_in_dim(cot_all, core * (seq_len // 2), seq_len // 2, 0)
+    cot_half = swap_y(cot_half)
+
+    qkv = jnp.dot(attn_low, qkv_w, preferred_element_type=wide)
+    qkv, *out_parts = together(qkv, *out_parts)
+    out_quad = gather_last(*out_parts)
     out_own = lax.dynamic_index_in_dim(out_quad, core, 0, keepdims=False)
     out_other = swap_core(lax.dynamic_index_in_dim(out_quad, 1 - core, 0, keepdims=False))
     out_w = jnp.moveaxis(in_order(out_own, out_other, core), 0, 1).reshape(own_width, model_width)
-
-    gate_w, up_w, down_w = w_gate.astype(low), w_up.astype(low), w_down.astype(low)
-    gate_w = jnp.concatenate([gate_w, swap_x(gate_w)], axis=2)
-    up_w = jnp.concatenate([up_w, swap_x(up_w)], axis=2)
-    down_w = jnp.concatenate([down_w, swap_x(down_w)], axis=1)
-    block_width = w_gate.shape[2]
-
-    route_pair = jnp.stack([routes[0], swap_y(routes[0])]).reshape(-1, 128)
+    query_pre, key_pre = qkv[:, :own_width], qkv[:, own_width : 2 * own_width]
+    squares = jnp.stack([jnp.sum(query_pre * query_pre, axis=1), jnp.sum(key_pre * key_pre, axis=1)])
+    squares = sum_experts(squares)
+    factors = lax.rsqrt(squares / model_width + EPSILON)
+    near_routes = swap_y(routes[0])
+    factors, near_routes = together(factors, near_routes)
+    query_factor, key_factor = factors[0][:, None], factors[1][:, None]
+    query_gain_own, key_gain_own = own_heads(query_gain), own_heads(key_gain)
+    cosine, sine_part = rope_tables(jnp.arange(seq_len))
+    cosine = jnp.concatenate([cosine[:, 0], cosine[:, 0]], axis=1)
+    sine_part = jnp.concatenate([-sine_part[:, 0], sine_part[:, 0]], axis=1)
+    norm_args = (
+        query_factor,
+        key_factor,
+        query_gain_own[None],
+        key_gain_own[None],
+        cosine,
+        sine_part,
+    )
+    query_low, key_low, value_low, attended, log_total, attn_part = attend(
+        lengths, qkv, *norm_args, out_w
+    )
+    attended_low = attended.astype(low)
+    attn_part, cot_all, gate_own, up_own, down_own = together(
+        attn_part, cot_all, gate_own, up_own, down_own
+    )
+    attn_out = lax.psum_scatter(attn_part, "expert", scatter_dimension=0, tiled=True)
+    gate_far += [swap_x(gate_own[i]) for i in range(1, local_count)]
+    up_far = [swap_x(up_own[0])]
+    route_pair = jnp.stack([routes[0], near_routes]).reshape(-1, 128)
     route_pair = lax.all_to_all(
         jnp.broadcast_to(route_pair[None], (groups,) + route_pair.shape),
         "expert",
         split_axis=0,
         concat_axis=0,
     ).reshape(groups, 2, tok_rows, TOP)
-    cot_all = lax.all_gather(cot, "expert", axis=0, tiled=True)
-    cot_near = lax.all_gather(swap_y(cot), "expert", axis=0, tiled=True)
-
-    all_normal_in = tok_all.astype(wide)
-    attn_in, attn_normal, _ = rms_parts(all_normal_in, attn_gain)
-    attn_low = attn_in.astype(low)
-    qkv = jnp.dot(attn_low, qkv_w, preferred_element_type=wide)
-    query_pre, key_pre = qkv[:, :own_width], qkv[:, own_width : 2 * own_width]
-    value_low = qkv[:, 2 * own_width :].astype(low)
-    squares = jnp.stack([jnp.sum(query_pre * query_pre, axis=1), jnp.sum(key_pre * key_pre, axis=1)])
-    squares = sum_experts(squares)
-    factors = lax.rsqrt(squares / model_width + EPSILON)
-    query_factor, key_factor = factors[0][:, None], factors[1][:, None]
-    query_gain_own, key_gain_own = own_heads(query_gain), own_heads(key_gain)
-    query_normal, key_normal = query_pre * query_factor, key_pre * key_factor
-    positions = jnp.arange(seq_len)
-    cosine, sine_part = rope_tables(positions)
-
-    def turned(values, direction):
-        return rotate(values.reshape(seq_len, 2, HEAD_DIM), cosine, sine_part, direction)
-
-    query_low = turned(query_normal * query_gain_own, 1.0).astype(low)
-    key_low = turned(key_normal * key_gain_own, 1.0).astype(low)
-    values = value_low.reshape(seq_len, 2, HEAD_DIM)
-
-    allowed = (positions[None, :] <= positions[:, None]) & (positions[None, :] < length)
-    scores = jnp.einsum("qhd,khd->hqk", query_low, key_low, preferred_element_type=wide) * factor
-    scores = jnp.where(allowed[None], scores, MASKED)
-    log_total = jax.nn.logsumexp(scores, axis=-1)
-    weights_low = jnp.where(allowed[None], jnp.exp(scores - log_total[:, :, None]), 0.0).astype(low)
-    attended = jnp.einsum("hqk,khd->qhd", weights_low, values, preferred_element_type=wide).reshape(
-        seq_len, own_width
-    )
-    attended_low = attended.astype(low)
-    attn_part = jnp.dot(attended_low, out_w, preferred_element_type=wide).astype(low)
-    attn_out = lax.psum_scatter(attn_part, "expert", scatter_dimension=0, tiled=True)
+    held = together(attn_out, cot_half, route_pair, up_far[0], up_own, down_own, *gate_far)
+    attn_out, cot_half, route_pair, up_far[0], up_own, down_own = held[:6]
+    gate_far = held[6:]
+    up_far += [swap_x(up_own[i]) for i in range(1, local_count)]
+    down_far = [swap_x(down_own[0])]
+    cot_near = in_order(cot_half, swap_core(cot_half), core).reshape(seq_len, model_width)
     hidden = tok.astype(wide) + attn_out.astype(wide)
     mlp_in, mlp_normal, mlp_factor = rms_parts(hidden, mlp_gain)
     mlp_low = mlp_in.astype(low)
     gates_own = dense_gates(times_transpose(mlp_low, router_t), routes[0])
 
     rows_own = lax.all_gather(mlp_low, "expert", axis=0, tiled=True)
-    rows_near = lax.all_gather(swap_y(mlp_low), "expert", axis=0, tiled=True)
-
-    def expert_part(rows_in, grad_rows, number):
+    mlp_near = swap_y(mlp_low)
+    gate_w = jnp.concatenate([gate_own, jnp.stack(gate_far)], axis=2)
+    cot_near, *up_far = together(cot_near, *up_far)
+    up_w = jnp.concatenate([up_own, jnp.stack(up_far)], axis=2)
+    held = together(rows_own, mlp_near, cot_near, gate_w, up_w, down_far[0], down_own)
+    rows_own, mlp_near, cot_near, gate_w, up_w, down_far[0], down_own = held
+    down_far += [swap_x(down_own[i]) for i in range(1, local_count)]
+    block_width = w_gate.shape[2]
+    rows_near = lax.all_gather(mlp_near, "expert", axis=0, tiled=True)
+
+    def gates_of(rows_in, number):
         ids = route_pair[:, number].reshape(seq_len, TOP)
         gates = dense_gates(times_transpose(rows_in, router_t), ids)
-        gates = lax.dynamic_slice_in_dim(gates, group * local_count, local_count, 1)
-        return expert_block(rows_in, grad_rows, gates, gate_w, up_w, down_w)
-
-    part_own = expert_part(rows_own, cot_all, 0)
-    part_near = expert_part(rows_near, cot_near, 1)
-
-    def home(own, near):
-        own = lax.psum_scatter(own, "expert", scatter_dimension=0, tiled=True)
-        near = lax.psum_scatter(near, "expert", scatter_dimension=0, tiled=True)
-        return own.astype(wide) + swap_y(near).astype(wide)
-
-    gate_grads = jnp.stack([part_own[2], part_near[2]])
+        return lax.dynamic_slice_in_dim(gates, group * local_count, local_count, 1)
+
+    def into(rows_in, weight):
+        return jnp.einsum("td,edf->etf", rows_in, weight, preferred_element_type=wide)
+
+    own_gates, own_up_pre = gates_of(rows_own, 0), into(rows_own, up_w)
+    held = together(own_gates, own_up_pre, *down_far)
+    own_gates, own_up_pre, down_far = held[0], held[1], held[2:]
+    down_w = jnp.concatenate([down_own, jnp.stack(down_far)], axis=1)
+    part_own = expert_block(
+        into(rows_own, gate_w), own_up_pre, cot_all, own_gates, gate_w, up_w, down_w
+    )
+    rows_near, *part_own = together(rows_near, *part_own)
+    part_near = expert_block(
+        into(rows_near, gate_w),
+        into(rows_near, up_w),
+        cot_near,
+        gates_of(rows_near, 1),
+        gate_w,
+        up_w,
+        down_w,
+    )
+
+    grad_in_own = lax.psum_scatter(part_own[0], "expert", scatter_dimension=0, tiled=True)
+    near_in, grad_in_own = together(part_near[0], grad_in_own)
+    grad_in_near = lax.psum_scatter(near_in, "expert", scatter_dimension=0, tiled=True)
+
+    tall_sources = [(part_own[i], part_near[i]) for i in (3, 4)]
+    flat_sources = [(part_own[2], part_near[2])]
+    rows_pair, cot_pair = (rows_own, rows_near), (cot_all, cot_near)
+    far = list(weight_grads(rows_pair, tall_sources, 1, True))
+    chunks = []
+    for size in (1, 1, 1, 4, 1):
+        chunks.append(far[: size * local_count // 2])
+        far = far[size * local_count // 2 :]
+
+    def send(number):
+        chunks[number] = [swap_x(piece) for piece in chunks[number]]
+
+    def tied(values, *numbers):
+        held = together(*values, *[piece for i in numbers for piece in chunks[i]])
+        place = len(values)
+        for i in numbers:
+            chunks[i] = list(held[place : place + len(chunks[i])])
+            place += len(chunks[i])
+        return held[: len(values)]
+
+    cot_pair = (cot_all, tied((cot_near,), 0)[0])
+    send(0)
+    far = list(weight_grads(cot_pair, flat_sources, 1, False))
+    for size in (2, 2):
+        chunks.append(far[: size * local_count // 2])
+        far = far[size * local_count // 2 :]
+    (near_scaled,) = tied((part_near[2],), 0, 1, 5, 6)
+
+    def mix(scaled):
+        return jnp.einsum("etf,efd->td", scaled, down_w, preferred_element_type=wide).astype(low)
+
+    gate_grads = jnp.stack([part_own[1], part_near[1]])
     gate_grads = gate_grads.reshape(2, local_count, groups, tok_rows).transpose(2, 0, 1, 3)
     gate_grads = lax.all_to_all(gate_grads, "expert", split_axis=0, concat_axis=0)
+    own_mixed, near_mixed = mix(part_own[2]), mix(near_scaled)
+    send(1)
+    own_mixed, near_mixed, gate_grads = tied((own_mixed, near_mixed, gate_grads), 1)
+    half_rows = seq_len // 2
+    mixed_kept = lax.dynamic_slice_in_dim(near_mixed, core * half_rows, half_rows, 0)
+    mixed_sent = lax.dynamic_slice_in_dim(near_mixed, (1 - core) * half_rows, half_rows, 0)
+    mixed_half = (mixed_kept.astype(wide) + swap_core(mixed_sent).astype(wide)).astype(low)
+
     gate_grads = gate_grads.transpose(1, 3, 0, 2).reshape(2, tok_rows, experts)
     gate_grads = gate_grads[0] + swap_y(gate_grads[1])
-
-    grad_mlp_in = home(part_own[0], part_near[0])
+    grad_in_near, gate_grads = tied((grad_in_near, gate_grads), 2)
+    send(2)
+    grad_mlp_in = grad_in_own.astype(wide) + swap_y(grad_in_near).astype(wide)
     grad_logits = gates_own * (gate_grads - jnp.sum(gates_own * gate_grads, axis=-1, keepdims=True))
     grad_router = jnp.einsum("te,td->ed", grad_logits, mlp_low.astype(wide), precision=PRECISE)
     grad_mlp_in = grad_mlp_in + jnp.einsum(
@@ -647,67 +1100,66 @@
     grad_out = cot.astype(wide)
     grad_hidden_norm, grad_gain_mlp = rms_back(grad_mlp_in, mlp_normal, mlp_factor, mlp_gain)
     grad_hidden = grad_out + grad_hidden_norm
-    grad_attn_all = lax.all_gather(grad_hidden.astype(low), "expert", axis=0, tiled=True)
-
-    grad_w_out = contract_rows(attended_low, grad_attn_all)
-    grad_attended = times_transpose(grad_attn_all, out_w).astype(low)
-    grad_heads = grad_attended.reshape(seq_len, 2, HEAD_DIM)
-    row_delta = jnp.sum(
-        grad_heads.astype(wide) * attended.reshape(seq_len, 2, HEAD_DIM), axis=-1
-    ).T
-    weights_part, grad_scores = score_grads(
+    grad_attn_low, mixed_half = tied((grad_hidden.astype(low), mixed_half), 2, 3)
+    grad_attn_all = lax.all_gather(grad_attn_low, "expert", axis=0, tiled=True)
+    mixed_half = swap_y(mixed_half)
+    send(3)
+
+    grad_attn_all, mixed_half = tied((grad_attn_all, mixed_half), 3, 4)
+    send(4)
+    mixed = own_mixed.astype(wide)
+    half_own = lax.dynamic_slice_in_dim(mixed, core * half_rows, half_rows, 0)
+    mixed = lax.dynamic_update_slice_in_dim(
+        own_mixed, (half_own + mixed_half.astype(wide)).astype(low), core * half_rows, 0
+    )
+    mixed = lax.psum_scatter(mixed, "expert", scatter_dimension=0, tiled=True)
+    grad_value_low, query_scaled, key_scaled, query_inner, key_inner, *gain_grads = attend_back(
+        lengths,
+        grad_attn_all,
+        out_w,
+        attended,
+        log_total,
         query_low,
         key_low,
-        values,
-        grad_heads,
-        log_total,
-        row_delta,
-        positions,
-        positions,
-        length,
-    )
-    grad_query = (
-        jnp.einsum("hqk,khd->qhd", grad_scores, key_low, preferred_element_type=wide) * factor
-    ).astype(low)
-    grad_key = (
-        jnp.einsum("hqk,qhd->khd", grad_scores, query_low, preferred_element_type=wide) * factor
-    ).astype(low)
-    grad_value_low = (
-        jnp.einsum("hqk,qhd->khd", weights_part, grad_heads, preferred_element_type=wide)
-        .astype(low)
-        .reshape(seq_len, own_width)
-    )
-    grad_query_norm = turned(grad_query.astype(wide), -1.0).reshape(seq_len, own_width)
-    grad_key_norm = turned(grad_key.astype(wide), -1.0).reshape(seq_len, own_width)
-    grad_gain_query = jnp.sum(grad_query_norm * query_normal, axis=0)
-    grad_gain_key = jnp.sum(grad_key_norm * key_normal, axis=0)
-    query_scaled, key_scaled = grad_query_norm * query_gain_own, grad_key_norm * key_gain_own
-    inner = jnp.stack(
-        [jnp.sum(query_scaled * query_normal, axis=1), jnp.sum(key_scaled * key_normal, axis=1)]
-    )
-    inner = sum_experts(inner) / model_width
+        value_low,
+        qkv,
+        *norm_args,
+    )
+    held = tied(
+        (grad_value_low, query_scaled, key_scaled, query_inner, key_inner, grad_attn_all), 4
+    )
+    grad_value_low, query_scaled, key_scaled, query_inner, key_inner, grad_attn_all = held
+    grad_w_out = contract_rows(attended_low, grad_attn_all).reshape(2, 2, shard, model_width)
+    kept = lax.dynamic_index_in_dim(grad_w_out, core, 1, keepdims=False)
+    given = lax.dynamic_index_in_dim(grad_w_out, 1 - core, 1, keepdims=False)
+    grad_w_out = in_order(kept.astype(low), swap_core(given.astype(low)), core)
+    grad_gain_query, grad_gain_key = gain_grads[0][0], gain_grads[1][0]
+
+    def by_parts(upstream):
+        return contract_rows(attn_low, upstream).reshape(2, 2, groups * shard, -1)
+
+    query_normal, key_normal = query_pre * query_factor, key_pre * key_factor
+    inner = jnp.stack([query_inner[:, 0], key_inner[:, 0]])
+    inner = sum_experts(inner)
+    inner, grad_w_out = tied((inner, grad_w_out), 5)
+    send(5)
+    out_parts = scatter_first(grad_w_out)
+    inner = inner / model_width
     grad_query_low = (query_factor * (query_scaled - query_normal * inner[0][:, None])).astype(low)
     grad_key_low = (key_factor * (key_scaled - key_normal * inner[1][:, None])).astype(low)
     grad_qkv = jnp.concatenate([grad_query_low, grad_key_low, grad_value_low], axis=1)
+    grad_qkv, mixed = together(grad_qkv, mixed)
+    qkv_w_grad = by_parts(grad_qkv)
+    grad_qkv, qkv_w_grad = together(grad_qkv, qkv_w_grad)
+    qkv_parts = scatter_first(qkv_w_grad)
     grad_in_part = times_transpose(grad_qkv, qkv_w)
-    grad_attn_in = lax.psum_scatter(
-        grad_in_part.astype(low), "expert", scatter_dimension=0, tiled=True
-    ).astype(wide)
+    grad_in_low, *qkv_parts = tied((grad_in_part.astype(low), *qkv_parts), 5)
+    grad_attn_in = lax.psum_scatter(grad_in_low, "expert", scatter_dimension=0, tiled=True)
+    grad_attn_in = grad_attn_in.astype(wide)
     grad_gain_attn = jnp.sum(grad_in_part * attn_normal, axis=0)
     _, own_normal, own_factor = rms_parts(tok.astype(wide), attn_gain)
     grad_attn_x, _ = rms_back(grad_attn_in, own_normal, own_factor, attn_gain)
     grad_tokens = (grad_hidden + grad_attn_x).astype(low)
-
-    grad_w_qkv = contract_rows(attn_low, grad_qkv).reshape(2, 2, groups * shard, 3 * own_width)
-    grad_w_qkv = scatter_quad(grad_w_qkv).astype(low).reshape(groups, shard, 3 * own_width)
-    grad_w_qkv = lax.all_to_all(grad_w_qkv, "expert", split_axis=0, concat_axis=0)
-    grad_w_qkv = grad_w_qkv.reshape(chips, 2, shard, 3, 2, HEAD_DIM).astype(wide)
-    grad_w_qkv = grad_w_qkv.transpose(3, 2, 1, 4, 0, 5).reshape(3, shard, model_width)
-
-    grad_w_out = grad_w_out.reshape(2, 2, shard, model_width)
-    kept = lax.dynamic_index_in_dim(grad_w_out, core, 1, keepdims=False)
-    given = lax.dynamic_index_in_dim(grad_w_out, 1 - core, 1, keepdims=False)
-    grad_w_out = scatter_quad(in_order(kept.astype(low), swap_core(given.astype(low)), core))
 
     small = jnp.concatenate(
         [
@@ -720,29 +1172,37 @@
         axis=0,
     )
     small = small.reshape(pack_rows, devices, shard).transpose(1, 0, 2).reshape(devices, -1, 128)
+    held = tied((*scatter_ready(*qkv_parts), *scatter_ready(*out_parts), small, *rows_pair), 4)
+    qkv_parts, out_parts, small, rows_pair = held[:5], held[5:10], held[10], held[11:]
     small = lax.all_to_all(small, everyone, split_axis=0, concat_axis=0)
     small = jnp.sum(small, axis=0).reshape(pack_rows, shard)
-
-    mix_part = home(part_own[1], part_near[1])
-    output = (hidden + mix_part).astype(low)
-
-    all_rows = jnp.concatenate([rows_own, rows_near], axis=0)
-    all_cot = jnp.concatenate([cot_all, cot_near], axis=0)
-    scaled, grad_gate_pre, grad_up_pre = (
-        jnp.concatenate([part_own[i], part_near[i]], axis=1) for i in (3, 4, 5)
-    )
-    grad_down = jnp.einsum("etf,td->efd", scaled, all_cot, preferred_element_type=wide)
-    grad_gate = jnp.einsum("td,etf->edf", all_rows, grad_gate_pre, preferred_element_type=wide)
-    grad_up = jnp.einsum("td,etf->edf", all_rows, grad_up_pre, preferred_element_type=wide)
-    grad_gate = grad_gate[:, :, :block_width] + swap_x(
-        grad_gate[:, :, block_width:].astype(low)
-    ).astype(wide)
-    grad_up = grad_up[:, :, :block_width] + swap_x(grad_up[:, :, block_width:].astype(low)).astype(
-        wide
-    )
-    grad_down = grad_down[:, :block_width] + swap_x(
-        grad_down[:, block_width:].astype(low)
-    ).astype(wide)
+    grad_gate, grad_up = weight_grads(
+        rows_pair,
+        tall_sources,
+        0,
+        True,
+        received=[piece for chunk in chunks[:5] for piece in chunk],
+    )
+    grad_w_qkv = scatter_last(*qkv_parts).astype(low)
+    grad_w_out = scatter_last(*out_parts)
+    small, grad_w_qkv, grad_w_out, grad_gate, grad_up = tied(
+        (small, grad_w_qkv, grad_w_out, grad_gate, grad_up), 6
+    )
+    send(6)
+    grad_w_qkv = grad_w_qkv.reshape(groups, shard, 3 * own_width)
+    grad_w_qkv = lax.all_to_all(grad_w_qkv, "expert", split_axis=0, concat_axis=0)
+    (grad_down,) = weight_grads(
+        cot_pair,
+        flat_sources,
+        0,
+        False,
+        received=[piece for chunk in chunks[5:] for piece in chunk],
+    )
+    grad_w_qkv, grad_down, grad_tokens = together(grad_w_qkv, grad_down, grad_tokens)
+    grad_w_qkv = grad_w_qkv.reshape(chips, 2, shard, 3, 2, HEAD_DIM).astype(wide)
+    grad_w_qkv = grad_w_qkv.transpose(3, 2, 1, 4, 0, 5).reshape(3, shard, model_width)
+
+    output = (hidden + mixed.astype(wide)).astype(low)
     return (
         output[None],
         grad_tokens[None],

time: 910 us -> 662 us (0.73)
  waiting for transfers between devices: 460 us -> 229 us
  matrix products: 202 us -> 120 us
  Pallas kernels: 0 us -> 80.5 us
  local copies, waits for them, and re-layouts: 74.3 us -> 53.9 us
  starting transfers between devices: 75.2 us -> 84.7 us
    pallas_call x0 -> x6, Pallas kernels: none -> 80.5 us  [the longest x4 52.7 us: weight_grads(): pl.pallas_call(functools.partial(tall_kernel if tall else flat_kernel, co...]
    dot_general x16 -> x6, matrix products: 112 us -> 43.8 us  [the longest x4 29.1 us: into(): jnp.einsum('td,edf->etf', rows_in, weight, preferred_element_type=wide)]
    reduce_scatter x1, waiting for transfers between devices: 48.1 us -> 0.01 us  [per_device_by_heads(): lax.psum_scatter(attn_part, 'expert', scatter_dimension=0, tiled=True)]
    ppermute x10 -> x16, waiting for transfers between devices: 64.5 us -> 16.9 us  [swap_y(): return lax.ppermute(block, 'dy', FLIP)]
    ppermute x10 -> x28, waiting for transfers between devices: 215 us -> 171 us  [swap_x(): return lax.ppermute(block, 'dx', FLIP)]
    all_gather x3 -> x2, waiting for transfers between devices: 42.4 us -> 0.01 us  [the longest x1 0.01 us: per_device_by_heads(): rows_near = lax.all_gather(mlp_near, 'expert', axis=0, tiled=True)]
    unnamed x186 -> x192, local copies, waits for them, and re-layouts: 38.8 us -> 6.32 us
    all_to_all x1, waiting for transfers between devices: 38.3 us -> 10.4 us  [per_device_by_heads(): arrived = lax.all_to_all(sent, 'expert', split_axis=0, concat_axis=0)]
  transfers between devices with their start and end apart: 42 -> 66, of which waited for: 20 -> 30; matrix products, arithmetic and copies ran while one was open for 33% -> 35% of each run, Pallas kernels for 0% -> 12%
where the time goes in v2:
time: 662 us; the launch traced here: 656 us
  waiting for transfers between devices  229 us (35%)
  matrix products  120 us (18%)
  starting transfers between devices  84.7 us (13%)
  Pallas kernels  80.5 us (12%)
  other arithmetic  71.3 us (11%)
  local copies, waits for them, and re-layouts  53.9 us (8%)
  between operations  16.7 us (3%)
    ppermute x28, waiting for transfers between devices, swap_x(): return lax.ppermute(block, 'dx', FLIP)  171 us
    pallas_call x4, Pallas kernels, weight_grads(): pl.pallas_call(functools.partial(tall_kernel if tall else flat_kernel, co...  52.7 us
    dot_general x4, matrix products, into(): jnp.einsum('td,edf->etf', rows_in, weight, preferred_element_type=wide)  29.1 us
    ppermute x28, starting transfers between devices, swap_x(): return lax.ppermute(block, 'dx', FLIP)  28.8 us
    dot_general x2, matrix products, expert_block(): jnp.einsum('td,efd->etf', grad_rows, down_w, preferred_element_type=wide)  20.7 us
    ppermute x16, starting transfers between devices, swap_y(): return lax.ppermute(block, 'dy', FLIP)  19.9 us
    ppermute x16, waiting for transfers between devices, swap_y(): return lax.ppermute(block, 'dy', FLIP)  16.9 us
    dot_general x2, matrix products, expert_block(): jnp.einsum('etf,edf->td', grad_up_pre, up_w, preferred_element_type=wide)  16.6 us
  transfers between devices with their start and end apart: 66, of which 30 were waited for; matrix products, arithmetic and copies ran while one was open for 35% of the time, Pallas kernels for 12%

profile of v2, /device:TPU:0, one launch (start us, length us, event | category | flops | bytes accessed | tf_op | source)
XLA Modules:
  0.0 656.5 jit_solution(4820911283668914478)
XLA Ops:
  31.0 22.2 %collective-permute-done.1 = bf16[64,2048]{1,0:T(8,128)(2,1)S(1)} collective-permute-done((bf16[64,2048]{1,0:T(8,128)(2,1)S(1)}, bf16[64,2048]{1,0:T(8,128)(2,1)S(1)}, u32[]{:S(2)}, u32[]{:S(2)}) %collective-permute-start.1) | collective-permute-done | bytes 262176 | tf_op jit(solution)/shard_map/ppermute | solution.py:416
  53.9 10.4 %all-to-all-done = bf16[8,64,768]{2,1,0:T(8,128)(2,1)S(1)} async-done(((bf16[8,64,768]{2,1,0:T(8,128)(2,1)}), bf16[8,64,768]{2,1,0:T(8,128)(2,1)S(1)}, u32[]{:S(2)}, u32[]{:S(2)}) %all-to-all-start) | async-done | bytes 786464 | tf_op jit(solution)/shard_map/all_to_all | solution.py:920
  125.4 12.2 %shard_map.263 = (bf16[1024,256]{1,0:T(8,128)(2,1)}, bf16[1024,256]{1,0:T(8,128)(2,1)}, bf16[1024,256]{1,0:T(8,128)(2,1)}, f32[1024,256]{1,0:T(8,128)}, f32[2,10...) custom-call(s32[1]{0:T(128)S(6)} %copy.171.length_ref, f32[1024,768]{1,0:T(8,128)} %copy-done.1, ...), custom_call_target="tpu_custom_call" | custom-call | flops 1610612736 | bytes 7864320 | tf_op jit(solution)/shard_map/pallas_call | solution.py:588
  160.0 9.6 %collective-permute-done.12 = bf16[2048,256]{1,0:T(8,128)(2,1)} collective-permute-done((bf16[2048,256]{1,0:T(8,128)(2,1)}, bf16[2048,256]{1,0:T(8,128)(2,1)}, u32[]{:S(2)}, u32[]{:S(2)}) %collective-permute-start.12) | collective-permute-done | bytes 1048608 | tf_op jit(solution)/shard_map/ppermute | solution.py:416
  169.6 20.9 %collective-permute-done.13 = bf16[2048,256]{1,0:T(8,128)(2,1)} collective-permute-done((bf16[2048,256]{1,0:T(8,128)(2,1)}, bf16[2048,256]{1,0:T(8,128)(2,1)}, u32[]{:S(2)}, u32[]{:S(2)}) %collective-permute-start.13) | collective-permute-done | bytes 1048608 | tf_op jit(solution)/shard_map/ppermute | solution.py:416
  213.0 11.3 %collective-permute-done.16 = bf16[2048,256]{1,0:T(8,128)(2,1)} collective-permute-done((bf16[2048,256]{1,0:T(8,128)(2,1)}, bf16[2048,256]{1,0:T(8,128)(2,1)}, u32[]{:S(2)}, u32[]{:S(2)}) %collective-permute-start.16) | collective-permute-done | bytes 1048608 | tf_op jit(solution)/shard_map/ppermute | solution.py:416
  227.9 18.2 %collective-permute-done.17 = bf16[256,2048]{1,0:T(8,128)(2,1)} collective-permute-done((bf16[256,2048]{1,0:T(8,128)(2,1)}, bf16[256,2048]{1,0:T(8,128)(2,1)}, u32[]{:S(2)}, u32[]{:S(2)}) %collective-permute-start.17) | collective-permute-done | bytes 1048608 | tf_op jit(solution)/shard_map/ppermute | solution.py:416
  251.5 8.4 %fusion.34 = f32[2,1024,512]{2,1,0:T(8,128)} fusion(bf16[2,2048,512]{2,1,0:T(8,128)(2,1)} %maximum_maximum_fusion.1, bf16[1024,2048]{1,0:T(8,128)(2,1)S(1)} %copy-done.24), kind=kOutput, calls=%fused_computation.63 | convolution fusion | flops 4294967296 | bytes 12582912 | tf_op jit(solution)/shard_map/td,edf->etf/dot_general | solution.py:1024
  271.3 10.1 %fusion.24 = (f32[2,1024]{1,0:T(2,128)S(1)}, bf16[2,1024,512]{2,1,0:T(8,128)(2,1)S(1)}, bf16[2,1024,512]{2,1,0:T(8,128)(2,1)S(1)}, bf16[2,1024,512]{2,1,0:T(8,128)(2,1)S(1)}) fusion(f32[2,1024,512]{2,1,0:T(8,128)} %fusion.34, f32[2,512,1024]{1,2,0:T(8,128)} %fusion.32, f32[2,1024]{1,0:T(2,128)S(1)} %bitcast.399, bf16[1024,2048]{1,0:T(8,128)(2,1)S(1)} %copy-done.5, ...), kind=kOutput, calls=%fused_computation.44 | convolution fusion | flops 4327471104 | bytes 23085056 | tf_op jit(solution)/shard_map/td,efd->etf/dot_general | solution.py:840
  288.3 8.3 %fusion.6 = bf16[1024,2048]{1,0:T(8,128)(2,1)} fusion(f32[1024,2048,1]{1,0,2:T(8,128)} %fusion.87, bf16[2,1024,512]{2,1,0:T(8,128)(2,1)S(1)} %get-tuple-element.263.refs_6_.refs_8_, bf16[2,2048,512]{2,1,0:T(8,128)(2,1)S(1)} %copy-done.35), kind=kOutput, calls=%fused_computation.12 | convolution fusion | flops 4299161600 | bytes 18874368 | tf_op jit(solution)/shard_map/etf,edf->td/dot_general | solution.py:854
  301.5 8.6 %fusion.14 = f32[2,512,1024]{1,2,0:T(8,128)} fusion(bf16[2,2048,512]{2,1,0:T(8,128)(2,1)} %maximum_maximum_fusion.1, bf16[1024,2048]{1,0:T(8,128)(2,1)S(1)} %copy-done.25), kind=kOutput, calls=%fused_computation.29 | convolution fusion | flops 4294967296 | bytes 12582912 | tf_op jit(solution)/shard_map/td,edf->etf/dot_general | solution.py:1024
  316.1 10.6 %fusion.27 = (f32[2,1024]{1,0:T(2,128)S(1)}, bf16[2,1024,512]{2,1,0:T(8,128)(2,1)S(1)}, bf16[2,1024,512]{2,1,0:T(8,128)(2,1)}, bf16[2,1024,512]{2,1,0:T(8,128)(2,1)S(1)}) fusion(f32[2,512,1024]{1,2,0:T(8,128)} %fusion.14, f32[2,512,1024]{1,2,0:T(8,128)} %fusion.16, f32[2,1024]{1,0:T(2,128)S(1)} %fusion.69, bf16[1024,2048]{1,0:T(8,128)(2,1)S(1)} %bitcast.357, ...), kind=kOutput, calls=%fused_computation.49 | convolution fusion | flops 4327471104 | bytes 23085056 | tf_op jit(solution)/shard_map/td,efd->etf/dot_general | solution.py:840
  333.7 8.3 %fusion.5 = bf16[1024,2048]{1,0:T(8,128)(2,1)} fusion(f32[1024,2048,1]{1,0,2:T(8,128)} %fusion.88, bf16[2,1024,512]{2,1,0:T(8,128)(2,1)S(1)} %get-tuple-element.390.refs_7_.refs_9_, bf16[2,2048,512]{2,1,0:T(8,128)(2,1)S(1)} %copy-done.36), kind=kOutput, calls=%fused_computation.10 | convolution fusion | flops 4299161600 | bytes 18874368 | tf_op jit(solution)/shard_map/etf,edf->td/dot_general | solution.py:854
  347.8 13.9 %shard_map.264 = (bf16[2048,128]{1,0:T(8,128)(2,1)}, bf16[2048,128]{1,0:T(8,128)(2,1)}, bf16[2048,128]{1,0:T(8,128)(2,1)}, bf16[2048,128]{1,0:T(8,128)(2,1)}, bf...) custom-call(bf16[1024,2048]{1,0:T(8,128)(2,1)} %all-gather.9.cloned., ...), custom_call_target="tpu_custom_call" | custom-call | flops 8589934592 | bytes 20971520 | tf_op jit(solution)/shard_map/pallas_call | solution.py:822
  374.8 11.1 %shard_map.265 = (bf16[128,2048]{1,0:T(8,128)(2,1)}, bf16[128,2048]{1,0:T(8,128)(2,1)}, bf16[128,2048]{1,0:T(8,128)(2,1)}, bf16[128,2048]{1,0:T(8,128)(2,1)}) custom-call(bf16[1024,2048]{1,0:T(8,128)(2,1)} %all-gather.7.cloned.1.call-done.refs_0_, bf16[1024,2048]{1,0:T(8,128)(2,1)} %bitcast.355, bf16[2,1024,512]{2,1,0:T(8,128)(2,1)} %copy-done.3, ...), custom_call_target="tpu_custom_call" | custom-call | flops 4294967296 | bytes 14680064 | tf_op jit(solution)/shard_map/pallas_call | solution.py:822
  432.2 11.1 %collective-permute-done.26.refs_13_ = bf16[2048,128]{1,0:T(8,128)(2,1)} collective-permute-done((bf16[2048,128]{1,0:T(8,128)(2,1)}, bf16[2048,128]{1,0:T(8,128)(2,1)}, u32[]{:S(2)}, u32[]{:S(2)}) %collective-permute-start.26) | collective-permute-done | bytes 524320 | tf_op jit(solution)/shard_map/ppermute | solution.py:416
  443.3 11.2 %collective-permute-done.27.refs_14_ = bf16[2048,128]{1,0:T(8,128)(2,1)} collective-permute-done((bf16[2048,128]{1,0:T(8,128)(2,1)}, bf16[2048,128]{1,0:T(8,128)(2,1)}, u32[]{:S(2)}, u32[]{:S(2)}) %collective-permute-start.27) | collective-permute-done | bytes 524320 | tf_op jit(solution)/shard_map/ppermute | solution.py:416
  454.5 11.2 %collective-permute-done.28.refs_15_ = bf16[2048,128]{1,0:T(8,128)(2,1)} collective-permute-done((bf16[2048,128]{1,0:T(8,128)(2,1)}, bf16[2048,128]{1,0:T(8,128)(2,1)}, u32[]{:S(2)}, u32[]{:S(2)}) %collective-permute-start.28) | collective-permute-done | bytes 524320 | tf_op jit(solution)/shard_map/ppermute | solution.py:416
  465.7 8.4 %collective-permute-done.29.refs_16_ = bf16[2048,128]{1,0:T(8,128)(2,1)} collective-permute-done((bf16[2048,128]{1,0:T(8,128)(2,1)}, bf16[2048,128]{1,0:T(8,128)(2,1)}, u32[]{:S(2)}, u32[]{:S(2)}) %collective-permute-start.29) | collective-permute-done | bytes 524320 | tf_op jit(solution)/shard_map/ppermute | solution.py:416
  479.7 15.6 %shard_map.266 = (bf16[1024,256]{1,0:T(8,128)(2,1)}, f32[1024,256]{1,0:T(8,128)}, f32[1024,256]{1,0:T(8,128)}, f32[1024,1]{1,0:T(8,128)}, f32[1024,1]{1,0:T(8,128)}, /*index=5*/f32[1,256]{1,0:T(1,128)}, f32[1,256]{1,0:T(1,128)}) custom-call(s32[1]{0:T(128)S(6)} %copy.171.length_ref, bf16[1024,2048]{1,0:T(8,128)(2,1)} %all-gather.13.cloned.1.call-done.upstream_ref, ...), custom_call_target="tpu_custom_call" | custom-call | flops 2684354560 | bytes 12058624 | tf_op jit(solution)/shard_map/pallas_call | solution.py:718
  519.6 9.7 %reduce-scatter.12.cloned.1.call-done = bf16[128,2048]{1,0:T(8,128)(2,1)} async-done(((bf16[1024,2048]{1,0:T(8,128)(2,1)}), bf16[128,2048]{1,0:T(8,128)(2,1)}) %reduce-scatter.12.cloned.1.call-update) | async-done | bytes 524304 | tf_op jit(solution)/shard_map/reduce_scatter | solution.py:1115
  583.0 15.8 %shard_map.267 = (f32[2,2048,256]{2,1,0:T(8,128)}, f32[2,2048,256]{2,1,0:T(8,128)}) custom-call(bf16[1024,2048]{1,0:T(8,128)(2,1)} %all-gather.9.cloned.1.call-done.refs_0_, bf16[1024,2048]{1,0:T(8,128)(2,1)} %all-gather.11.cloned.1.call-done.refs_1_, bf16[2,1024,512]{2,1,0:T(8,128)(2,1)} %copy-done.91, bf16[2,1024,512]{2,1,0:T(8,128)(2,1)} %copy-done.93, ...), custom_call_target="tpu_custom_call" | custom-call | flops 8589934592 | bytes 20971520 | tf_op jit(solution)/shard_map/pallas_call | solution.py:822
  618.5 9.3 %collective-permute-done.47.refs_9_ = bf16[128,2048]{1,0:T(8,128)(2,1)} collective-permute-done((bf16[128,2048]{1,0:T(8,128)(2,1)}, bf16[128,2048]{1,0:T(8,128)(2,1)}, u32[]{:S(2)}, u32[]{:S(2)}) %collective-permute-start.47) | collective-permute-done | bytes 524320 | tf_op jit(solution)/shard_map/ppermute | solution.py:416
  627.8 11.8 %shard_map.268 = f32[2,256,2048]{2,1,0:T(8,128)} custom-call(bf16[1024,2048]{1,0:T(8,128)(2,1)} %all-gather.7.cloned.1.call-done.refs_0_, bf16[1024,2048]{1,0:T(8,128)(2,1)} %bitcast.356, bf16[2,1024,512]{2,1,0:T(8,128)(2,1)} %copy-done.3, bf16[2,1024,512]{2,1,0:T(8,128)(2,1)} %get-tuple-element.272.refs_3_.refs_5_, bf16[2,1024,512]{2,1,0:T(8,128)(2,1)} %copy-done.3, ...), custom_call_target="tpu_custom_call" | custom-call | flops 4294967296 | bytes 14680064 | tf_op jit(solution)/shard_map/pallas_call | solution.py:822
  (502 shorter events, 351.3 us)
Async XLA Ops:
  7.3 86.0 %all-gather.15.cloned.1.call-start = ((), (), s32[]{:S(2)}) async-start(), calls=%async_computation.22 | async-start | bytes 4718592 | tf_op jit(solution)/shard_map/all_gather | solution.py:944
  15.5 48.8 %all-to-all-start = ((bf16[8,64,768]{2,1,0:T(8,128)(2,1)}), bf16[8,64,768]{2,1,0:T(8,128)(2,1)S(1)}, u32[]{:S(2)}, u32[]{:S(2)}) async-start(bf16[8,64,768]{2,1,0:T(8,128)(2,1)} %pad_maximum_fusion.6), calls=%async_computation | async-start | bytes 1572864 | tf_op jit(solution)/shard_map/all_to_all | solution.py:920
  22.0 32.0 %collective-permute-start = (bf16[2048,256]{1,0:T(8,128)(2,1)S(1)}, bf16[2048,256]{1,0:T(8,128)(2,1)}, u32[]{:S(2)}, u32[]{:S(2)}) collective-permute-start(bf16[2048,256]{1,0:T(8,128)(2,1)S(1)} %slice_bitcast_fusion.5), channel_id=1, source_target_pairs={{0,8},{8,0},{1,9},{9,1},{2,10},{10,2},{3,11},{11,3},{4,12},{12,4},... | collective-permute-start | bytes 3145736 | tf_op jit(solution)/shard_map/ppermute | solution.py:416
  23.5 29.7 %collective-permute-start.1 = (bf16[64,2048]{1,0:T(8,128)(2,1)S(1)}, bf16[64,2048]{1,0:T(8,128)(2,1)S(1)}, u32[]{:S(2)}, u32[]{:S(2)}) collective-permute-start(bf16[64,2048]{1,0:T(8,128)(2,1)S(1)} %convert_element_type.288), channel_id=1, source_target_pairs={{0,8},{8,0},{1,9},{9,1},{2,10},{10,2},{3,11},{11,3},{4,12},{12,4},... | collective-permute-start | bytes 786440 | tf_op jit(solution)/shard_map/ppermute | solution.py:416
  24.0 29.2 %collective-permute-start.2 = (bf16[64,2048]{1,0:T(8,128)(2,1)S(1)}, bf16[64,2048]{1,0:T(8,128)(2,1)S(1)}, u32[]{:S(2)}, u32[]{:S(2)}) collective-permute-start(bf16[64,2048]{1,0:T(8,128)(2,1)S(1)} %convert_element_type.288), channel_id=1, source_target_pairs={{0,16},{16,0},{1,17},{17,1},{2,18},{18,2},{3,19},{19,3},{4,20},{20... | collective-permute-start | bytes 786440 | tf_op jit(solution)/shard_map/ppermute | solution.py:420
  67.4 52.5 %collective-permute-start.9 = (s32[128,8]{0,1:T(8,128)S(1)}, s32[128,8]{0,1:T(8,128)S(1)}, u32[]{:S(2)}, u32[]{:S(2)}) collective-permute-start(s32[128,8]{0,1:T(8,128)S(1)} %bitcast.395), channel_id=1, source_target_pairs={{0,16},{16,0},{1,17},{17,1},{2,18},{18,2},{3,19},{19,3},{4,20},{20... | collective-permute-start | bytes 12296 | tf_op jit(solution)/shard_map/ppermute | solution.py:420
  71.7 65.9 %all-gather.7.cloned.1.call-start = ((), (), s32[]{:S(2)}) async-start(), calls=%async_computation.13 | async-start | bytes 4718592 | tf_op jit(solution)/shard_map/all_gather | solution.py:950
  112.8 77.7 %reduce-scatter.6.cloned.1.call-start = ((), (), s32[]{:S(2)}) async-start(), calls=%async_computation.14 | async-start | bytes 4718592 | tf_op jit(solution)/shard_map/reduce_scatter | solution.py:986
  141.1 49.4 %collective-permute-start.11 = (bf16[512,2048]{1,0:T(8,128)(2,1)}, bf16[512,2048]{1,0:T(8,128)(2,1)}, u32[]{:S(2)}, u32[]{:S(2)}) collective-permute-start(bf16[512,2048]{1,0:T(8,128)(2,1)} %constant_dynamic-slice_fusion.1), channel_id=1, source_target_pairs={{0,16},{16,0},{1,17},{17,1},{2,18},{18,2},{3,19},{19,3},{4,20},{20... | collective-permute-start | bytes 6291464 | tf_op jit(solution)/shard_map/ppermute | solution.py:420
  145.7 44.8 %collective-permute-start.13 = (bf16[2048,256]{1,0:T(8,128)(2,1)}, bf16[2048,256]{1,0:T(8,128)(2,1)}, u32[]{:S(2)}, u32[]{:S(2)}) collective-permute-start(bf16[2048,256]{1,0:T(8,128)(2,1)} %slice_bitcast_fusion.3), channel_id=1, source_target_pairs={{0,8},{8,0},{1,9},{9,1},{2,10},{10,2},{3,11},{11,3},{4,12},{12,4},... | collective-permute-start | bytes 3145736 | tf_op jit(solution)/shard_map/ppermute | solution.py:416
  151.5 94.6 %all-gather.9.cloned.1.call-start = ((), (), s32[]{:S(2)}) async-start(), calls=%async_computation.15 | async-start | bytes 4718592 | tf_op jit(solution)/shard_map/all_gather | solution.py:1007
  194.4 102.1 %all-gather.11.cloned.1.call-start = ((), (), s32[]{:S(2)}) async-start(), calls=%async_computation.16 | async-start | bytes 4718592 | tf_op jit(solution)/shard_map/all_gather | solution.py:1016
  194.8 33.0 %collective-permute-start.14 = (bf16[128,2048]{1,0:T(8,128)(2,1)}, bf16[128,2048]{1,0:T(8,128)(2,1)}, u32[]{:S(2)}, u32[]{:S(2)}) collective-permute-start(bf16[128,2048]{1,0:T(8,128)(2,1)} %multiply_convert_fusion.6), channel_id=1, source_target_pairs={{0,16},{16,0},{1,17},{17,1},{2,18},{18,2},{3,19},{19,3},{4,20},{20... | collective-permute-start | bytes 1572872 | tf_op jit(solution)/shard_map/ppermute | solution.py:420
  201.5 44.6 %collective-permute-start.17 = (bf16[256,2048]{1,0:T(8,128)(2,1)}, bf16[256,2048]{1,0:T(8,128)(2,1)}, u32[]{:S(2)}, u32[]{:S(2)}) collective-permute-start(bf16[256,2048]{1,0:T(8,128)(2,1)} %slice_bitcast_fusion.1), channel_id=1, source_target_pairs={{0,8},{8,0},{1,9},{9,1},{2,10},{10,2},{3,11},{11,3},{4,12},{12,4},... | collective-permute-start | bytes 3145736 | tf_op jit(solution)/shard_map/ppermute | solution.py:416
  246.1 101.6 %reduce-scatter.8.cloned.1.call-start = ((), (), s32[]{:S(2)}) async-start(), calls=%async_computation.17 | async-start | bytes 4718592 | tf_op jit(solution)/shard_map/reduce_scatter | solution.py:1044
  296.6 111.1 %reduce-scatter.10.cloned.1.call-start = ((), (), s32[]{:S(2)}) async-start(), calls=%async_computation.18 | async-start | bytes 4718592 | tf_op jit(solution)/shard_map/reduce_scatter | solution.py:1046
  374.7 99.4 %all-gather.13.cloned.1.call-start = ((), (), s32[]{:S(2)}) async-start(), calls=%async_computation.19 | async-start | bytes 4718592 | tf_op jit(solution)/shard_map/all_gather | solution.py:1104
  426.1 103.2 %reduce-scatter.12.cloned.1.call-start = ((), (), s32[]{:S(2)}) async-start(), calls=%async_computation.20 | async-start | bytes 4718592 | tf_op jit(solution)/shard_map/reduce_scatter | solution.py:1115
  426.6 47.6 %collective-permute-start.25 = (bf16[512,2048]{1,0:T(8,128)(2,1)S(1)}, bf16[512,2048]{1,0:T(8,128)(2,1)}, u32[]{:S(2)}, u32[]{:S(2)}) collective-permute-start(bf16[512,2048]{1,0:T(8,128)(2,1)S(1)} %add_convert_fusion.1), channel_id=1, source_target_pairs={{0,16},{16,0},{1,17},{17,1},{2,18},{18,2},{3,19},{19,3},{4,20},{20... | collective-permute-start | bytes 6291464 | tf_op jit(solution)/shard_map/ppermute | solution.py:420
  430.1 35.6 %collective-permute-start.28 = (bf16[2048,128]{1,0:T(8,128)(2,1)}, bf16[2048,128]{1,0:T(8,128)(2,1)}, u32[]{:S(2)}, u32[]{:S(2)}) collective-permute-start(bf16[2048,128]{1,0:T(8,128)(2,1)} %get-tuple-element.289), channel_id=1, source_target_pairs={{0,8},{8,0},{1,9},{9,1},{2,10},{10,2},{3,11},{11,3},{4,12},{12,4},... | collective-permute-start | bytes 1572872 | tf_op jit(solution)/shard_map/ppermute | solution.py:416
  430.7 43.5 %collective-permute-start.29 = (bf16[2048,128]{1,0:T(8,128)(2,1)}, bf16[2048,128]{1,0:T(8,128)(2,1)}, u32[]{:S(2)}, u32[]{:S(2)}) collective-permute-start(bf16[2048,128]{1,0:T(8,128)(2,1)} %get-tuple-element.290), channel_id=1, source_target_pairs={{0,8},{8,0},{1,9},{9,1},{2,10},{10,2},{3,11},{11,3},{4,12},{12,4},... | collective-permute-start | bytes 1572872 | tf_op jit(solution)/shard_map/ppermute | solution.py:416
  506.9 132.7 %reduce-scatter.14.cloned.1.call-start = ((), (), s32[]{:S(2)}) async-start(), calls=%async_computation.21 | async-start | bytes 4718592 | tf_op jit(solution)/shard_map/reduce_scatter | solution.py:1157
  517.8 28.0 %collective-permute-start.37 = (bf16[128,2048]{1,0:T(8,128)(2,1)}, bf16[128,2048]{1,0:T(8,128)(2,1)}, u32[]{:S(2)}, u32[]{:S(2)}) collective-permute-start(bf16[128,2048]{1,0:T(8,128)(2,1)} %get-tuple-element.320), channel_id=1, source_target_pairs={{0,8},{8,0},{1,9},{9,1},{2,10},{10,2},{3,11},{11,3},{4,12},{12,4},... | collective-permute-start | bytes 1572872 | tf_op jit(solution)/shard_map/ppermute | solution.py:416
  605.3 38.7 %all-to-all-start.7 = ((bf16[8,64,768]{2,1,0:T(8,128)(2,1)}), bf16[8,64,768]{2,1,0:T(8,128)(2,1)S(1)}, u32[]{:S(2)}, u32[]{:S(2)}) async-start(bf16[8,64,768]{2,1,0:T(8,128)(2,1)} %bitcast.373), calls=%async_computation.11 | async-start | bytes 1572864 | tf_op jit(solution)/shard_map/all_to_all | solution.py:1193
  (137 other events, 1952.4 us)
Sparse Core Ops, SparseCore 0:
  9.7 66.5 all-gather.14
  79.0 47.6 all-gather.6
  137.8 51.2 reduce-scatter.5
  194.6 47.4 all-gather.8
  246.2 48.0 all-gather.10
  296.7 50.9 reduce-scatter.7
  350.6 48.3 reduce-scatter.9
  426.2 47.2 all-gather.12
  478.8 50.3 reduce-scatter.11
  558.4 52.4 reduce-scatter.13

commit v3 on v2

--- a/solution.py
+++ b/solution.py
@@ -463,26 +463,26 @@
         pick(row, column),
         beside[:half],
         below[half:],
-        swap_x(beside[half:].astype(low)),
-        swap_y(below[:half].astype(low)),
+        beside[half:].astype(low),
+        below[:half].astype(low),
         swap_y(across[:half]),
         swap_x(across[half:]),
     )
 
 
-def scatter_ready(kept, beside, below, from_beside, from_below, far_below, far_beside):
+def scatter_ready(kept, beside, below, beside_rest, below_rest, far_below, far_beside):
     low, wide = jnp.bfloat16, jnp.float32
     beside = (beside + far_below.astype(wide)).astype(low)
     below = (below + far_beside.astype(wide)).astype(low)
-    return (kept, beside, below, from_beside, from_below)
-
-
-def scatter_last(kept, beside, below, from_beside, from_below):
+    return (kept, beside, below, beside_rest, below_rest)
+
+
+def scatter_last(kept, beside, below, beside_rest, below_rest):
     wide = jnp.float32
     added = jnp.concatenate(
         [
-            swap_x(beside).astype(wide) + from_below.astype(wide),
-            from_beside.astype(wide) + swap_y(below).astype(wide),
+            swap_x(beside).astype(wide) + swap_y(below_rest).astype(wide),
+            swap_x(beside_rest).astype(wide) + swap_y(below).astype(wide),
         ]
     )
     return kept + added
@@ -738,34 +738,30 @@
     )(length, upstream, out_w, attended, total, query, key, value, qkv, *rest)
 
 
-def put_halves(outs, received, place, expert, axis, value):
-    low, wide = jnp.bfloat16, jnp.float32
+def put_halves(outs, place, expert, axis, value):
+    if len(outs[0].shape) == 3:
+        outs[expert[0]][expert[1]] = value
+        return
     length = value.shape[axis] // 2
     for half in range(2):
         span = slice(half * length, (half + 1) * length)
         at = (span, slice(None)) if axis == 0 else (slice(None), span)
-        number = 2 * place + half
-        if received is None:
-            outs[number][...] = value[at].astype(low)
-        else:
-            outs[expert[0]][(expert[1],) + at] = value[at] + received[number][...].astype(wide)
-
-
-def tall_kernel(count, adding, *refs):
-    outs = refs[2 + (8 if adding else 4) * count :]
-    received = refs[2 + 4 * count : 2 + 8 * count] if adding else None
+        outs[2 * place + half][...] = value[at].astype(jnp.bfloat16)
+
+
+def tall_kernel(count, *refs):
+    outs = refs[2 + 4 * count :]
     first, second = refs[0][...].T, refs[1][...].T
     for kind in range(2):
         for expert in range(count):
             place = count * kind + expert
             one, two = refs[2 + 2 * place], refs[3 + 2 * place]
             value = mul_nn(first, one[...]) + mul_nn(second, two[...])
-            put_halves(outs, received, place, (kind, expert), 1, value)
-
-
-def flat_kernel(count, adding, *refs):
-    outs = refs[2 + (4 if adding else 2) * count : -1]
-    received = refs[2 + 2 * count : 2 + 4 * count] if adding else None
+            put_halves(outs, place, (kind, expert), 1, value)
+
+
+def flat_kernel(count, *refs):
+    outs = refs[2 + 2 * count : -1]
     turned_ref = refs[-1]
     length, block = refs[2].shape
 
@@ -782,10 +778,10 @@
         value = mul_nn(turned_ref[span, :length], refs[0][...]) + mul_nn(
             turned_ref[span, length:], refs[1][...]
         )
-        put_halves(outs, received, expert, (0, expert), 0, value)
-
-
-def weight_grads(rows, sources, which, tall, received=None):
+        put_halves(outs, expert, (0, expert), 0, value)
+
+
+def weight_grads(rows, sources, which, tall):
     length, model_width = rows[0].shape
     count, _, doubled = sources[0][0].shape
     block = doubled // 2
@@ -803,28 +799,26 @@
                 )
             ] * 2
     kinds = len(sources)
-    if tall:
-        piece, shape = pl.BlockSpec((tile, block // 2), lambda i: (i, 0)), (model_width, block // 2)
-        full = pl.BlockSpec((count, tile, block), lambda i: (0, i, 0))
-        full_shape = (count, model_width, block)
+    if which == 0:
+        number, dtype = kinds, jnp.float32
+        if tall:
+            spec, shape = pl.BlockSpec((count, tile, block), lambda i: (0, i, 0)), (model_width, block)
+        else:
+            spec, shape = pl.BlockSpec((count, block, tile), lambda i: (0, 0, i)), (block, model_width)
+        shape = (count,) + shape
     else:
-        piece, shape = pl.BlockSpec((block // 2, tile), lambda i: (0, i)), (block // 2, model_width)
-        full = pl.BlockSpec((count, block, tile), lambda i: (0, 0, i))
-        full_shape = (count, block, model_width)
-    pieces = 2 * count * kinds
-    if received is None:
-        out_specs, shapes, dtype = [piece] * pieces, [shape] * pieces, jnp.bfloat16
-    else:
-        operands += list(received)
-        in_specs += [piece] * pieces
-        out_specs, shapes, dtype = [full] * kinds, [full_shape] * kinds, jnp.float32
+        number, dtype = 2 * count * kinds, jnp.bfloat16
+        if tall:
+            spec, shape = pl.BlockSpec((tile, block // 2), lambda i: (i, 0)), (model_width, block // 2)
+        else:
+            spec, shape = pl.BlockSpec((block // 2, tile), lambda i: (0, i)), (block // 2, model_width)
     scratch = [] if tall else [pltpu.VMEM((count * block, 2 * length), jnp.bfloat16)]
     return pl.pallas_call(
-        functools.partial(tall_kernel if tall else flat_kernel, count, received is not None),
+        functools.partial(tall_kernel if tall else flat_kernel, count),
         grid=(model_width // tile,),
         in_specs=in_specs,
-        out_specs=out_specs,
-        out_shape=[jax.ShapeDtypeStruct(shape, dtype) for shape in shapes],
+        out_specs=[spec] * number,
+        out_shape=[jax.ShapeDtypeStruct(shape, dtype)] * number,
         scratch_shapes=scratch,
         compiler_params=pltpu.CompilerParams(vmem_limit_bytes=VMEM_BYTES),
         cost_estimate=pl.CostEstimate(
@@ -835,6 +829,36 @@
     )(*operands)
 
 
+def add_kernel(axis, own_ref, *refs):
+    out_ref = refs[-1]
+    for expert in range(out_ref.shape[0]):
+        pair = [ref[...].astype(jnp.float32) for ref in refs[2 * expert : 2 * expert + 2]]
+        out_ref[expert] = own_ref[expert] + jnp.concatenate(pair, axis=axis)
+
+
+def add_pieces(own, pieces, axis):
+    count, rows, columns = own.shape
+    tile = min(512, rows if axis else columns)
+    if axis:
+        full = pl.BlockSpec((count, tile, columns), lambda i: (0, i, 0))
+        piece = pl.BlockSpec((tile, columns // 2), lambda i: (i, 0))
+    else:
+        full = pl.BlockSpec((count, rows, tile), lambda i: (0, 0, i))
+        piece = pl.BlockSpec((rows // 2, tile), lambda i: (0, i))
+    return pl.pallas_call(
+        functools.partial(add_kernel, axis),
+        grid=((rows if axis else columns) // tile,),
+        in_specs=[full] + [piece] * len(pieces),
+        out_specs=full,
+        out_shape=jax.ShapeDtypeStruct(own.shape, own.dtype),
+        input_output_aliases={0: 0},
+        compiler_params=pltpu.CompilerParams(vmem_limit_bytes=VMEM_BYTES),
+        cost_estimate=pl.CostEstimate(
+            flops=own.size, bytes_accessed=10 * own.size, transcendentals=0
+        ),
+    )(own, *pieces)
+
+
 def expert_block(gate_pre, up_pre, grad_rows, gates, gate_w, up_w, down_w):
     wide = jnp.float32
     back = jnp.einsum("td,efd->etf", grad_rows, down_w, preferred_element_type=wide)
@@ -842,7 +866,7 @@
     silu = gate_pre * sigmoid
     activity = silu * up_pre
     gate_grads = jnp.sum(activity * back, axis=-1)
-    weight = gates.T[:, :, None]
+    weight = gates
     scaled = (activity * weight).astype(jnp.bfloat16)
     back = back * weight
     grad_gate_pre = (back * up_pre * sigmoid * (1.0 + gate_pre * (1.0 - sigmoid))).astype(
@@ -914,17 +938,47 @@
     ).astype(low)
     pack_rows = experts + 4
     packed = packed.reshape(-1, 128)
-    sent, packed, out_rows, gate_own = together(
-        sent, packed, w_output.astype(low), row_major(w_gate.astype(low))
-    )
+    numbers = range(local_count)
+
+    def experts_low(weight):
+        pieces = [weight[0]]
+        for i in numbers[1:]:
+            pieces += jnp.split(weight[i], 2)
+        return [row_major(piece.astype(low)) for piece in pieces]
+
+    def joined(pieces):
+        return [pieces[0]] + [
+            jnp.concatenate(pieces[i : i + 2]) for i in range(1, len(pieces), 2)
+        ]
+
+    many = 2 * local_count - 1
+
+    cosine, sine_part = rope_tables(jnp.arange(seq_len))
+    cosine = jnp.concatenate([cosine[:, 0], cosine[:, 0]], axis=1)
+    sine_part = jnp.concatenate([-sine_part[:, 0], sine_part[:, 0]], axis=1)
+    sent, packed, out_rows, *gate_own = together(
+        sent, packed, w_output.astype(low), *experts_low(w_gate)
+    )
+    up_own, down_own = experts_low(w_up), experts_low(w_down)
+    out_rows, up_own[0], *gate_own = together(out_rows, up_own[0], *gate_own)
     arrived = lax.all_to_all(sent, "expert", split_axis=0, concat_axis=0)
-    gate_far = [swap_x(gate_own[0])]
-    up_own, down_own = row_major(w_up.astype(low)), row_major(w_down.astype(low))
+    gate_far = [swap_x(piece) for piece in gate_own[:-1]]
     held = together(
-        arrived, packed, gate_far[0], gate_own, up_own, down_own, cot, *gather_first(out_rows)
-    )
-    arrived, packed, gate_far[0], gate_own, up_own, down_own, cot = held[:7]
-    out_parts = held[7:]
+        arrived,
+        packed,
+        cot,
+        cosine,
+        sine_part,
+        *gather_first(out_rows),
+        *gate_far,
+        gate_own[-1],
+        *up_own,
+        *down_own,
+    )
+    arrived, packed, cot, cosine, sine_part = held[:5]
+    out_parts, held = held[5:8], held[8:]
+    gate_far, gate_last, held = list(held[: many - 1]), held[many - 1], held[many:]
+    up_own, down_own = held[:many], held[many:]
     packed = lax.all_to_all(
         jnp.broadcast_to(packed[None], (devices,) + packed.shape),
         everyone,
@@ -954,20 +1008,16 @@
     qkv = jnp.dot(attn_low, qkv_w, preferred_element_type=wide)
     qkv, *out_parts = together(qkv, *out_parts)
     out_quad = gather_last(*out_parts)
-    out_own = lax.dynamic_index_in_dim(out_quad, core, 0, keepdims=False)
+    out_first = lax.dynamic_index_in_dim(out_quad, core, 0, keepdims=False)
     out_other = swap_core(lax.dynamic_index_in_dim(out_quad, 1 - core, 0, keepdims=False))
-    out_w = jnp.moveaxis(in_order(out_own, out_other, core), 0, 1).reshape(own_width, model_width)
+    out_w = jnp.moveaxis(in_order(out_first, out_other, core), 0, 1)
+    out_w = out_w.reshape(own_width, model_width)
     query_pre, key_pre = qkv[:, :own_width], qkv[:, own_width : 2 * own_width]
     squares = jnp.stack([jnp.sum(query_pre * query_pre, axis=1), jnp.sum(key_pre * key_pre, axis=1)])
     squares = sum_experts(squares)
     factors = lax.rsqrt(squares / model_width + EPSILON)
-    near_routes = swap_y(routes[0])
-    factors, near_routes = together(factors, near_routes)
     query_factor, key_factor = factors[0][:, None], factors[1][:, None]
     query_gain_own, key_gain_own = own_heads(query_gain), own_heads(key_gain)
-    cosine, sine_part = rope_tables(jnp.arange(seq_len))
-    cosine = jnp.concatenate([cosine[:, 0], cosine[:, 0]], axis=1)
-    sine_part = jnp.concatenate([-sine_part[:, 0], sine_part[:, 0]], axis=1)
     norm_args = (
         query_factor,
         key_factor,
@@ -980,24 +1030,19 @@
         lengths, qkv, *norm_args, out_w
     )
     attended_low = attended.astype(low)
-    attn_part, cot_all, gate_own, up_own, down_own = together(
-        attn_part, cot_all, gate_own, up_own, down_own
-    )
+    held = together(attn_part, cot_all, gate_last, *up_own, *down_own)
+    attn_part, cot_all, gate_last, held = held[0], held[1], held[2], held[3:]
+    up_own, down_own = held[:many], held[many:]
     attn_out = lax.psum_scatter(attn_part, "expert", scatter_dimension=0, tiled=True)
-    gate_far += [swap_x(gate_own[i]) for i in range(1, local_count)]
-    up_far = [swap_x(up_own[0])]
-    route_pair = jnp.stack([routes[0], near_routes]).reshape(-1, 128)
-    route_pair = lax.all_to_all(
-        jnp.broadcast_to(route_pair[None], (groups,) + route_pair.shape),
-        "expert",
-        split_axis=0,
-        concat_axis=0,
-    ).reshape(groups, 2, tok_rows, TOP)
-    held = together(attn_out, cot_half, route_pair, up_far[0], up_own, down_own, *gate_far)
-    attn_out, cot_half, route_pair, up_far[0], up_own, down_own = held[:6]
-    gate_far = held[6:]
-    up_far += [swap_x(up_own[i]) for i in range(1, local_count)]
-    down_far = [swap_x(down_own[0])]
+    gate_far.append(swap_x(gate_last))
+    up_far = [swap_x(piece) for piece in up_own[:-1]]
+    held = together(attn_out, cot_half, *gate_far, *up_far, up_own[-1], *down_own)
+    attn_out, cot_half, held = held[0], held[1], held[2:]
+    gate_far, held = list(held[:many]), held[many:]
+    up_far, down_own = list(held[: many - 1]), held[many:]
+    up_own = [*up_own[:-1], held[many - 1]]
+    up_far.append(swap_x(up_own[-1]))
+    down_far = [swap_x(piece) for piece in down_own[:-1]]
     cot_near = in_order(cot_half, swap_core(cot_half), core).reshape(seq_len, model_width)
     hidden = tok.astype(wide) + attn_out.astype(wide)
     mlp_in, mlp_normal, mlp_factor = rms_parts(hidden, mlp_gain)
@@ -1006,43 +1051,55 @@
 
     rows_own = lax.all_gather(mlp_low, "expert", axis=0, tiled=True)
     mlp_near = swap_y(mlp_low)
-    gate_w = jnp.concatenate([gate_own, jnp.stack(gate_far)], axis=2)
+
+    def doubled(own, far, axis):
+        return jnp.stack(
+            [jnp.concatenate(pair, axis=axis) for pair in zip(joined(own), joined(far))]
+        )
+
+    gates_sent = jnp.stack([gates_own, swap_y(gates_own)])
+    gates_sent = gates_sent.reshape(2, tok_rows, groups, local_count).transpose(2, 0, 3, 1)
+    gates_sent = lax.all_to_all(gates_sent, "expert", split_axis=0, concat_axis=0)
+    gate_w = doubled(gate_own, gate_far, 1)
     cot_near, *up_far = together(cot_near, *up_far)
-    up_w = jnp.concatenate([up_own, jnp.stack(up_far)], axis=2)
-    held = together(rows_own, mlp_near, cot_near, gate_w, up_w, down_far[0], down_own)
-    rows_own, mlp_near, cot_near, gate_w, up_w, down_far[0], down_own = held
-    down_far += [swap_x(down_own[i]) for i in range(1, local_count)]
-    block_width = w_gate.shape[2]
+    up_w = doubled(up_own, up_far, 1)
+    held = together(
+        rows_own, mlp_near, cot_near, gate_w, up_w, gates_sent, *down_far, down_own[-1]
+    )
+    rows_own, mlp_near, cot_near, gate_w, up_w, gates_sent = held[:6]
+    down_far, down_own = list(held[6:-1]), [*down_own[:-1], held[-1]]
+    gates_all = gates_sent.transpose(1, 2, 0, 3).reshape(2, local_count, seq_len, 1)
+    down_far.append(swap_x(down_own[-1]))
     rows_near = lax.all_gather(mlp_near, "expert", axis=0, tiled=True)
-
-    def gates_of(rows_in, number):
-        ids = route_pair[:, number].reshape(seq_len, TOP)
-        gates = dense_gates(times_transpose(rows_in, router_t), ids)
-        return lax.dynamic_slice_in_dim(gates, group * local_count, local_count, 1)
 
     def into(rows_in, weight):
         return jnp.einsum("td,edf->etf", rows_in, weight, preferred_element_type=wide)
 
-    own_gates, own_up_pre = gates_of(rows_own, 0), into(rows_own, up_w)
-    held = together(own_gates, own_up_pre, *down_far)
-    own_gates, own_up_pre, down_far = held[0], held[1], held[2:]
-    down_w = jnp.concatenate([down_own, jnp.stack(down_far)], axis=1)
+    own_up_pre = into(rows_own, up_w)
+    own_up_pre, *down_far = together(own_up_pre, *down_far)
+    down_w = doubled(down_own, down_far, 0)
     part_own = expert_block(
-        into(rows_own, gate_w), own_up_pre, cot_all, own_gates, gate_w, up_w, down_w
+        into(rows_own, gate_w), own_up_pre, cot_all, gates_all[0], gate_w, up_w, down_w
     )
     rows_near, *part_own = together(rows_near, *part_own)
     part_near = expert_block(
         into(rows_near, gate_w),
         into(rows_near, up_w),
         cot_near,
-        gates_of(rows_near, 1),
+        gates_all[1],
         gate_w,
         up_w,
         down_w,
     )
 
     grad_in_own = lax.psum_scatter(part_own[0], "expert", scatter_dimension=0, tiled=True)
-    near_in, grad_in_own = together(part_near[0], grad_in_own)
+
+    def mix(scaled):
+        return jnp.einsum("etf,efd->td", scaled, down_w, preferred_element_type=wide).astype(low)
+
+    near_in, grad_in_own, own_mixed, near_mixed = together(
+        part_near[0], grad_in_own, mix(part_own[2]), mix(part_near[2])
+    )
     grad_in_near = lax.psum_scatter(near_in, "expert", scatter_dimension=0, tiled=True)
 
     tall_sources = [(part_own[i], part_near[i]) for i in (3, 4)]
@@ -1050,7 +1107,7 @@
     rows_pair, cot_pair = (rows_own, rows_near), (cot_all, cot_near)
     far = list(weight_grads(rows_pair, tall_sources, 1, True))
     chunks = []
-    for size in (1, 1, 1, 4, 1):
+    for size in (2, 1, 1, 4):
         chunks.append(far[: size * local_count // 2])
         far = far[size * local_count // 2 :]
 
@@ -1065,31 +1122,26 @@
             place += len(chunks[i])
         return held[: len(values)]
 
-    cot_pair = (cot_all, tied((cot_near,), 0)[0])
+    held = tied((cot_near, near_mixed, part_own[1], part_near[1]), 0, 1, 2, 3)
+    cot_pair, near_mixed, part_gates = (cot_all, held[0]), held[1], held[2:]
     send(0)
     far = list(weight_grads(cot_pair, flat_sources, 1, False))
-    for size in (2, 2):
+    for size in (1, 3):
         chunks.append(far[: size * local_count // 2])
         far = far[size * local_count // 2 :]
-    (near_scaled,) = tied((part_near[2],), 0, 1, 5, 6)
-
-    def mix(scaled):
-        return jnp.einsum("etf,efd->td", scaled, down_w, preferred_element_type=wide).astype(low)
-
-    gate_grads = jnp.stack([part_own[1], part_near[1]])
+    gate_grads = jnp.stack(part_gates)
     gate_grads = gate_grads.reshape(2, local_count, groups, tok_rows).transpose(2, 0, 1, 3)
     gate_grads = lax.all_to_all(gate_grads, "expert", split_axis=0, concat_axis=0)
-    own_mixed, near_mixed = mix(part_own[2]), mix(near_scaled)
-    send(1)
-    own_mixed, near_mixed, gate_grads = tied((own_mixed, near_mixed, gate_grads), 1)
     half_rows = seq_len // 2
     mixed_kept = lax.dynamic_slice_in_dim(near_mixed, core * half_rows, half_rows, 0)
     mixed_sent = lax.dynamic_slice_in_dim(near_mixed, (1 - core) * half_rows, half_rows, 0)
     mixed_half = (mixed_kept.astype(wide) + swap_core(mixed_sent).astype(wide)).astype(low)
+    mixed_half, gate_grads = tied((mixed_half, gate_grads), 0, 1, 4, 5)
+    send(1)
 
     gate_grads = gate_grads.transpose(1, 3, 0, 2).reshape(2, tok_rows, experts)
     gate_grads = gate_grads[0] + swap_y(gate_grads[1])
-    grad_in_near, gate_grads = tied((grad_in_near, gate_grads), 2)
+    grad_in_near, gate_grads = tied((grad_in_near, gate_grads), 1, 2)
     send(2)
     grad_mlp_in = grad_in_own.astype(wide) + swap_y(grad_in_near).astype(wide)
     grad_logits = gates_own * (gate_grads - jnp.sum(gates_own * gate_grads, axis=-1, keepdims=True))
@@ -1105,7 +1157,10 @@
     mixed_half = swap_y(mixed_half)
     send(3)
 
-    grad_attn_all, mixed_half = tied((grad_attn_all, mixed_half), 3, 4)
+    grad_gate, grad_up = weight_grads(rows_pair, tall_sources, 0, True)
+    (grad_down,) = weight_grads(cot_pair, flat_sources, 0, False)
+    held = tied((grad_attn_all, mixed_half, grad_gate, grad_up, grad_down), 3, 4)
+    grad_attn_all, mixed_half, grad_gate, grad_up, grad_down = held
     send(4)
     mixed = own_mixed.astype(wide)
     half_own = lax.dynamic_slice_in_dim(mixed, core * half_rows, half_rows, 0)
@@ -1141,19 +1196,19 @@
     query_normal, key_normal = query_pre * query_factor, key_pre * key_factor
     inner = jnp.stack([query_inner[:, 0], key_inner[:, 0]])
     inner = sum_experts(inner)
-    inner, grad_w_out = tied((inner, grad_w_out), 5)
-    send(5)
+    inner, grad_w_out = together(inner, grad_w_out)
     out_parts = scatter_first(grad_w_out)
     inner = inner / model_width
     grad_query_low = (query_factor * (query_scaled - query_normal * inner[0][:, None])).astype(low)
     grad_key_low = (key_factor * (key_scaled - key_normal * inner[1][:, None])).astype(low)
     grad_qkv = jnp.concatenate([grad_query_low, grad_key_low, grad_value_low], axis=1)
-    grad_qkv, mixed = together(grad_qkv, mixed)
     qkv_w_grad = by_parts(grad_qkv)
     grad_qkv, qkv_w_grad = together(grad_qkv, qkv_w_grad)
     qkv_parts = scatter_first(qkv_w_grad)
     grad_in_part = times_transpose(grad_qkv, qkv_w)
-    grad_in_low, *qkv_parts = tied((grad_in_part.astype(low), *qkv_parts), 5)
+    count = len(qkv_parts)
+    held = together(grad_in_part.astype(low), mixed, *qkv_parts, *out_parts)
+    grad_in_low, mixed, qkv_parts, out_parts = held[0], held[1], held[2 : 2 + count], held[2 + count :]
     grad_attn_in = lax.psum_scatter(grad_in_low, "expert", scatter_dimension=0, tiled=True)
     grad_attn_in = grad_attn_in.astype(wide)
     grad_gain_attn = jnp.sum(grad_in_part * attn_normal, axis=0)
@@ -1172,35 +1227,29 @@
         axis=0,
     )
     small = small.reshape(pack_rows, devices, shard).transpose(1, 0, 2).reshape(devices, -1, 128)
-    held = tied((*scatter_ready(*qkv_parts), *scatter_ready(*out_parts), small, *rows_pair), 4)
-    qkv_parts, out_parts, small, rows_pair = held[:5], held[5:10], held[10], held[11:]
+    held = tied((*scatter_ready(*qkv_parts), *scatter_ready(*out_parts), small), 5)
+    send(5)
+    qkv_parts, out_parts, small = held[:5], held[5:10], held[10]
     small = lax.all_to_all(small, everyone, split_axis=0, concat_axis=0)
     small = jnp.sum(small, axis=0).reshape(pack_rows, shard)
-    grad_gate, grad_up = weight_grads(
-        rows_pair,
-        tall_sources,
-        0,
-        True,
-        received=[piece for chunk in chunks[:5] for piece in chunk],
-    )
     grad_w_qkv = scatter_last(*qkv_parts).astype(low)
     grad_w_out = scatter_last(*out_parts)
-    small, grad_w_qkv, grad_w_out, grad_gate, grad_up = tied(
-        (small, grad_w_qkv, grad_w_out, grad_gate, grad_up), 6
-    )
-    send(6)
+    small, grad_w_qkv, grad_w_out, grad_gate, grad_up = together(
+        small, grad_w_qkv, grad_w_out, grad_gate, grad_up
+    )
+    pieces = [piece for chunk in chunks for piece in chunk]
+    part = 2 * local_count
+    grad_gate = add_pieces(grad_gate, pieces[:part], 1)
+    grad_up = add_pieces(grad_up, pieces[part : 2 * part], 1)
     grad_w_qkv = grad_w_qkv.reshape(groups, shard, 3 * own_width)
     grad_w_qkv = lax.all_to_all(grad_w_qkv, "expert", split_axis=0, concat_axis=0)
-    (grad_down,) = weight_grads(
-        cot_pair,
-        flat_sources,
-        0,
-        False,
-        received=[piece for chunk in chunks[5:] for piece in chunk],
-    )
-    grad_w_qkv, grad_down, grad_tokens = together(grad_w_qkv, grad_down, grad_tokens)
+    grad_w_qkv, grad_gate, grad_up, grad_tokens = together(
+        grad_w_qkv, grad_gate, grad_up, grad_tokens
+    )
     grad_w_qkv = grad_w_qkv.reshape(chips, 2, shard, 3, 2, HEAD_DIM).astype(wide)
     grad_w_qkv = grad_w_qkv.transpose(3, 2, 1, 4, 0, 5).reshape(3, shard, model_width)
+    grad_down, grad_w_qkv, grad_tokens = together(grad_down, grad_w_qkv, grad_tokens)
+    grad_down = add_pieces(grad_down, pieces[2 * part :], 0)
 
     output = (hidden + mixed.astype(wide)).astype(low)
     return (

time: 662 us -> 633 us (0.956)
  waiting for transfers between devices: 229 us -> 186 us
  Pallas kernels: 80.5 us -> 95.5 us
  matrix products: 120 us -> 109 us
  other arithmetic: 71.3 us -> 78.6 us
    ppermute x28 -> x31, waiting for transfers between devices: 171 us -> 145 us  [swap_x(): return lax.ppermute(block, 'dx', FLIP)]
    another operation x1 -> x11, other arithmetic: 0.01 us -> 18.1 us  [the longest x8 13 us: doubled(): jnp.stack([jnp.concatenate(pair, axis=axis) for pair in zip(joined(own),...]
    pallas_call x0 -> x3, Pallas kernels: none -> 15.6 us  [add_pieces(): pl.pallas_call(functools.partial(add_kernel, axis), grid=((rows if axis e...]
    reduce_scatter x1, waiting for transfers between devices: 9.69 us -> 0.01 us  [per_device_by_heads(): mixed = lax.psum_scatter(mixed, 'expert', scatter_dimension=0, tiled=True)]
    squeeze x8 -> x0, local copies, waits for them, and re-layouts: 8.84 us -> none  [the longest x1 2.29 us: per_device_by_heads(): down_far = [swap_x(down_own[0])]]
    ppermute x28 -> x31, starting transfers between devices: 28.8 us -> 36.6 us  [swap_x(): return lax.ppermute(block, 'dx', FLIP)]
    convert_element_type x3 -> x0, other arithmetic: 7.77 us -> none  [the longest x1 3.75 us: per_device_by_heads(): w_up.astype(low)]
    concatenate x2 -> x0, other arithmetic: 6.92 us -> none  [the longest x1 3.55 us: per_device_by_heads(): up_w = jnp.concatenate([up_own, jnp.stack(up_far)], axis=2)]
  transfers between devices with their start and end apart: 66 -> 69, of which waited for: 30 -> 26; matrix products, arithmetic and copies ran while one was open for 35% -> 35% of each run, Pallas kernels for 12% -> 14%
where the time goes in v3:
time: 633 us; the launch traced here: 625 us
  waiting for transfers between devices  186 us (29%)
  matrix products  109 us (17%)
  Pallas kernels  95.5 us (15%)
  starting transfers between devices  90.7 us (14%)
  other arithmetic  78.6 us (12%)
  local copies, waits for them, and re-layouts  48.8 us (8%)
  between operations  16.8 us (3%)
    ppermute x31, waiting for transfers between devices, swap_x(): return lax.ppermute(block, 'dx', FLIP)  145 us
    pallas_call x4, Pallas kernels, weight_grads(): pl.pallas_call(functools.partial(tall_kernel if tall else flat_kernel, co...  52.1 us
    ppermute x31, starting transfers between devices, swap_x(): return lax.ppermute(block, 'dx', FLIP)  36.6 us
    dot_general x4, matrix products, into(): jnp.einsum('td,edf->etf', rows_in, weight, preferred_element_type=wide)  26.4 us
    ppermute x16, starting transfers between devices, swap_y(): return lax.ppermute(block, 'dy', FLIP)  21.8 us
    dot_general x2, matrix products, expert_block(): jnp.einsum('td,efd->etf', grad_rows, down_w, preferred_element_type=wide)  19 us
    dot_general x2, matrix products, expert_block(): jnp.einsum('etf,edf->td', grad_up_pre, up_w, preferred_element_type=wide)  16.8 us
    ppermute x16, waiting for transfers between devices, swap_y(): return lax.ppermute(block, 'dy', FLIP)  16.5 us
  transfers between devices with their start and end apart: 69, of which 26 were waited for; matrix products, arithmetic and copies ran while one was open for 35% of the time, Pallas kernels for 14%

profile of v3, /device:TPU:0, one launch (start us, length us, event | category | flops | bytes accessed | tf_op | source)
XLA Modules:
  0.0 625.4 jit_solution(16148479947237191226)
XLA Ops:
  45.2 22.1 %collective-permute-done.2 = bf16[2048,256]{1,0:T(8,128)(2,1)} collective-permute-done((bf16[2048,256]{1,0:T(8,128)(2,1)S(1)}, bf16[2048,256]{1,0:T(8,128)(2,1)}, u32[]{:S(2)}, u32[]{:S(2)}) %collective-permute-start.2) | collective-permute-done | bytes 1048608 | tf_op jit(solution)/shard_map/ppermute | solution.py:416
  83.0 13.2 %collective-permute-done.6 = bf16[32,2048]{1,0:T(8,128)(2,1)S(1)} collective-permute-done((bf16[32,2048]{1,0:T(8,128)(2,1)S(1)}, bf16[32,2048]{1,0:T(8,128)(2,1)S(1)}, u32[]{:S(2)}, u32[]{:S(2)}) %collective-permute-start.6) | collective-permute-done | bytes 131104 | tf_op jit(solution)/shard_map/ppermute | solution.py:416
  131.3 12.2 %shard_map.263 = (bf16[1024,256]{1,0:T(8,128)(2,1)}, bf16[1024,256]{1,0:T(8,128)(2,1)}, bf16[1024,256]{1,0:T(8,128)(2,1)}, f32[1024,256]{1,0:T(8,128)}, f32[2,10...) custom-call(s32[1]{0:T(128)S(6)} %copy.169.length_ref, f32[1024,768]{1,0:T(8,128)} %copy-done.1, ...), custom_call_target="tpu_custom_call" | custom-call | flops 1610612736 | bytes 7864320 | tf_op jit(solution)/shard_map/pallas_call | solution.py:588
  151.8 34.1 %collective-permute-done.12 = bf16[1024,256]{1,0:T(8,128)(2,1)} collective-permute-done((bf16[1024,256]{1,0:T(8,128)(2,1)S(1)}, bf16[1024,256]{1,0:T(8,128)(2,1)}, u32[]{:S(2)}, u32[]{:S(2)}) %collective-permute-start.12) | collective-permute-done | bytes 524320 | tf_op jit(solution)/shard_map/ppermute | solution.py:416
  185.9 9.6 %collective-permute-done.14 = bf16[1024,256]{1,0:T(8,128)(2,1)} collective-permute-done((bf16[1024,256]{1,0:T(8,128)(2,1)}, bf16[1024,256]{1,0:T(8,128)(2,1)}, u32[]{:S(2)}, u32[]{:S(2)}) %collective-permute-start.14) | collective-permute-done | bytes 524320 | tf_op jit(solution)/shard_map/ppermute | solution.py:416
  230.9 20.1 %collective-permute-done.19 = bf16[256,2048]{1,0:T(8,128)(2,1)S(1)} collective-permute-done((bf16[256,2048]{1,0:T(8,128)(2,1)S(1)}, bf16[256,2048]{1,0:T(8,128)(2,1)S(1)}, u32[]{:S(2)}, u32[]{:S(2)}) %collective-permute-start.19) | collective-permute-done | bytes 1048608 | tf_op jit(solution)/shard_map/ppermute | solution.py:416
  253.2 8.4 %fusion.34 = f32[2,1024,512]{2,1,0:T(8,128)S(1)} fusion(bf16[2,2048,512]{2,1,0:T(8,128)(2,1)} %pad_maximum_fusion.2, bf16[1024,2048]{1,0:T(8,128)(2,1)} %all-gather.9.cloned.1.call-done.refs_0_), kind=kOutput, calls=%fused_computation.63 | convolution fusion | flops 4294967296 | bytes 12582912 | tf_op jit(solution)/shard_map/td,edf->etf/dot_general | solution.py:1076
  271.0 8.8 %fusion.24 = (f32[2,1024]{1,0:T(2,128)S(1)}, bf16[2,1024,512]{2,1,0:T(8,128)(2,1)S(1)}, bf16[2,1024,512]{2,1,0:T(8,128)(2,1)S(1)}, bf16[2,1024,512]{2,1,0:T(8,128)(2,1)S(1)}) fusion(f32[2,1024,512]{2,1,0:T(8,128)S(1)} %fusion.34, f32[2,512,1024]{1,2,0:T(8,128)} %fusion.32, f32[2,1024]{1,0:T(2,128)S(1)} %get-tuple-element.515, ...), kind=kOutput, calls=%fused_computation.44 | convolution fusion | flops 4316985344 | bytes 23085056 | tf_op jit(solution)/shard_map/td,efd->etf/dot_general | solution.py:864
  279.8 6.8 %fusion.76 = f32[1024,2048,1]{1,0,2:T(8,128)} fusion(bf16[2,1024,512]{2,1,0:T(8,128)(2,1)S(1)} %get-tuple-element.326.refs_2_.refs_4_, bf16[2,2048,512]{2,1,0:T(8,128)(2,1)S(1)} %copy-done.24), kind=kOutput, calls=%fused_computation.249 | convolution fusion | flops 4294967296 | bytes 14680064 | tf_op jit(solution)/shard_map/etf,edf->td/dot_general | solution.py:877
  286.6 8.3 %fusion.6 = bf16[1024,2048]{1,0:T(8,128)(2,1)} fusion(f32[1024,2048,1]{1,0,2:T(8,128)} %fusion.76, bf16[2,1024,512]{2,1,0:T(8,128)(2,1)S(1)} %get-tuple-element.327.refs_6_.refs_8_, bf16[2,2048,512]{2,1,0:T(8,128)(2,1)S(1)} %copy-done.26), kind=kOutput, calls=%fused_computation.12 | convolution fusion | flops 4299161600 | bytes 18874368 | tf_op jit(solution)/shard_map/etf,edf->td/dot_general | solution.py:878
  298.9 8.4 %bitcast_convert_fusion.1 = bf16[1024,2048]{1,0:T(8,128)(2,1)} fusion(bf16[2,1024,512]{2,1,0:T(8,128)(2,1)S(1)} %get-tuple-element.321.refs_2_.refs_4_, bf16[1,512,2048]{2,1,0:T(8,128)(2,1)} %copy-done.38, bf16[1,512,2048]{2,1,0:T(8,128)(2,1)} %copy-done.36), kind=kOutput, calls=%fused_computation.8 | convolution fusion | flops 4299161600 | bytes 10485760 | tf_op jit(solution)/shard_map/etf,efd->td/dot_general | solution.py:1098
  319.4 10.2 %fusion.27 = (f32[2,1024]{1,0:T(2,128)S(1)}, bf16[2,1024,512]{2,1,0:T(8,128)(2,1)S(1)}, bf16[2,1024,512]{2,1,0:T(8,128)(2,1)S(1)}, bf16[2,1024,512]{2,1,0:T(8,128)(2,1)}) fusion(f32[2,512,1024]{1,2,0:T(8,128)} %fusion.14, f32[2,512,1024]{1,2,0:T(8,128)} %fusion.16, f32[2,1024]{1,0:T(2,128)S(1)} %get-tuple-element.514, bf16[1024,2048]{1,0:T(8,128)(2,1)S(1)} %bitcast.371, ...), kind=kOutput, calls=%fused_computation.49 | convolution fusion | flops 4316985344 | bytes 23085056 | tf_op jit(solution)/shard_map/td,efd->etf/dot_general | solution.py:864
  335.7 6.9 %fusion.77 = f32[1024,2048,1]{1,0,2:T(8,128)} fusion(bf16[2,1024,512]{2,1,0:T(8,128)(2,1)S(1)} %get-tuple-element.460.refs_3_.refs_5_, bf16[2,2048,512]{2,1,0:T(8,128)(2,1)S(1)} %copy-done.25), kind=kOutput, calls=%fused_computation.250 | convolution fusion | flops 4294967296 | bytes 14680064 | tf_op jit(solution)/shard_map/etf,edf->td/dot_general | solution.py:877
  342.5 8.5 %fusion.5 = bf16[1024,2048]{1,0:T(8,128)(2,1)} fusion(f32[1024,2048,1]{1,0,2:T(8,128)} %fusion.77, bf16[2,1024,512]{2,1,0:T(8,128)(2,1)S(1)} %copy-done.96, bf16[2,2048,512]{2,1,0:T(8,128)(2,1)S(1)} %copy-done.27), kind=kOutput, calls=%fused_computation.10 | convolution fusion | flops 4299161600 | bytes 18874368 | tf_op jit(solution)/shard_map/etf,edf->td/dot_general | solution.py:878
  351.1 14.1 %shard_map.264 = (bf16[2048,128]{1,0:T(8,128)(2,1)}, bf16[2048,128]{1,0:T(8,128)(2,1)}, bf16[2048,128]{1,0:T(8,128)(2,1)}, bf16[2048,128]{1,0:T(8,128)(2,1)}, bf...) custom-call(bf16[1024,2048]{1,0:T(8,128)(2,1)} %all-gather.9.cloned., ...), custom_call_target="tpu_custom_call" | custom-call | flops 8589934592 | bytes 20971520 | tf_op jit(solution)/shard_map/pallas_call | solution.py:816
  373.1 11.0 %shard_map.265 = (bf16[128,2048]{1,0:T(8,128)(2,1)}, bf16[128,2048]{1,0:T(8,128)(2,1)}, bf16[128,2048]{1,0:T(8,128)(2,1)}, bf16[128,2048]{1,0:T(8,128)(2,1)}) custom-call(bf16[1024,2048]{1,0:T(8,128)(2,1)} %all-gather.7.cloned.1.call-done.refs_0_, bf16[1024,2048]{1,0:T(8,128)(2,1)} %bitcast.369, bf16[2,1024,512]{2,1,0:T(8,128)(2,1)} %copy-done.3, ...), custom_call_target="tpu_custom_call" | custom-call | flops 4294967296 | bytes 14680064 | tf_op jit(solution)/shard_map/pallas_call | solution.py:816
  388.2 8.5 %collective-permute-done.24.refs_1_ = bf16[2048,128]{1,0:T(8,128)(2,1)S(1)} collective-permute-done((bf16[2048,128]{1,0:T(8,128)(2,1)}, bf16[2048,128]{1,0:T(8,128)(2,1)S(1)}, u32[]{:S(2)}, u32[]{:S(2)}) %collective-permute-start.24) | collective-permute-done | bytes 524320 | tf_op jit(solution)/shard_map/ppermute | solution.py:416
  401.8 8.4 %collective-permute-done.26.refs_2_ = bf16[2048,128]{1,0:T(8,128)(2,1)} collective-permute-done((bf16[2048,128]{1,0:T(8,128)(2,1)S(1)}, bf16[2048,128]{1,0:T(8,128)(2,1)}, u32[]{:S(2)}, u32[]{:S(2)}) %collective-permute-start.26) | collective-permute-done | bytes 524320 | tf_op jit(solution)/shard_map/ppermute | solution.py:416
  413.2 9.8 %collective-permute-done.27 = bf16[128,2048]{1,0:T(8,128)(2,1)S(1)} collective-permute-done((bf16[128,2048]{1,0:T(8,128)(2,1)}, bf16[128,2048]{1,0:T(8,128)(2,1)S(1)}, u32[]{:S(2)}, u32[]{:S(2)}) %collective-permute-start.27) | collective-permute-done | bytes 524320 | tf_op jit(solution)/shard_map/ppermute | solution.py:420
  433.7 15.6 %shard_map.266 = (f32[2,2048,256]{2,1,0:T(8,128)}, f32[2,2048,256]{2,1,0:T(8,128)}) custom-call(bf16[1024,2048]{1,0:T(8,128)(2,1)} %all-gather.9.cloned.1.call-done.refs_0_, bf16[1024,2048]{1,0:T(8,128)(2,1)} %all-gather.11.cloned.1.call-done.refs_1_, bf16[2,1024,512]{2,1,0:T(8,128)(2,1)} %copy-done.93, bf16[2,1024,512]{2,1,0:T(8,128)(2,1)} %copy-done.95, ...), custom_call_target="tpu_custom_call" | custom-call | flops 8589934592 | bytes 20971520 | tf_op jit(solution)/shard_map/pallas_call | solution.py:816
  449.3 11.5 %shard_map.267.own_ref = f32[2,256,2048]{2,1,0:T(8,128)} custom-call(bf16[1024,2048]{1,0:T(8,128)(2,1)} %all-gather.7.cloned.1.call-done.refs_0_, bf16[1024,2048]{1,0:T(8,128)(2,1)} %bitcast.370, bf16[2,1024,512]{2,1,0:T(8,128)(2,1)} %copy-done.3, bf16[2,1024,512]{2,1,0:T(8,128)(2,1)} %copy-done.4, bf16[2,1024,512]{2,1,0:T(8,128)(2,1)} %copy-done.3, ...), custom_call_target="tpu_custom_call" | custom-call | flops 4294967296 | bytes 14680064 | tf_op jit(solution)/shard_map/pallas_call | solution.py:816
  467.2 7.7 %collective-permute-done.33.refs_3_ = bf16[2048,128]{1,0:T(8,128)(2,1)S(1)} collective-permute-done((bf16[2048,128]{1,0:T(8,128)(2,1)}, bf16[2048,128]{1,0:T(8,128)(2,1)S(1)}, u32[]{:S(2)}, u32[]{:S(2)}) %collective-permute-start.33) | collective-permute-done | bytes 524320 | tf_op jit(solution)/shard_map/ppermute | solution.py:416
  481.4 15.6 %shard_map.268 = (bf16[1024,256]{1,0:T(8,128)(2,1)}, f32[1024,256]{1,0:T(8,128)}, f32[1024,256]{1,0:T(8,128)}, f32[1024,1]{1,0:T(8,128)}, f32[1024,1]{1,0:T(8,128)}, /*index=5*/f32[1,256]{1,0:T(1,128)}, f32[1,256]{1,0:T(1,128)}) custom-call(s32[1]{0:T(128)S(6)} %copy.169.length_ref, bf16[1024,2048]{1,0:T(8,128)(2,1)} %all-gather.13.cloned.1.call-done.upstream_ref, ...), custom_call_target="tpu_custom_call" | custom-call | flops 2684354560 | bytes 12058624 | tf_op jit(solution)/shard_map/pallas_call | solution.py:718
  508.2 6.7 %all-to-all-done.5 = f32[8,16,128]{2,1,0:T(8,128)S(1)} async-done(((f32[8,16,128]{2,1,0:T(8,128)}), f32[8,16,128]{2,1,0:T(8,128)S(1)}, u32[]{:S(2)}, u32[]{:S(2)}) %all-to-all-start.5) | async-done | bytes 65568 | tf_op jit(solution)/shard_map/all_to_all | solution.py:495
  (504 shorter events, 322.2 us)
Async XLA Ops:
  7.2 93.7 %all-gather.15.cloned.1.call-start = ((), (), s32[]{:S(2)}) async-start(), calls=%async_computation.22 | async-start | bytes 4718592 | tf_op jit(solution)/shard_map/all_gather | solution.py:998
  25.4 45.9 %all-to-all-start = ((bf16[8,64,768]{2,1,0:T(8,128)(2,1)}), bf16[8,64,768]{2,1,0:T(8,128)(2,1)}, u32[]{:S(2)}, u32[]{:S(2)}) async-start(bf16[8,64,768]{2,1,0:T(8,128)(2,1)} %pad_maximum_fusion.9), calls=%async_computation | async-start | bytes 1572864 | tf_op jit(solution)/shard_map/all_to_all | solution.py:964
  30.8 36.6 %collective-permute-start.2 = (bf16[2048,256]{1,0:T(8,128)(2,1)S(1)}, bf16[2048,256]{1,0:T(8,128)(2,1)}, u32[]{:S(2)}, u32[]{:S(2)}) collective-permute-start(bf16[2048,256]{1,0:T(8,128)(2,1)S(1)} %slice_bitcast_fusion.2), channel_id=1, source_target_pairs={{0,8},{8,0},{1,9},{9,1},{2,10},{10,2},{3,11},{11,3},{4,12},{12,4},... | collective-permute-start | bytes 3145736 | tf_op jit(solution)/shard_map/ppermute | solution.py:416
  77.0 66.5 %all-gather.7.cloned.1.call-start = ((), (), s32[]{:S(2)}) async-start(), calls=%async_computation.13 | async-start | bytes 4718592 | tf_op jit(solution)/shard_map/all_gather | solution.py:1004
  118.8 76.7 %reduce-scatter.6.cloned.1.call-start = ((), (), s32[]{:S(2)}) async-start(), calls=%async_computation.14 | async-start | bytes 4718592 | tf_op jit(solution)/shard_map/reduce_scatter | solution.py:1036
  143.5 107.4 %all-gather.9.cloned.1.call-start = ((), (), s32[]{:S(2)}) async-start(), calls=%async_computation.15 | async-start | bytes 4718592 | tf_op jit(solution)/shard_map/all_gather | solution.py:1052
  146.9 48.5 %collective-permute-start.11 = (bf16[512,2048]{1,0:T(8,128)(2,1)}, bf16[512,2048]{1,0:T(8,128)(2,1)}, u32[]{:S(2)}, u32[]{:S(2)}) collective-permute-start(bf16[512,2048]{1,0:T(8,128)(2,1)} %constant_dynamic-slice_fusion.1), channel_id=1, source_target_pairs={{0,16},{16,0},{1,17},{17,1},{2,18},{18,2},{3,19},{19,3},{4,20},{20... | collective-permute-start | bytes 6291464 | tf_op jit(solution)/shard_map/ppermute | solution.py:420
  148.4 47.0 %collective-permute-start.13 = (bf16[2048,256]{1,0:T(8,128)(2,1)S(1)}, bf16[2048,256]{1,0:T(8,128)(2,1)}, u32[]{:S(2)}, u32[]{:S(2)}) collective-permute-start(bf16[2048,256]{1,0:T(8,128)(2,1)S(1)} %copy-done.31), channel_id=1, source_target_pairs={{0,8},{8,0},{1,9},{9,1},{2,10},{10,2},{3,11},{11,3},{4,12},{12,4},... | collective-permute-start | bytes 3145736 | tf_op jit(solution)/shard_map/ppermute | solution.py:416
  149.7 36.2 %collective-permute-start.12 = (bf16[1024,256]{1,0:T(8,128)(2,1)S(1)}, bf16[1024,256]{1,0:T(8,128)(2,1)}, u32[]{:S(2)}, u32[]{:S(2)}) collective-permute-start(bf16[1024,256]{1,0:T(8,128)(2,1)S(1)} %copy-done.41), channel_id=1, source_target_pairs={{0,8},{8,0},{1,9},{9,1},{2,10},{10,2},{3,11},{11,3},{4,12},{12,4},... | collective-permute-start | bytes 1572872 | tf_op jit(solution)/shard_map/ppermute | solution.py:416
  150.5 45.0 %collective-permute-start.14 = (bf16[1024,256]{1,0:T(8,128)(2,1)}, bf16[1024,256]{1,0:T(8,128)(2,1)}, u32[]{:S(2)}, u32[]{:S(2)}) collective-permute-start(bf16[1024,256]{1,0:T(8,128)(2,1)} %get-tuple-element.285), channel_id=1, source_target_pairs={{0,8},{8,0},{1,9},{9,1},{2,10},{10,2},{3,11},{11,3},{4,12},{12,4},... | collective-permute-start | bytes 1572872 | tf_op jit(solution)/shard_map/ppermute | solution.py:416
  199.7 31.1 %collective-permute-start.15 = (bf16[128,2048]{1,0:T(8,128)(2,1)}, bf16[128,2048]{1,0:T(8,128)(2,1)}, u32[]{:S(2)}, u32[]{:S(2)}) collective-permute-start(bf16[128,2048]{1,0:T(8,128)(2,1)} %multiply_convert_fusion.6), channel_id=1, source_target_pairs={{0,16},{16,0},{1,17},{17,1},{2,18},{18,2},{3,19},{19,3},{4,20},{20... | collective-permute-start | bytes 1572872 | tf_op jit(solution)/shard_map/ppermute | solution.py:420
  214.5 36.4 %collective-permute-start.19 = (bf16[256,2048]{1,0:T(8,128)(2,1)S(1)}, bf16[256,2048]{1,0:T(8,128)(2,1)S(1)}, u32[]{:S(2)}, u32[]{:S(2)}) collective-permute-start(bf16[256,2048]{1,0:T(8,128)(2,1)S(1)} %copy-done.28), channel_id=1, source_target_pairs={{0,8},{8,0},{1,9},{9,1},{2,10},{10,2},{3,11},{11,3},{4,12},{12,4},... | collective-permute-start | bytes 3145736 | tf_op jit(solution)/shard_map/ppermute | solution.py:416
  220.6 78.1 %all-gather.11.cloned.1.call-start = ((), (), s32[]{:S(2)}) async-start(), calls=%async_computation.16 | async-start | bytes 4718592 | tf_op jit(solution)/shard_map/all_gather | solution.py:1073
  251.0 100.1 %reduce-scatter.8.cloned.1.call-start = ((), (), s32[]{:S(2)}) async-start(), calls=%async_computation.17 | async-start | bytes 4718592 | tf_op jit(solution)/shard_map/reduce_scatter | solution.py:1095
  298.7 111.6 %reduce-scatter.10.cloned.1.call-start = ((), (), s32[]{:S(2)}) async-start(), calls=%async_computation.18 | async-start | bytes 4718592 | tf_op jit(solution)/shard_map/reduce_scatter | solution.py:1103
  370.9 105.0 %all-gather.13.cloned.1.call-start = ((), (), s32[]{:S(2)}) async-start(), calls=%async_computation.19 | async-start | bytes 4718592 | tf_op jit(solution)/shard_map/all_gather | solution.py:1156
  428.0 108.1 %reduce-scatter.12.cloned.1.call-start = ((), (), s32[]{:S(2)}) async-start(), calls=%async_computation.20 | async-start | bytes 4718592 | tf_op jit(solution)/shard_map/reduce_scatter | solution.py:1170
  428.1 47.7 %collective-permute-start.29 = (bf16[512,2048]{1,0:T(8,128)(2,1)}, bf16[512,2048]{1,0:T(8,128)(2,1)S(1)}, u32[]{:S(2)}, u32[]{:S(2)}) collective-permute-start(bf16[512,2048]{1,0:T(8,128)(2,1)} %add_convert_fusion.1), channel_id=1, source_target_pairs={{0,16},{16,0},{1,17},{17,1},{2,18},{18,2},{3,19},{19,3},{4,20},{20... | collective-permute-start | bytes 6291464 | tf_op jit(solution)/shard_map/ppermute | solution.py:420
  431.7 35.5 %collective-permute-start.32 = (bf16[2048,128]{1,0:T(8,128)(2,1)}, bf16[2048,128]{1,0:T(8,128)(2,1)S(1)}, u32[]{:S(2)}, u32[]{:S(2)}) collective-permute-start(bf16[2048,128]{1,0:T(8,128)(2,1)} %get-tuple-element.364), channel_id=1, source_target_pairs={{0,8},{8,0},{1,9},{9,1},{2,10},{10,2},{3,11},{11,3},{4,12},{12,4},... | collective-permute-start | bytes 1572872 | tf_op jit(solution)/shard_map/ppermute | solution.py:416
  433.1 41.8 %collective-permute-start.33 = (bf16[2048,128]{1,0:T(8,128)(2,1)}, bf16[2048,128]{1,0:T(8,128)(2,1)S(1)}, u32[]{:S(2)}, u32[]{:S(2)}) collective-permute-start(bf16[2048,128]{1,0:T(8,128)(2,1)} %get-tuple-element.365), channel_id=1, source_target_pairs={{0,8},{8,0},{1,9},{9,1},{2,10},{10,2},{3,11},{11,3},{4,12},{12,4},... | collective-permute-start | bytes 1572872 | tf_op jit(solution)/shard_map/ppermute | solution.py:416
  507.9 91.0 %reduce-scatter.14.cloned.1.call-start = ((), (), s32[]{:S(2)}) async-start(), calls=%async_computation.21 | async-start | bytes 4718592 | tf_op jit(solution)/shard_map/reduce_scatter | solution.py:1212
  563.2 48.6 %collective-permute-start.48 = (bf16[128,2048]{1,0:T(8,128)(2,1)}, bf16[128,2048]{1,0:T(8,128)(2,1)}, u32[]{:S(2)}, u32[]{:S(2)}) collective-permute-start(bf16[128,2048]{1,0:T(8,128)(2,1)} %get-tuple-element.447), channel_id=1, source_target_pairs={{0,8},{8,0},{1,9},{9,1},{2,10},{10,2},{3,11},{11,3},{4,12},{12,4},... | collective-permute-start | bytes 1572872 | tf_op jit(solution)/shard_map/ppermute | solution.py:416
  571.4 40.5 %collective-permute-start.49 = (bf16[128,2048]{1,0:T(8,128)(2,1)}, bf16[128,2048]{1,0:T(8,128)(2,1)}, u32[]{:S(2)}, u32[]{:S(2)}) collective-permute-start(bf16[128,2048]{1,0:T(8,128)(2,1)} %get-tuple-element.448), channel_id=1, source_target_pairs={{0,8},{8,0},{1,9},{9,1},{2,10},{10,2},{3,11},{11,3},{4,12},{12,4},... | collective-permute-start | bytes 1572872 | tf_op jit(solution)/shard_map/ppermute | solution.py:416
  572.8 40.4 %collective-permute-start.50 = (bf16[128,2048]{1,0:T(8,128)(2,1)}, bf16[128,2048]{1,0:T(8,128)(2,1)}, u32[]{:S(2)}, u32[]{:S(2)}) collective-permute-start(bf16[128,2048]{1,0:T(8,128)(2,1)} %get-tuple-element.449), channel_id=1, source_target_pairs={{0,8},{8,0},{1,9},{9,1},{2,10},{10,2},{3,11},{11,3},{4,12},{12,4},... | collective-permute-start | bytes 1572872 | tf_op jit(solution)/shard_map/ppermute | solution.py:416
  (142 other events, 1994.4 us)
Sparse Core Ops, SparseCore 0:
  9.6 66.4 all-gather.14
  82.5 47.7 all-gather.6
  143.6 49.7 reduce-scatter.5
  199.5 47.8 all-gather.8
  251.1 47.5 all-gather.10
  301.4 48.7 reduce-scatter.7
  353.0 48.4 reduce-scatter.9
  428.2 47.7 all-gather.12
  479.9 50.3 reduce-scatter.11
  536.3 52.2 reduce-scatter.13

commit v4 on v3

--- a/solution.py
+++ b/solution.py
@@ -960,7 +960,8 @@
         sent, packed, w_output.astype(low), *experts_low(w_gate)
     )
     up_own, down_own = experts_low(w_up), experts_low(w_down)
-    out_rows, up_own[0], *gate_own = together(out_rows, up_own[0], *gate_own)
+    out_rows, *held = together(out_rows, *up_own, *down_own)
+    up_own, down_own = held[:many], held[many:]
     arrived = lax.all_to_all(sent, "expert", split_axis=0, concat_axis=0)
     gate_far = [swap_x(piece) for piece in gate_own[:-1]]
     held = together(
@@ -986,7 +987,7 @@
         concat_axis=0,
     )
     qkv_parts = gather_first(arrived.reshape(groups * shard, 3 * own_width))
-    held = together(packed, *qkv_parts, *gather_second(*out_parts))
+    held = together(packed, *qkv_parts, *out_parts)
     packed, qkv_parts, out_parts = held[0], held[1:4], held[4:]
     packed = (
         packed.reshape(devices, pack_rows, shard).transpose(1, 0, 2).reshape(pack_rows, model_width)
@@ -997,8 +998,10 @@
     )
     tok_all = lax.all_gather(tok, "expert", axis=0, tiled=True)
     attn_in, attn_normal, _ = rms_parts(tok_all.astype(wide), attn_gain)
-    held = together(attn_in.astype(low), *gather_second(*qkv_parts))
-    attn_low, qkv_parts = held[0], held[1:]
+    held = together(
+        attn_in.astype(low), *gather_second(*qkv_parts), *gather_second(*out_parts)
+    )
+    attn_low, qkv_parts, out_parts = held[0], held[1:6], held[6:]
     qkv_w = gather_last(*qkv_parts).reshape(model_width, 3 * own_width)
 
     cot_all = lax.all_gather(cot, "expert", axis=0, tiled=True)
@@ -1006,7 +1009,8 @@
     cot_half = swap_y(cot_half)
 
     qkv = jnp.dot(attn_low, qkv_w, preferred_element_type=wide)
-    qkv, *out_parts = together(qkv, *out_parts)
+    qkv, gate_last, *out_parts = together(qkv, gate_last, *out_parts)
+    gate_far.append(swap_x(gate_last))
     out_quad = gather_last(*out_parts)
     out_first = lax.dynamic_index_in_dim(out_quad, core, 0, keepdims=False)
     out_other = swap_core(lax.dynamic_index_in_dim(out_quad, 1 - core, 0, keepdims=False))
@@ -1030,18 +1034,13 @@
         lengths, qkv, *norm_args, out_w
     )
     attended_low = attended.astype(low)
-    held = together(attn_part, cot_all, gate_last, *up_own, *down_own)
-    attn_part, cot_all, gate_last, held = held[0], held[1], held[2], held[3:]
+    held = together(attn_part, cot_all, *gate_far, *up_own, *down_own)
+    attn_part, cot_all, gate_far, held = held[0], held[1], held[2 : 2 + many], held[2 + many :]
     up_own, down_own = held[:many], held[many:]
     attn_out = lax.psum_scatter(attn_part, "expert", scatter_dimension=0, tiled=True)
-    gate_far.append(swap_x(gate_last))
-    up_far = [swap_x(piece) for piece in up_own[:-1]]
-    held = together(attn_out, cot_half, *gate_far, *up_far, up_own[-1], *down_own)
-    attn_out, cot_half, held = held[0], held[1], held[2:]
-    gate_far, held = list(held[:many]), held[many:]
-    up_far, down_own = list(held[: many - 1]), held[many:]
-    up_own = [*up_own[:-1], held[many - 1]]
-    up_far.append(swap_x(up_own[-1]))
+    up_far = [swap_x(piece) for piece in up_own]
+    held = together(attn_out, cot_half, *up_far, *down_own)
+    attn_out, cot_half, up_far, down_own = held[0], held[1], held[2 : 2 + many], held[2 + many :]
     down_far = [swap_x(piece) for piece in down_own[:-1]]
     cot_near = in_order(cot_half, swap_core(cot_half), core).reshape(seq_len, model_width)
     hidden = tok.astype(wide) + attn_out.astype(wide)
@@ -1097,18 +1096,27 @@
     def mix(scaled):
         return jnp.einsum("etf,efd->td", scaled, down_w, preferred_element_type=wide).astype(low)
 
-    near_in, grad_in_own, own_mixed, near_mixed = together(
-        part_near[0], grad_in_own, mix(part_own[2]), mix(part_near[2])
-    )
+    tall_sources = [(part_own[i], part_near[i]) for i in (3, 4)]
+    rows_pair = (rows_own, rows_near)
+    far = list(weight_grads(rows_pair, tall_sources, 1, True))
+    far[0] = swap_x(far[0])
+    held = together(
+        part_near[0],
+        grad_in_own,
+        part_own[1],
+        part_near[1],
+        part_own[2],
+        part_near[2],
+        cot_near,
+        *far,
+    )
+    near_in, grad_in_own, part_gates, scaled_pair = held[0], held[1], held[2:4], held[4:6]
+    cot_pair, far = (cot_all, held[6]), held[7:]
+    flat_sources = [tuple(scaled_pair)]
     grad_in_near = lax.psum_scatter(near_in, "expert", scatter_dimension=0, tiled=True)
-
-    tall_sources = [(part_own[i], part_near[i]) for i in (3, 4)]
-    flat_sources = [(part_own[2], part_near[2])]
-    rows_pair, cot_pair = (rows_own, rows_near), (cot_all, cot_near)
-    far = list(weight_grads(rows_pair, tall_sources, 1, True))
     chunks = []
-    for size in (2, 1, 1, 4):
-        chunks.append(far[: size * local_count // 2])
+    for size in (1, 2, 1, 4):
+        chunks.append(list(far[: size * local_count // 2]))
         far = far[size * local_count // 2 :]
 
     def send(number):
@@ -1122,13 +1130,12 @@
             place += len(chunks[i])
         return held[: len(values)]
 
-    held = tied((cot_near, near_mixed, part_own[1], part_near[1]), 0, 1, 2, 3)
-    cot_pair, near_mixed, part_gates = (cot_all, held[0]), held[1], held[2:]
-    send(0)
-    far = list(weight_grads(cot_pair, flat_sources, 1, False))
+    send(1)
+    far = weight_grads(cot_pair, flat_sources, 1, False)
     for size in (1, 3):
-        chunks.append(far[: size * local_count // 2])
+        chunks.append(list(far[: size * local_count // 2]))
         far = far[size * local_count // 2 :]
+    own_mixed, near_mixed = mix(scaled_pair[0]), mix(scaled_pair[1])
     gate_grads = jnp.stack(part_gates)
     gate_grads = gate_grads.reshape(2, local_count, groups, tok_rows).transpose(2, 0, 1, 3)
     gate_grads = lax.all_to_all(gate_grads, "expert", split_axis=0, concat_axis=0)
@@ -1136,12 +1143,11 @@
     mixed_kept = lax.dynamic_slice_in_dim(near_mixed, core * half_rows, half_rows, 0)
     mixed_sent = lax.dynamic_slice_in_dim(near_mixed, (1 - core) * half_rows, half_rows, 0)
     mixed_half = (mixed_kept.astype(wide) + swap_core(mixed_sent).astype(wide)).astype(low)
-    mixed_half, gate_grads = tied((mixed_half, gate_grads), 0, 1, 4, 5)
-    send(1)
+    mixed_half, own_mixed, gate_grads = tied((mixed_half, own_mixed, gate_grads), 1, 4, 5)
 
     gate_grads = gate_grads.transpose(1, 3, 0, 2).reshape(2, tok_rows, experts)
     gate_grads = gate_grads[0] + swap_y(gate_grads[1])
-    grad_in_near, gate_grads = tied((grad_in_near, gate_grads), 1, 2)
+    grad_in_near, gate_grads = tied((grad_in_near, gate_grads), 2)
     send(2)
     grad_mlp_in = grad_in_own.astype(wide) + swap_y(grad_in_near).astype(wide)
     grad_logits = gates_own * (gate_grads - jnp.sum(gates_own * gate_grads, axis=-1, keepdims=True))

time: 633 us -> 628 us (level)
  waiting for transfers between devices: 186 us -> 168 us
    ppermute x31, waiting for transfers between devices: 145 us -> 116 us  [swap_x(): return lax.ppermute(block, 'dx', FLIP)]
    all_to_all x1, waiting for transfers between devices: 0.01 us -> 12.8 us  [per_device_by_heads(): lax.all_to_all(jnp.broadcast_to(packed[None], (devices,) + packed.shape),...]
    unnamed x196 -> x212, local copies, waits for them, and re-layouts: 10.8 us -> 14 us
  transfers between devices with their start and end apart: 69 -> 69, of which waited for: 26 -> 24; matrix products, arithmetic and copies ran while one was open for 35% -> 36% of each run, Pallas kernels for 14% -> 15%
where the time goes in v4:
time: 628 us; the launch traced here: 620 us
  waiting for transfers between devices  168 us (27%)
  matrix products  112 us (18%)
  starting transfers between devices  95.5 us (15%)
  Pallas kernels  95.1 us (15%)
  other arithmetic  78 us (12%)
  local copies, waits for them, and re-layouts  54.3 us (9%)
  between operations  16.9 us (3%)
    ppermute x31, waiting for transfers between devices, swap_x(): return lax.ppermute(block, 'dx', FLIP)  116 us
    pallas_call x4, Pallas kernels, weight_grads(): pl.pallas_call(functools.partial(tall_kernel if tall else flat_kernel, co...  52.2 us
    ppermute x31, starting transfers between devices, swap_x(): return lax.ppermute(block, 'dx', FLIP)  36.5 us
    dot_general x4, matrix products, into(): jnp.einsum('td,edf->etf', rows_in, weight, preferred_element_type=wide)  28.4 us
    dot_general x2, matrix products, expert_block(): jnp.einsum('td,efd->etf', grad_rows, down_w, preferred_element_type=wide)  20.4 us
    ppermute x16, starting transfers between devices, swap_y(): return lax.ppermute(block, 'dy', FLIP)  18.6 us
    dot_general x2, matrix products, expert_block(): jnp.einsum('etf,edf->td', grad_up_pre, up_w, preferred_element_type=wide)  16.6 us
    dot_general x2, matrix products, expert_block(): jnp.einsum('etf,edf->td', grad_gate_pre, gate_w, preferred_element_type=w...  15.6 us
  transfers between devices with their start and end apart: 69, of which 24 were waited for; matrix products, arithmetic and copies ran while one was open for 36% of the time, Pallas kernels for 15%

profile of v4, /device:TPU:0, one launch (start us, length us, event | category | flops | bytes accessed | tf_op | source)
XLA Modules:
  0.0 620.1 jit_solution(17941219058662097260)
XLA Ops:
  41.7 14.6 %collective-permute-done = bf16[64,2048]{1,0:T(8,128)(2,1)S(1)} collective-permute-done((bf16[64,2048]{1,0:T(8,128)(2,1)S(1)}, bf16[64,2048]{1,0:T(8,128)(2,1)S(1)}, u32[]{:S(2)}, u32[]{:S(2)}) %collective-permute-start) | collective-permute-done | bytes 262176 | tf_op jit(solution)/shard_map/ppermute | solution.py:416
  56.3 10.8 %collective-permute-done.3 = bf16[1024,256]{1,0:T(8,128)(2,1)S(1)} collective-permute-done((bf16[1024,256]{1,0:T(8,128)(2,1)S(1)}, bf16[1024,256]{1,0:T(8,128)(2,1)S(1)}, u32[]{:S(2)}, u32[]{:S(2)}) %collective-permute-start.3) | collective-permute-done | bytes 524320 | tf_op jit(solution)/shard_map/ppermute | solution.py:416
  76.9 12.8 %all-to-all-done.1 = bf16[32,10,128]{2,1,0:T(8,128)(2,1)S(1)} async-done(((bf16[32,10,128]{2,1,0:T(8,128)(2,1)}), bf16[32,10,128]{2,1,0:T(8,128)(2,1)S(1)}, u32[]{:S(2)}, u32[]{:S(2)}) %all-to-all-start.1) | async-done | bytes 81952 | tf_op jit(solution)/shard_map/all_to_all | solution.py:983
  134.4 12.2 %shard_map.263 = (bf16[1024,256]{1,0:T(8,128)(2,1)}, bf16[1024,256]{1,0:T(8,128)(2,1)}, bf16[1024,256]{1,0:T(8,128)(2,1)}, f32[1024,256]{1,0:T(8,128)}, f32[2,10...) custom-call(s32[1]{0:T(128)S(6)} %copy.169.length_ref, f32[1024,768]{1,0:T(8,128)} %copy-done.1, ...), custom_call_target="tpu_custom_call" | custom-call | flops 1610612736 | bytes 7864320 | tf_op jit(solution)/shard_map/pallas_call | solution.py:588
  154.8 34.0 %collective-permute-done.14 = bf16[1024,256]{1,0:T(8,128)(2,1)} collective-permute-done((bf16[1024,256]{1,0:T(8,128)(2,1)}, bf16[1024,256]{1,0:T(8,128)(2,1)}, u32[]{:S(2)}, u32[]{:S(2)}) %collective-permute-start.14) | collective-permute-done | bytes 524320 | tf_op jit(solution)/shard_map/ppermute | solution.py:416
  188.8 9.7 %collective-permute-done.15 = bf16[1024,256]{1,0:T(8,128)(2,1)} collective-permute-done((bf16[1024,256]{1,0:T(8,128)(2,1)S(1)}, bf16[1024,256]{1,0:T(8,128)(2,1)}, u32[]{:S(2)}, u32[]{:S(2)}) %collective-permute-start.15) | collective-permute-done | bytes 524320 | tf_op jit(solution)/shard_map/ppermute | solution.py:416
  228.7 18.2 %collective-permute-done.19 = bf16[256,2048]{1,0:T(8,128)(2,1)} collective-permute-done((bf16[256,2048]{1,0:T(8,128)(2,1)S(1)}, bf16[256,2048]{1,0:T(8,128)(2,1)}, u32[]{:S(2)}, u32[]{:S(2)}) %collective-permute-start.19) | collective-permute-done | bytes 1048608 | tf_op jit(solution)/shard_map/ppermute | solution.py:416
  252.8 8.4 %fusion.34 = f32[2,1024,512]{2,1,0:T(8,128)S(1)} fusion(bf16[2,2048,512]{2,1,0:T(8,128)(2,1)} %pad_maximum_fusion.2, bf16[1024,2048]{1,0:T(8,128)(2,1)} %all-gather.9.cloned.1.call-done.refs_0_), kind=kOutput, calls=%fused_computation.63 | convolution fusion | flops 4294967296 | bytes 12582912 | tf_op jit(solution)/shard_map/td,edf->etf/dot_general | solution.py:1075
  270.5 10.5 %fusion.24 = (f32[2,1024]{1,0:T(2,128)S(1)}, bf16[2,1024,512]{2,1,0:T(8,128)(2,1)S(1)}, bf16[2,1024,512]{2,1,0:T(8,128)(2,1)}, bf16[2,1024,512]{2,1,0:T(8,128)(2,1)S(1)}) fusion(f32[2,1024,512]{2,1,0:T(8,128)S(1)} %fusion.34, f32[2,512,1024]{1,2,0:T(8,128)} %fusion.32, f32[2,1024]{1,0:T(2,128)S(1)} %get-tuple-element.521, ...), kind=kOutput, calls=%fused_computation.44 | convolution fusion | flops 4316985344 | bytes 23085056 | tf_op jit(solution)/shard_map/td,efd->etf/dot_general | solution.py:864
  280.9 6.8 %fusion.76 = f32[1024,2048,1]{1,0,2:T(8,128)} fusion(bf16[2,1024,512]{2,1,0:T(8,128)(2,1)S(1)} %get-tuple-element.331.refs_2_.refs_4_, bf16[2,2048,512]{2,1,0:T(8,128)(2,1)S(1)} %copy-done.25), kind=kOutput, calls=%fused_computation.249 | convolution fusion | flops 4294967296 | bytes 14680064 | tf_op jit(solution)/shard_map/etf,edf->td/dot_general | solution.py:877
  287.8 8.3 %fusion.6 = bf16[1024,2048]{1,0:T(8,128)(2,1)} fusion(f32[1024,2048,1]{1,0,2:T(8,128)} %fusion.76, bf16[2,1024,512]{2,1,0:T(8,128)(2,1)S(1)} %get-tuple-element.332.refs_6_.refs_8_, bf16[2,2048,512]{2,1,0:T(8,128)(2,1)S(1)} %copy-done.27), kind=kOutput, calls=%fused_computation.12 | convolution fusion | flops 4299161600 | bytes 18874368 | tf_op jit(solution)/shard_map/etf,edf->td/dot_general | solution.py:878
  298.1 8.0 %fusion.14 = f32[2,512,1024]{1,2,0:T(8,128)S(1)} fusion(bf16[2,2048,512]{2,1,0:T(8,128)(2,1)} %pad_maximum_fusion.2, bf16[1024,2048]{1,0:T(8,128)(2,1)} %all-gather.11.cloned.1.call-done.refs_1_), kind=kOutput, calls=%fused_computation.29 | convolution fusion | flops 4294967296 | bytes 12582912 | tf_op jit(solution)/shard_map/td,edf->etf/dot_general | solution.py:1075
  312.2 9.9 %fusion.27 = (f32[2,1024]{1,0:T(2,128)S(1)}, bf16[2,1024,512]{2,1,0:T(8,128)(2,1)}, bf16[2,1024,512]{2,1,0:T(8,128)(2,1)S(1)}, bf16[2,1024,512]{2,1,0:T(8,128)(2,1)}) fusion(f32[2,512,1024]{1,2,0:T(8,128)S(1)} %fusion.14, f32[2,512,1024]{1,2,0:T(8,128)} %fusion.16, f32[2,1024]{1,0:T(2,128)S(1)} %get-tuple-element.520, bf16[1024,2048]{1,0:T(8,128)(2,1)S(1)} %bitcast.371, ...), kind=kOutput, calls=%fused_computation.49 | convolution fusion | flops 4316985344 | bytes 23085056 | tf_op jit(solution)/shard_map/td,efd->etf/dot_general | solution.py:864
  322.2 14.6 %shard_map.264 = (bf16[2048,128]{1,0:T(8,128)(2,1)}, bf16[2048,128]{1,0:T(8,128)(2,1)}, bf16[2048,128]{1,0:T(8,128)(2,1)}, bf16[2048,128]{1,0:T(8,128)(2,1)}, bf...) custom-call(bf16[1024,2048]{1,0:T(8,128)(2,1)} %all-gather.9.cloned., ...), custom_call_target="tpu_custom_call" | custom-call | flops 8589934592 | bytes 20971520 | tf_op jit(solution)/shard_map/pallas_call | solution.py:816
  338.3 8.8 %fusion.77 = f32[1024,2048,1]{1,0,2:T(8,128)} fusion(bf16[2,1024,512]{2,1,0:T(8,128)(2,1)} %get-tuple-element.466.refs_3_.refs_5_, bf16[2,2048,512]{2,1,0:T(8,128)(2,1)S(1)} %copy-done.26), kind=kOutput, calls=%fused_computation.250 | convolution fusion | flops 4294967296 | bytes 14680064 | tf_op jit(solution)/shard_map/etf,edf->td/dot_general | solution.py:877
  347.1 8.3 %fusion.5 = bf16[1024,2048]{1,0:T(8,128)(2,1)} fusion(f32[1024,2048,1]{1,0,2:T(8,128)} %fusion.77, bf16[2,1024,512]{2,1,0:T(8,128)(2,1)S(1)} %copy-done.104, bf16[2,2048,512]{2,1,0:T(8,128)(2,1)S(1)} %copy-done.28), kind=kOutput, calls=%fused_computation.10 | convolution fusion | flops 4299161600 | bytes 18874368 | tf_op jit(solution)/shard_map/etf,edf->td/dot_general | solution.py:878
  355.5 7.5 %bitcast_convert_fusion.1 = bf16[1024,2048]{1,0:T(8,128)(2,1)S(1)} fusion(bf16[2,1024,512]{2,1,0:T(8,128)(2,1)S(1)} %get-tuple-element.343.refs_3_.refs_5_, bf16[1,512,2048]{2,1,0:T(8,128)(2,1)} %copy-done.40, bf16[1,512,2048]{2,1,0:T(8,128)(2,1)} %copy-done.37), kind=kOutput, calls=%fused_computation.8 | convolution fusion | flops 4299161600 | bytes 10485760 | tf_op jit(solution)/shard_map/etf,efd->td/dot_general | solution.py:1097
  372.7 11.0 %shard_map.265 = (bf16[128,2048]{1,0:T(8,128)(2,1)}, bf16[128,2048]{1,0:T(8,128)(2,1)}, bf16[128,2048]{1,0:T(8,128)(2,1)}, bf16[128,2048]{1,0:T(8,128)(2,1)}) custom-call(bf16[1024,2048]{1,0:T(8,128)(2,1)} %all-gather.7.cloned.1.call-done.refs_0_, bf16[1024,2048]{1,0:T(8,128)(2,1)} %bitcast.369, bf16[2,1024,512]{2,1,0:T(8,128)(2,1)} %get-tuple-element.344.refs_2_.refs_4_, ...), custom_call_target="tpu_custom_call" | custom-call | flops 4294967296 | bytes 14680064 | tf_op jit(solution)/shard_map/pallas_call | solution.py:816
  406.7 8.8 %collective-permute-done.27 = bf16[128,2048]{1,0:T(8,128)(2,1)S(1)} collective-permute-done((bf16[128,2048]{1,0:T(8,128)(2,1)}, bf16[128,2048]{1,0:T(8,128)(2,1)S(1)}, u32[]{:S(2)}, u32[]{:S(2)}) %collective-permute-start.27) | collective-permute-done | bytes 524320 | tf_op jit(solution)/shard_map/ppermute | solution.py:420
  426.7 15.2 %shard_map.266 = (f32[2,2048,256]{2,1,0:T(8,128)}, f32[2,2048,256]{2,1,0:T(8,128)}) custom-call(bf16[1024,2048]{1,0:T(8,128)(2,1)} %all-gather.9.cloned.1.call-done.refs_0_, bf16[1024,2048]{1,0:T(8,128)(2,1)} %all-gather.11.cloned.1.call-done.refs_1_, bf16[2,1024,512]{2,1,0:T(8,128)(2,1)} %copy-done.102, ...), custom_call_target="tpu_custom_call" | custom-call | flops 8589934592 | bytes 20971520 | tf_op jit(solution)/shard_map/pallas_call | solution.py:816
  441.9 11.4 %shard_map.267.own_ref = f32[2,256,2048]{2,1,0:T(8,128)} custom-call(bf16[1024,2048]{1,0:T(8,128)(2,1)} %all-gather.7.cloned.1.call-done.refs_0_, bf16[1024,2048]{1,0:T(8,128)(2,1)} %bitcast.370, bf16[2,1024,512]{2,1,0:T(8,128)(2,1)} %get-tuple-element.344.refs_2_.refs_4_, bf16[2,1024,512]{2,1,0:T(8,128)(2,1)} %copy-done.4, ...), custom_call_target="tpu_custom_call" | custom-call | flops 4294967296 | bytes 14680064 | tf_op jit(solution)/shard_map/pallas_call | solution.py:816
  453.4 6.8 %collective-permute-done.32.refs_2_ = bf16[2048,128]{1,0:T(8,128)(2,1)S(1)} collective-permute-done((bf16[2048,128]{1,0:T(8,128)(2,1)}, bf16[2048,128]{1,0:T(8,128)(2,1)S(1)}, u32[]{:S(2)}, u32[]{:S(2)}) %collective-permute-start.32) | collective-permute-done | bytes 524320 | tf_op jit(solution)/shard_map/ppermute | solution.py:416
  473.5 15.1 %shard_map.268 = (bf16[1024,256]{1,0:T(8,128)(2,1)}, f32[1024,256]{1,0:T(8,128)}, f32[1024,256]{1,0:T(8,128)}, f32[1024,1]{1,0:T(8,128)}, f32[1024,1]{1,0:T(8,128)}, /*index=5*/f32[1,256]{1,0:T(1,128)}, f32[1,256]{1,0:T(1,128)}) custom-call(s32[1]{0:T(128)S(6)} %copy.169.length_ref, bf16[1024,2048]{1,0:T(8,128)(2,1)} %all-gather.13.cloned.1.call-done.upstream_ref, ...), custom_call_target="tpu_custom_call" | custom-call | flops 2684354560 | bytes 12058624 | tf_op jit(solution)/shard_map/pallas_call | solution.py:718
  495.8 7.2 %all-to-all-start.5 = ((f32[8,16,128]{2,1,0:T(8,128)}), f32[8,16,128]{2,1,0:T(8,128)S(1)}, u32[]{:S(2)}, u32[]{:S(2)}) async-start(f32[8,16,128]{2,1,0:T(8,128)} %broadcast_in_dim.113), calls=%async_computation.8 | async-start | bytes 131072 | tf_op jit(solution)/shard_map/all_to_all | solution.py:495
  (520 shorter events, 324.4 us)
Async XLA Ops:
  7.2 91.2 %all-gather.15.cloned.1.call-start = ((), (), s32[]{:S(2)}) async-start(), calls=%async_computation.22 | async-start | bytes 4718592 | tf_op jit(solution)/shard_map/all_gather | solution.py:999
  18.3 49.6 %all-to-all-start = ((bf16[8,64,768]{2,1,0:T(8,128)(2,1)}), bf16[8,64,768]{2,1,0:T(8,128)(2,1)S(1)}, u32[]{:S(2)}, u32[]{:S(2)}) async-start(bf16[8,64,768]{2,1,0:T(8,128)(2,1)} %pad_maximum_fusion.9), calls=%async_computation | async-start | bytes 1572864 | tf_op jit(solution)/shard_map/all_to_all | solution.py:965
  24.7 43.2 %collective-permute-start.2 = (bf16[2048,256]{1,0:T(8,128)(2,1)S(1)}, bf16[2048,256]{1,0:T(8,128)(2,1)}, u32[]{:S(2)}, u32[]{:S(2)}) collective-permute-start(bf16[2048,256]{1,0:T(8,128)(2,1)S(1)} %slice_bitcast_fusion.2), channel_id=1, source_target_pairs={{0,8},{8,0},{1,9},{9,1},{2,10},{10,2},{3,11},{11,3},{4,12},{12,4},... | collective-permute-start | bytes 3145736 | tf_op jit(solution)/shard_map/ppermute | solution.py:416
  35.8 31.4 %collective-permute-start.3 = (bf16[1024,256]{1,0:T(8,128)(2,1)S(1)}, bf16[1024,256]{1,0:T(8,128)(2,1)S(1)}, u32[]{:S(2)}, u32[]{:S(2)}) collective-permute-start(bf16[1024,256]{1,0:T(8,128)(2,1)S(1)} %get-tuple-element.240), channel_id=1, source_target_pairs={{0,8},{8,0},{1,9},{9,1},{2,10},{10,2},{3,11},{11,3},{4,12},{12,4},... | collective-permute-start | bytes 1572872 | tf_op jit(solution)/shard_map/ppermute | solution.py:416
  75.4 71.2 %all-gather.7.cloned.1.call-start = ((), (), s32[]{:S(2)}) async-start(), calls=%async_computation.13 | async-start | bytes 4718592 | tf_op jit(solution)/shard_map/all_gather | solution.py:1007
  120.0 78.5 %reduce-scatter.6.cloned.1.call-start = ((), (), s32[]{:S(2)}) async-start(), calls=%async_computation.14 | async-start | bytes 4718592 | tf_op jit(solution)/shard_map/reduce_scatter | solution.py:1040
  147.5 103.2 %all-gather.9.cloned.1.call-start = ((), (), s32[]{:S(2)}) async-start(), calls=%async_computation.15 | async-start | bytes 4718592 | tf_op jit(solution)/shard_map/all_gather | solution.py:1051
  150.9 47.6 %collective-permute-start.12 = (bf16[512,2048]{1,0:T(8,128)(2,1)}, bf16[512,2048]{1,0:T(8,128)(2,1)}, u32[]{:S(2)}, u32[]{:S(2)}) collective-permute-start(bf16[512,2048]{1,0:T(8,128)(2,1)} %constant_dynamic-slice_fusion.1), channel_id=1, source_target_pairs={{0,16},{16,0},{1,17},{17,1},{2,18},{18,2},{3,19},{19,3},{4,20},{20... | collective-permute-start | bytes 6291464 | tf_op jit(solution)/shard_map/ppermute | solution.py:420
  151.4 47.1 %collective-permute-start.13 = (bf16[2048,256]{1,0:T(8,128)(2,1)S(1)}, bf16[2048,256]{1,0:T(8,128)(2,1)}, u32[]{:S(2)}, u32[]{:S(2)}) collective-permute-start(bf16[2048,256]{1,0:T(8,128)(2,1)S(1)} %copy-done.32), channel_id=1, source_target_pairs={{0,8},{8,0},{1,9},{9,1},{2,10},{10,2},{3,11},{11,3},{4,12},{12,4},... | collective-permute-start | bytes 3145736 | tf_op jit(solution)/shard_map/ppermute | solution.py:416
  152.7 36.1 %collective-permute-start.14 = (bf16[1024,256]{1,0:T(8,128)(2,1)}, bf16[1024,256]{1,0:T(8,128)(2,1)}, u32[]{:S(2)}, u32[]{:S(2)}) collective-permute-start(bf16[1024,256]{1,0:T(8,128)(2,1)} %get-tuple-element.293), channel_id=1, source_target_pairs={{0,8},{8,0},{1,9},{9,1},{2,10},{10,2},{3,11},{11,3},{4,12},{12,4},... | collective-permute-start | bytes 1572872 | tf_op jit(solution)/shard_map/ppermute | solution.py:416
  153.4 45.1 %collective-permute-start.15 = (bf16[1024,256]{1,0:T(8,128)(2,1)S(1)}, bf16[1024,256]{1,0:T(8,128)(2,1)}, u32[]{:S(2)}, u32[]{:S(2)}) collective-permute-start(bf16[1024,256]{1,0:T(8,128)(2,1)S(1)} %copy-done.45), channel_id=1, source_target_pairs={{0,8},{8,0},{1,9},{9,1},{2,10},{10,2},{3,11},{11,3},{4,12},{12,4},... | collective-permute-start | bytes 1572872 | tf_op jit(solution)/shard_map/ppermute | solution.py:416
  211.9 35.0 %collective-permute-start.19 = (bf16[256,2048]{1,0:T(8,128)(2,1)S(1)}, bf16[256,2048]{1,0:T(8,128)(2,1)}, u32[]{:S(2)}, u32[]{:S(2)}) collective-permute-start(bf16[256,2048]{1,0:T(8,128)(2,1)S(1)} %copy-done.29), channel_id=1, source_target_pairs={{0,8},{8,0},{1,9},{9,1},{2,10},{10,2},{3,11},{11,3},{4,12},{12,4},... | collective-permute-start | bytes 3145736 | tf_op jit(solution)/shard_map/ppermute | solution.py:416
  218.3 79.8 %all-gather.11.cloned.1.call-start = ((), (), s32[]{:S(2)}) async-start(), calls=%async_computation.16 | async-start | bytes 4718592 | tf_op jit(solution)/shard_map/all_gather | solution.py:1072
  250.7 104.7 %reduce-scatter.8.cloned.1.call-start = ((), (), s32[]{:S(2)}) async-start(), calls=%async_computation.17 | async-start | bytes 4718592 | tf_op jit(solution)/shard_map/reduce_scatter | solution.py:1094
  298.0 105.6 %reduce-scatter.10.cloned.1.call-start = ((), (), s32[]{:S(2)}) async-start(), calls=%async_computation.18 | async-start | bytes 4718592 | tf_op jit(solution)/shard_map/reduce_scatter | solution.py:1116
  370.6 97.7 %all-gather.13.cloned.1.call-start = ((), (), s32[]{:S(2)}) async-start(), calls=%async_computation.19 | async-start | bytes 4718592 | tf_op jit(solution)/shard_map/all_gather | solution.py:1162
  421.2 109.9 %reduce-scatter.12.cloned.1.call-start = ((), (), s32[]{:S(2)}) async-start(), calls=%async_computation.20 | async-start | bytes 4718592 | tf_op jit(solution)/shard_map/reduce_scatter | solution.py:1176
  421.2 46.5 %collective-permute-start.29 = (bf16[512,2048]{1,0:T(8,128)(2,1)}, bf16[512,2048]{1,0:T(8,128)(2,1)S(1)}, u32[]{:S(2)}, u32[]{:S(2)}) collective-permute-start(bf16[512,2048]{1,0:T(8,128)(2,1)} %add_convert_fusion.1), channel_id=1, source_target_pairs={{0,16},{16,0},{1,17},{17,1},{2,18},{18,2},{3,19},{19,3},{4,20},{20... | collective-permute-start | bytes 6291464 | tf_op jit(solution)/shard_map/ppermute | solution.py:420
  424.7 35.5 %collective-permute-start.32 = (bf16[2048,128]{1,0:T(8,128)(2,1)}, bf16[2048,128]{1,0:T(8,128)(2,1)S(1)}, u32[]{:S(2)}, u32[]{:S(2)}) collective-permute-start(bf16[2048,128]{1,0:T(8,128)(2,1)} %get-tuple-element.370), channel_id=1, source_target_pairs={{0,8},{8,0},{1,9},{9,1},{2,10},{10,2},{3,11},{11,3},{4,12},{12,4},... | collective-permute-start | bytes 1572872 | tf_op jit(solution)/shard_map/ppermute | solution.py:416
  426.1 40.8 %collective-permute-start.33 = (bf16[2048,128]{1,0:T(8,128)(2,1)}, bf16[2048,128]{1,0:T(8,128)(2,1)S(1)}, u32[]{:S(2)}, u32[]{:S(2)}) collective-permute-start(bf16[2048,128]{1,0:T(8,128)(2,1)} %get-tuple-element.371), channel_id=1, source_target_pairs={{0,8},{8,0},{1,9},{9,1},{2,10},{10,2},{3,11},{11,3},{4,12},{12,4},... | collective-permute-start | bytes 1572872 | tf_op jit(solution)/shard_map/ppermute | solution.py:416
  503.0 90.7 %reduce-scatter.14.cloned.1.call-start = ((), (), s32[]{:S(2)}) async-start(), calls=%async_computation.21 | async-start | bytes 4718592 | tf_op jit(solution)/shard_map/reduce_scatter | solution.py:1218
  558.0 48.6 %collective-permute-start.48 = (bf16[128,2048]{1,0:T(8,128)(2,1)}, bf16[128,2048]{1,0:T(8,128)(2,1)}, u32[]{:S(2)}, u32[]{:S(2)}) collective-permute-start(bf16[128,2048]{1,0:T(8,128)(2,1)} %get-tuple-element.453), channel_id=1, source_target_pairs={{0,8},{8,0},{1,9},{9,1},{2,10},{10,2},{3,11},{11,3},{4,12},{12,4},... | collective-permute-start | bytes 1572872 | tf_op jit(solution)/shard_map/ppermute | solution.py:416
  566.1 40.5 %collective-permute-start.49 = (bf16[128,2048]{1,0:T(8,128)(2,1)}, bf16[128,2048]{1,0:T(8,128)(2,1)}, u32[]{:S(2)}, u32[]{:S(2)}) collective-permute-start(bf16[128,2048]{1,0:T(8,128)(2,1)} %get-tuple-element.454), channel_id=1, source_target_pairs={{0,8},{8,0},{1,9},{9,1},{2,10},{10,2},{3,11},{11,3},{4,12},{12,4},... | collective-permute-start | bytes 1572872 | tf_op jit(solution)/shard_map/ppermute | solution.py:416
  567.5 40.4 %collective-permute-start.50 = (bf16[128,2048]{1,0:T(8,128)(2,1)}, bf16[128,2048]{1,0:T(8,128)(2,1)}, u32[]{:S(2)}, u32[]{:S(2)}) collective-permute-start(bf16[128,2048]{1,0:T(8,128)(2,1)} %get-tuple-element.455), channel_id=1, source_target_pairs={{0,8},{8,0},{1,9},{9,1},{2,10},{10,2},{3,11},{11,3},{4,12},{12,4},... | collective-permute-start | bytes 1572872 | tf_op jit(solution)/shard_map/ppermute | solution.py:416
  (150 other events, 2027.0 us)
Sparse Core Ops, SparseCore 0:
  9.6 66.5 all-gather.14
  77.9 49.0 all-gather.6
  147.6 49.9 reduce-scatter.5
  202.7 47.9 all-gather.8
  252.1 45.8 all-gather.10
  300.7 48.7 reduce-scatter.7
  355.6 48.0 reduce-scatter.9
  420.5 47.6 all-gather.12
  472.1 53.1 reduce-scatter.11
  531.2 52.4 reduce-scatter.13

commit v5 on v4

--- a/solution.py
+++ b/solution.py
@@ -987,7 +987,7 @@
         concat_axis=0,
     )
     qkv_parts = gather_first(arrived.reshape(groups * shard, 3 * own_width))
-    held = together(packed, *qkv_parts, *out_parts)
+    held = together(packed, *qkv_parts, *gather_second(*out_parts))
     packed, qkv_parts, out_parts = held[0], held[1:4], held[4:]
     packed = (
         packed.reshape(devices, pack_rows, shard).transpose(1, 0, 2).reshape(pack_rows, model_width)
@@ -998,10 +998,8 @@
     )
     tok_all = lax.all_gather(tok, "expert", axis=0, tiled=True)
     attn_in, attn_normal, _ = rms_parts(tok_all.astype(wide), attn_gain)
-    held = together(
-        attn_in.astype(low), *gather_second(*qkv_parts), *gather_second(*out_parts)
-    )
-    attn_low, qkv_parts, out_parts = held[0], held[1:6], held[6:]
+    held = together(attn_in.astype(low), *gather_second(*qkv_parts))
+    attn_low, qkv_parts = held[0], held[1:]
     qkv_w = gather_last(*qkv_parts).reshape(model_width, 3 * own_width)
 
     cot_all = lax.all_gather(cot, "expert", axis=0, tiled=True)

time: 628 us -> 625 us (level)
    all_to_all x1, waiting for transfers between devices: 12.8 us -> 0.01 us  [per_device_by_heads(): lax.all_to_all(jnp.broadcast_to(packed[None], (devices,) + packed.shape),...]
    ppermute x31, waiting for transfers between devices: 116 us -> 128 us  [swap_x(): return lax.ppermute(block, 'dx', FLIP)]
    unnamed x212 -> x214, local copies, waits for them, and re-layouts: 14 us -> 14.6 us
  transfers between devices with their start and end apart: 69 -> 69, of which waited for: 24 -> 26; matrix products, arithmetic and copies ran while one was open for 36% -> 36% of each run, Pallas kernels for 15% -> 15%
where the time goes in v5:
time: 625 us; the launch traced here: 618 us
  waiting for transfers between devices  168 us (27%)
  matrix products  112 us (18%)
  Pallas kernels  95.1 us (15%)
  starting transfers between devices  93.9 us (15%)
  other arithmetic  78 us (12%)
  local copies, waits for them, and re-layouts  53.6 us (9%)
  between operations  16.9 us (3%)
    ppermute x31, waiting for transfers between devices, swap_x(): return lax.ppermute(block, 'dx', FLIP)  128 us
    pallas_call x4, Pallas kernels, weight_grads(): pl.pallas_call(functools.partial(tall_kernel if tall else flat_kernel, co...  52.2 us
    ppermute x31, starting transfers between devices, swap_x(): return lax.ppermute(block, 'dx', FLIP)  35.8 us
    dot_general x4, matrix products, into(): jnp.einsum('td,edf->etf', rows_in, weight, preferred_element_type=wide)  28.4 us
    dot_general x2, matrix products, expert_block(): jnp.einsum('td,efd->etf', grad_rows, down_w, preferred_element_type=wide)  20.4 us
    ppermute x16, starting transfers between devices, swap_y(): return lax.ppermute(block, 'dy', FLIP)  19.6 us
    dot_general x2, matrix products, expert_block(): jnp.einsum('etf,edf->td', grad_up_pre, up_w, preferred_element_type=wide)  16.6 us
    pallas_call x3, Pallas kernels, add_pieces(): pl.pallas_call(functools.partial(add_kernel, axis), grid=((rows if axis e...  15.6 us
  transfers between devices with their start and end apart: 69, of which 26 were waited for; matrix products, arithmetic and copies ran while one was open for 36% of the time, Pallas kernels for 15%

profile of v5, /device:TPU:0, one launch (start us, length us, event | category | flops | bytes accessed | tf_op | source)
XLA Modules:
  0.0 617.6 jit_solution(8118661351307711409)
XLA Ops:
  41.7 14.6 %collective-permute-done = bf16[64,2048]{1,0:T(8,128)(2,1)S(1)} collective-permute-done((bf16[64,2048]{1,0:T(8,128)(2,1)S(1)}, bf16[64,2048]{1,0:T(8,128)(2,1)S(1)}, u32[]{:S(2)}, u32[]{:S(2)}) %collective-permute-start) | collective-permute-done | bytes 262176 | tf_op jit(solution)/shard_map/ppermute | solution.py:416
  56.4 10.8 %collective-permute-done.3 = bf16[1024,256]{1,0:T(8,128)(2,1)S(1)} collective-permute-done((bf16[1024,256]{1,0:T(8,128)(2,1)S(1)}, bf16[1024,256]{1,0:T(8,128)(2,1)S(1)}, u32[]{:S(2)}, u32[]{:S(2)}) %collective-permute-start.3) | collective-permute-done | bytes 524320 | tf_op jit(solution)/shard_map/ppermute | solution.py:416
  81.0 11.6 %collective-permute-done.6 = bf16[32,2048]{1,0:T(8,128)(2,1)S(1)} collective-permute-done((bf16[32,2048]{1,0:T(8,128)(2,1)}, bf16[32,2048]{1,0:T(8,128)(2,1)S(1)}, u32[]{:S(2)}, u32[]{:S(2)}) %collective-permute-start.6) | collective-permute-done | bytes 131104 | tf_op jit(solution)/shard_map/ppermute | solution.py:416
  131.8 12.2 %shard_map.263 = (bf16[1024,256]{1,0:T(8,128)(2,1)}, bf16[1024,256]{1,0:T(8,128)(2,1)}, bf16[1024,256]{1,0:T(8,128)(2,1)}, f32[1024,256]{1,0:T(8,128)}, f32[2,10...) custom-call(s32[1]{0:T(128)S(6)} %copy.169.length_ref, f32[1024,768]{1,0:T(8,128)} %copy-done.1, ...), custom_call_target="tpu_custom_call" | custom-call | flops 1610612736 | bytes 7864320 | tf_op jit(solution)/shard_map/pallas_call | solution.py:588
  152.4 34.7 %collective-permute-done.14 = bf16[1024,256]{1,0:T(8,128)(2,1)} collective-permute-done((bf16[1024,256]{1,0:T(8,128)(2,1)}, bf16[1024,256]{1,0:T(8,128)(2,1)}, u32[]{:S(2)}, u32[]{:S(2)}) %collective-permute-start.14) | collective-permute-done | bytes 524320 | tf_op jit(solution)/shard_map/ppermute | solution.py:416
  187.1 9.9 %collective-permute-done.15 = bf16[1024,256]{1,0:T(8,128)(2,1)} collective-permute-done((bf16[1024,256]{1,0:T(8,128)(2,1)S(1)}, bf16[1024,256]{1,0:T(8,128)(2,1)}, u32[]{:S(2)}, u32[]{:S(2)}) %collective-permute-start.15) | collective-permute-done | bytes 524320 | tf_op jit(solution)/shard_map/ppermute | solution.py:416
  226.0 19.3 %collective-permute-done.19 = bf16[256,2048]{1,0:T(8,128)(2,1)} collective-permute-done((bf16[256,2048]{1,0:T(8,128)(2,1)S(1)}, bf16[256,2048]{1,0:T(8,128)(2,1)}, u32[]{:S(2)}, u32[]{:S(2)}) %collective-permute-start.19) | collective-permute-done | bytes 1048608 | tf_op jit(solution)/shard_map/ppermute | solution.py:416
  250.4 8.4 %fusion.34 = f32[2,1024,512]{2,1,0:T(8,128)S(1)} fusion(bf16[2,2048,512]{2,1,0:T(8,128)(2,1)} %pad_maximum_fusion.2, bf16[1024,2048]{1,0:T(8,128)(2,1)} %all-gather.9.cloned.1.call-done.refs_0_), kind=kOutput, calls=%fused_computation.63 | convolution fusion | flops 4294967296 | bytes 12582912 | tf_op jit(solution)/shard_map/td,edf->etf/dot_general | solution.py:1073
  268.0 10.4 %fusion.24 = (f32[2,1024]{1,0:T(2,128)S(1)}, bf16[2,1024,512]{2,1,0:T(8,128)(2,1)S(1)}, bf16[2,1024,512]{2,1,0:T(8,128)(2,1)}, bf16[2,1024,512]{2,1,0:T(8,128)(2,1)S(1)}) fusion(f32[2,1024,512]{2,1,0:T(8,128)S(1)} %fusion.34, f32[2,512,1024]{1,2,0:T(8,128)} %fusion.32, f32[2,1024]{1,0:T(2,128)S(1)} %get-tuple-element.515, ...), kind=kOutput, calls=%fused_computation.44 | convolution fusion | flops 4316985344 | bytes 23085056 | tf_op jit(solution)/shard_map/td,efd->etf/dot_general | solution.py:864
  285.2 8.3 %fusion.6 = bf16[1024,2048]{1,0:T(8,128)(2,1)} fusion(f32[1024,2048,1]{1,0,2:T(8,128)} %fusion.76, bf16[2,1024,512]{2,1,0:T(8,128)(2,1)S(1)} %get-tuple-element.326.refs_6_.refs_8_, bf16[2,2048,512]{2,1,0:T(8,128)(2,1)S(1)} %copy-done.27), kind=kOutput, calls=%fused_computation.12 | convolution fusion | flops 4299161600 | bytes 18874368 | tf_op jit(solution)/shard_map/etf,edf->td/dot_general | solution.py:878
  295.7 8.0 %fusion.14 = f32[2,512,1024]{1,2,0:T(8,128)S(1)} fusion(bf16[2,2048,512]{2,1,0:T(8,128)(2,1)} %pad_maximum_fusion.2, bf16[1024,2048]{1,0:T(8,128)(2,1)} %all-gather.11.cloned.1.call-done.refs_1_), kind=kOutput, calls=%fused_computation.29 | convolution fusion | flops 4294967296 | bytes 12582912 | tf_op jit(solution)/shard_map/td,edf->etf/dot_general | solution.py:1073
  309.8 9.9 %fusion.27 = (f32[2,1024]{1,0:T(2,128)S(1)}, bf16[2,1024,512]{2,1,0:T(8,128)(2,1)}, bf16[2,1024,512]{2,1,0:T(8,128)(2,1)S(1)}, bf16[2,1024,512]{2,1,0:T(8,128)(2,1)}) fusion(f32[2,512,1024]{1,2,0:T(8,128)S(1)} %fusion.14, f32[2,512,1024]{1,2,0:T(8,128)} %fusion.16, f32[2,1024]{1,0:T(2,128)S(1)} %get-tuple-element.514, bf16[1024,2048]{1,0:T(8,128)(2,1)S(1)} %bitcast.371, ...), kind=kOutput, calls=%fused_computation.49 | convolution fusion | flops 4316985344 | bytes 23085056 | tf_op jit(solution)/shard_map/td,efd->etf/dot_general | solution.py:864
  319.7 14.6 %shard_map.264 = (bf16[2048,128]{1,0:T(8,128)(2,1)}, bf16[2048,128]{1,0:T(8,128)(2,1)}, bf16[2048,128]{1,0:T(8,128)(2,1)}, bf16[2048,128]{1,0:T(8,128)(2,1)}, bf...) custom-call(bf16[1024,2048]{1,0:T(8,128)(2,1)} %all-gather.9.cloned., ...), custom_call_target="tpu_custom_call" | custom-call | flops 8589934592 | bytes 20971520 | tf_op jit(solution)/shard_map/pallas_call | solution.py:816
  335.9 8.7 %fusion.77 = f32[1024,2048,1]{1,0,2:T(8,128)} fusion(bf16[2,1024,512]{2,1,0:T(8,128)(2,1)} %get-tuple-element.460.refs_3_.refs_5_, bf16[2,2048,512]{2,1,0:T(8,128)(2,1)S(1)} %copy-done.26), kind=kOutput, calls=%fused_computation.250 | convolution fusion | flops 4294967296 | bytes 14680064 | tf_op jit(solution)/shard_map/etf,edf->td/dot_general | solution.py:877
  344.6 8.3 %fusion.5 = bf16[1024,2048]{1,0:T(8,128)(2,1)} fusion(f32[1024,2048,1]{1,0,2:T(8,128)} %fusion.77, bf16[2,1024,512]{2,1,0:T(8,128)(2,1)S(1)} %copy-done.105, bf16[2,2048,512]{2,1,0:T(8,128)(2,1)S(1)} %copy-done.28), kind=kOutput, calls=%fused_computation.10 | convolution fusion | flops 4299161600 | bytes 18874368 | tf_op jit(solution)/shard_map/etf,edf->td/dot_general | solution.py:878
  352.9 7.5 %bitcast_convert_fusion.1 = bf16[1024,2048]{1,0:T(8,128)(2,1)S(1)} fusion(bf16[2,1024,512]{2,1,0:T(8,128)(2,1)S(1)} %get-tuple-element.337.refs_3_.refs_5_, bf16[1,512,2048]{2,1,0:T(8,128)(2,1)} %copy-done.40, bf16[1,512,2048]{2,1,0:T(8,128)(2,1)} %copy-done.37), kind=kOutput, calls=%fused_computation.8 | convolution fusion | flops 4299161600 | bytes 10485760 | tf_op jit(solution)/shard_map/etf,efd->td/dot_general | solution.py:1095
  370.2 11.0 %shard_map.265 = (bf16[128,2048]{1,0:T(8,128)(2,1)}, bf16[128,2048]{1,0:T(8,128)(2,1)}, bf16[128,2048]{1,0:T(8,128)(2,1)}, bf16[128,2048]{1,0:T(8,128)(2,1)}) custom-call(bf16[1024,2048]{1,0:T(8,128)(2,1)} %all-gather.7.cloned.1.call-done.refs_0_, bf16[1024,2048]{1,0:T(8,128)(2,1)} %bitcast.369, bf16[2,1024,512]{2,1,0:T(8,128)(2,1)} %get-tuple-element.338.refs_2_.refs_4_, ...), custom_call_target="tpu_custom_call" | custom-call | flops 4294967296 | bytes 14680064 | tf_op jit(solution)/shard_map/pallas_call | solution.py:816
  404.1 8.7 %collective-permute-done.27 = bf16[128,2048]{1,0:T(8,128)(2,1)S(1)} collective-permute-done((bf16[128,2048]{1,0:T(8,128)(2,1)}, bf16[128,2048]{1,0:T(8,128)(2,1)S(1)}, u32[]{:S(2)}, u32[]{:S(2)}) %collective-permute-start.27) | collective-permute-done | bytes 524320 | tf_op jit(solution)/shard_map/ppermute | solution.py:420
  424.2 15.2 %shard_map.266 = (f32[2,2048,256]{2,1,0:T(8,128)}, f32[2,2048,256]{2,1,0:T(8,128)}) custom-call(bf16[1024,2048]{1,0:T(8,128)(2,1)} %all-gather.9.cloned.1.call-done.refs_0_, bf16[1024,2048]{1,0:T(8,128)(2,1)} %all-gather.11.cloned.1.call-done.refs_1_, bf16[2,1024,512]{2,1,0:T(8,128)(2,1)} %copy-done.103, ...), custom_call_target="tpu_custom_call" | custom-call | flops 8589934592 | bytes 20971520 | tf_op jit(solution)/shard_map/pallas_call | solution.py:816
  439.3 11.4 %shard_map.267.own_ref = f32[2,256,2048]{2,1,0:T(8,128)} custom-call(bf16[1024,2048]{1,0:T(8,128)(2,1)} %all-gather.7.cloned.1.call-done.refs_0_, bf16[1024,2048]{1,0:T(8,128)(2,1)} %bitcast.370, bf16[2,1024,512]{2,1,0:T(8,128)(2,1)} %get-tuple-element.338.refs_2_.refs_4_, bf16[2,1024,512]{2,1,0:T(8,128)(2,1)} %copy-done.4, ...), custom_call_target="tpu_custom_call" | custom-call | flops 4294967296 | bytes 14680064 | tf_op jit(solution)/shard_map/pallas_call | solution.py:816
  450.8 6.8 %collective-permute-done.32.refs_2_ = bf16[2048,128]{1,0:T(8,128)(2,1)S(1)} collective-permute-done((bf16[2048,128]{1,0:T(8,128)(2,1)}, bf16[2048,128]{1,0:T(8,128)(2,1)S(1)}, u32[]{:S(2)}, u32[]{:S(2)}) %collective-permute-start.32) | collective-permute-done | bytes 524320 | tf_op jit(solution)/shard_map/ppermute | solution.py:416
  471.0 15.2 %shard_map.268 = (bf16[1024,256]{1,0:T(8,128)(2,1)}, f32[1024,256]{1,0:T(8,128)}, f32[1024,256]{1,0:T(8,128)}, f32[1024,1]{1,0:T(8,128)}, f32[1024,1]{1,0:T(8,128)}, /*index=5*/f32[1,256]{1,0:T(1,128)}, f32[1,256]{1,0:T(1,128)}) custom-call(s32[1]{0:T(128)S(6)} %copy.169.length_ref, bf16[1024,2048]{1,0:T(8,128)(2,1)} %all-gather.13.cloned.1.call-done.upstream_ref, ...), custom_call_target="tpu_custom_call" | custom-call | flops 2684354560 | bytes 12058624 | tf_op jit(solution)/shard_map/pallas_call | solution.py:718
  493.2 7.2 %all-to-all-start.5 = ((f32[8,16,128]{2,1,0:T(8,128)}), f32[8,16,128]{2,1,0:T(8,128)S(1)}, u32[]{:S(2)}, u32[]{:S(2)}) async-start(f32[8,16,128]{2,1,0:T(8,128)} %broadcast_in_dim.113), calls=%async_computation.8 | async-start | bytes 131072 | tf_op jit(solution)/shard_map/all_to_all | solution.py:495
  500.7 6.7 %all-to-all-done.5 = f32[8,16,128]{2,1,0:T(8,128)S(1)} async-done(((f32[8,16,128]{2,1,0:T(8,128)}), f32[8,16,128]{2,1,0:T(8,128)S(1)}, u32[]{:S(2)}, u32[]{:S(2)}) %all-to-all-start.5) | async-done | bytes 65568 | tf_op jit(solution)/shard_map/all_to_all | solution.py:495
  (522 shorter events, 321.4 us)
Async XLA Ops:
  7.2 90.8 %all-gather.15.cloned.1.call-start = ((), (), s32[]{:S(2)}) async-start(), calls=%async_computation.22 | async-start | bytes 4718592 | tf_op jit(solution)/shard_map/all_gather | solution.py:999
  18.4 49.6 %all-to-all-start = ((bf16[8,64,768]{2,1,0:T(8,128)(2,1)}), bf16[8,64,768]{2,1,0:T(8,128)(2,1)S(1)}, u32[]{:S(2)}, u32[]{:S(2)}) async-start(bf16[8,64,768]{2,1,0:T(8,128)(2,1)} %pad_maximum_fusion.9), calls=%async_computation | async-start | bytes 1572864 | tf_op jit(solution)/shard_map/all_to_all | solution.py:965
  24.7 43.3 %collective-permute-start.2 = (bf16[2048,256]{1,0:T(8,128)(2,1)S(1)}, bf16[2048,256]{1,0:T(8,128)(2,1)}, u32[]{:S(2)}, u32[]{:S(2)}) collective-permute-start(bf16[2048,256]{1,0:T(8,128)(2,1)S(1)} %slice_bitcast_fusion.2), channel_id=1, source_target_pairs={{0,8},{8,0},{1,9},{9,1},{2,10},{10,2},{3,11},{11,3},{4,12},{12,4},... | collective-permute-start | bytes 3145736 | tf_op jit(solution)/shard_map/ppermute | solution.py:416
  35.7 31.4 %collective-permute-start.3 = (bf16[1024,256]{1,0:T(8,128)(2,1)S(1)}, bf16[1024,256]{1,0:T(8,128)(2,1)S(1)}, u32[]{:S(2)}, u32[]{:S(2)}) collective-permute-start(bf16[1024,256]{1,0:T(8,128)(2,1)S(1)} %get-tuple-element.237), channel_id=1, source_target_pairs={{0,8},{8,0},{1,9},{9,1},{2,10},{10,2},{3,11},{11,3},{4,12},{12,4},... | collective-permute-start | bytes 1572872 | tf_op jit(solution)/shard_map/ppermute | solution.py:416
  75.5 68.6 %all-gather.7.cloned.1.call-start = ((), (), s32[]{:S(2)}) async-start(), calls=%async_computation.13 | async-start | bytes 4718592 | tf_op jit(solution)/shard_map/all_gather | solution.py:1005
  118.4 78.6 %reduce-scatter.6.cloned.1.call-start = ((), (), s32[]{:S(2)}) async-start(), calls=%async_computation.14 | async-start | bytes 4718592 | tf_op jit(solution)/shard_map/reduce_scatter | solution.py:1038
  145.0 103.3 %all-gather.9.cloned.1.call-start = ((), (), s32[]{:S(2)}) async-start(), calls=%async_computation.15 | async-start | bytes 4718592 | tf_op jit(solution)/shard_map/all_gather | solution.py:1049
  148.3 48.6 %collective-permute-start.12 = (bf16[512,2048]{1,0:T(8,128)(2,1)}, bf16[512,2048]{1,0:T(8,128)(2,1)}, u32[]{:S(2)}, u32[]{:S(2)}) collective-permute-start(bf16[512,2048]{1,0:T(8,128)(2,1)} %constant_dynamic-slice_fusion.1), channel_id=1, source_target_pairs={{0,16},{16,0},{1,17},{17,1},{2,18},{18,2},{3,19},{19,3},{4,20},{20... | collective-permute-start | bytes 6291464 | tf_op jit(solution)/shard_map/ppermute | solution.py:420
  149.6 47.3 %collective-permute-start.13 = (bf16[2048,256]{1,0:T(8,128)(2,1)S(1)}, bf16[2048,256]{1,0:T(8,128)(2,1)}, u32[]{:S(2)}, u32[]{:S(2)}) collective-permute-start(bf16[2048,256]{1,0:T(8,128)(2,1)S(1)} %copy-done.32), channel_id=1, source_target_pairs={{0,8},{8,0},{1,9},{9,1},{2,10},{10,2},{3,11},{11,3},{4,12},{12,4},... | collective-permute-start | bytes 3145736 | tf_op jit(solution)/shard_map/ppermute | solution.py:416
  150.3 36.8 %collective-permute-start.14 = (bf16[1024,256]{1,0:T(8,128)(2,1)}, bf16[1024,256]{1,0:T(8,128)(2,1)}, u32[]{:S(2)}, u32[]{:S(2)}) collective-permute-start(bf16[1024,256]{1,0:T(8,128)(2,1)} %get-tuple-element.287), channel_id=1, source_target_pairs={{0,8},{8,0},{1,9},{9,1},{2,10},{10,2},{3,11},{11,3},{4,12},{12,4},... | collective-permute-start | bytes 1572872 | tf_op jit(solution)/shard_map/ppermute | solution.py:416
  151.7 45.3 %collective-permute-start.15 = (bf16[1024,256]{1,0:T(8,128)(2,1)S(1)}, bf16[1024,256]{1,0:T(8,128)(2,1)}, u32[]{:S(2)}, u32[]{:S(2)}) collective-permute-start(bf16[1024,256]{1,0:T(8,128)(2,1)S(1)} %copy-done.45), channel_id=1, source_target_pairs={{0,8},{8,0},{1,9},{9,1},{2,10},{10,2},{3,11},{11,3},{4,12},{12,4},... | collective-permute-start | bytes 1572872 | tf_op jit(solution)/shard_map/ppermute | solution.py:416
  209.4 35.9 %collective-permute-start.19 = (bf16[256,2048]{1,0:T(8,128)(2,1)S(1)}, bf16[256,2048]{1,0:T(8,128)(2,1)}, u32[]{:S(2)}, u32[]{:S(2)}) collective-permute-start(bf16[256,2048]{1,0:T(8,128)(2,1)S(1)} %copy-done.29), channel_id=1, source_target_pairs={{0,8},{8,0},{1,9},{9,1},{2,10},{10,2},{3,11},{11,3},{4,12},{12,4},... | collective-permute-start | bytes 3145736 | tf_op jit(solution)/shard_map/ppermute | solution.py:416
  215.6 80.0 %all-gather.11.cloned.1.call-start = ((), (), s32[]{:S(2)}) async-start(), calls=%async_computation.16 | async-start | bytes 4718592 | tf_op jit(solution)/shard_map/all_gather | solution.py:1070
  248.3 104.6 %reduce-scatter.8.cloned.1.call-start = ((), (), s32[]{:S(2)}) async-start(), calls=%async_computation.17 | async-start | bytes 4718592 | tf_op jit(solution)/shard_map/reduce_scatter | solution.py:1092
  295.6 105.5 %reduce-scatter.10.cloned.1.call-start = ((), (), s32[]{:S(2)}) async-start(), calls=%async_computation.18 | async-start | bytes 4718592 | tf_op jit(solution)/shard_map/reduce_scatter | solution.py:1114
  368.0 97.7 %all-gather.13.cloned.1.call-start = ((), (), s32[]{:S(2)}) async-start(), calls=%async_computation.19 | async-start | bytes 4718592 | tf_op jit(solution)/shard_map/all_gather | solution.py:1160
  418.6 109.9 %reduce-scatter.12.cloned.1.call-start = ((), (), s32[]{:S(2)}) async-start(), calls=%async_computation.20 | async-start | bytes 4718592 | tf_op jit(solution)/shard_map/reduce_scatter | solution.py:1174
  418.6 46.5 %collective-permute-start.29 = (bf16[512,2048]{1,0:T(8,128)(2,1)}, bf16[512,2048]{1,0:T(8,128)(2,1)S(1)}, u32[]{:S(2)}, u32[]{:S(2)}) collective-permute-start(bf16[512,2048]{1,0:T(8,128)(2,1)} %add_convert_fusion.1), channel_id=1, source_target_pairs={{0,16},{16,0},{1,17},{17,1},{2,18},{18,2},{3,19},{19,3},{4,20},{20... | collective-permute-start | bytes 6291464 | tf_op jit(solution)/shard_map/ppermute | solution.py:420
  422.1 35.5 %collective-permute-start.32 = (bf16[2048,128]{1,0:T(8,128)(2,1)}, bf16[2048,128]{1,0:T(8,128)(2,1)S(1)}, u32[]{:S(2)}, u32[]{:S(2)}) collective-permute-start(bf16[2048,128]{1,0:T(8,128)(2,1)} %get-tuple-element.364), channel_id=1, source_target_pairs={{0,8},{8,0},{1,9},{9,1},{2,10},{10,2},{3,11},{11,3},{4,12},{12,4},... | collective-permute-start | bytes 1572872 | tf_op jit(solution)/shard_map/ppermute | solution.py:416
  423.6 40.8 %collective-permute-start.33 = (bf16[2048,128]{1,0:T(8,128)(2,1)}, bf16[2048,128]{1,0:T(8,128)(2,1)S(1)}, u32[]{:S(2)}, u32[]{:S(2)}) collective-permute-start(bf16[2048,128]{1,0:T(8,128)(2,1)} %get-tuple-element.365), channel_id=1, source_target_pairs={{0,8},{8,0},{1,9},{9,1},{2,10},{10,2},{3,11},{11,3},{4,12},{12,4},... | collective-permute-start | bytes 1572872 | tf_op jit(solution)/shard_map/ppermute | solution.py:416
  500.4 90.7 %reduce-scatter.14.cloned.1.call-start = ((), (), s32[]{:S(2)}) async-start(), calls=%async_computation.21 | async-start | bytes 4718592 | tf_op jit(solution)/shard_map/reduce_scatter | solution.py:1216
  555.4 48.6 %collective-permute-start.48 = (bf16[128,2048]{1,0:T(8,128)(2,1)}, bf16[128,2048]{1,0:T(8,128)(2,1)}, u32[]{:S(2)}, u32[]{:S(2)}) collective-permute-start(bf16[128,2048]{1,0:T(8,128)(2,1)} %get-tuple-element.447), channel_id=1, source_target_pairs={{0,8},{8,0},{1,9},{9,1},{2,10},{10,2},{3,11},{11,3},{4,12},{12,4},... | collective-permute-start | bytes 1572872 | tf_op jit(solution)/shard_map/ppermute | solution.py:416
  563.6 40.5 %collective-permute-start.49 = (bf16[128,2048]{1,0:T(8,128)(2,1)}, bf16[128,2048]{1,0:T(8,128)(2,1)}, u32[]{:S(2)}, u32[]{:S(2)}) collective-permute-start(bf16[128,2048]{1,0:T(8,128)(2,1)} %get-tuple-element.448), channel_id=1, source_target_pairs={{0,8},{8,0},{1,9},{9,1},{2,10},{10,2},{3,11},{11,3},{4,12},{12,4},... | collective-permute-start | bytes 1572872 | tf_op jit(solution)/shard_map/ppermute | solution.py:416
  565.0 40.4 %collective-permute-start.50 = (bf16[128,2048]{1,0:T(8,128)(2,1)}, bf16[128,2048]{1,0:T(8,128)(2,1)}, u32[]{:S(2)}, u32[]{:S(2)}) collective-permute-start(bf16[128,2048]{1,0:T(8,128)(2,1)} %get-tuple-element.449), channel_id=1, source_target_pairs={{0,8},{8,0},{1,9},{9,1},{2,10},{10,2},{3,11},{11,3},{4,12},{12,4},... | collective-permute-start | bytes 1572872 | tf_op jit(solution)/shard_map/ppermute | solution.py:416
  (151 other events, 2025.8 us)
Sparse Core Ops, SparseCore 0:
  9.6 66.5 all-gather.14
  80.4 47.6 all-gather.6
  145.1 50.0 reduce-scatter.5
  201.1 47.1 all-gather.8
  249.7 45.8 all-gather.10
  298.3 48.7 reduce-scatter.7
  353.0 48.0 reduce-scatter.9
  418.0 47.6 all-gather.12
  469.5 53.1 reduce-scatter.11
  528.7 52.3 reduce-scatter.13
